TPU v7x, 512 devices: a whole 4x8x8 slice. The times are simulated.
512 devices in a mesh: pair: 64 (over z, x, y_lo), grp: 8 (over y_hi, core).
Axes of the slice: x: 4, y: 8 (y_hi: 4, y_lo: 2; y = y_hi * 2 + y_lo), z: 8, core: 2. Of those that a mesh axis runs over, the one named last changes fastest.
Arguments:
- c_occ: bfloat16 [768, 8], replicated, may hold values from -0.75 to 0.75
- c_vir: bfloat16 [768, 2048], replicated, may hold values from -0.125 to 0.125
- ints: bfloat16 [32, 2048, 4096], P('grp', 'pair'), may hold values from -4 to 4
- blocks: int32 [32, 2], P('grp'), may hold values from 0 to 11
- screen: int32 [32], P('grp'), may hold values 0 or 1
- eps_occ: float32 [8], replicated, may hold values from -1.5 to -0.4
- eps_vir: float32 [2048], replicated, may hold values from 0.3 to 3.2
Outputs:
- bmat: bfloat16 [8, 2048, 2048], P('grp', 'pair')
- pair_energy: float32 [8, 8], replicated
All inputs are finite; a program needn't handle non-finite values. No bound on the sum of `screen` on one device may be relied on, other than what follows from the above.
Results may differ from a plain program's by a relative error of at most 0.001.
Values may be sent and summed in bfloat16 or wider, within the bound.
No kernel may reach another device: no remote copies, remote signals or barrier semaphores. Data moves between devices by JAX's collectives and lax.ppermute only.
A program may use at most 64 MiB of HBM per device.

v0:
```python
import math

import jax
import jax.numpy as jnp
from jax import lax
from jax.sharding import PartitionSpec as P

SHELL = 64


def from_behind(block, axis, distance):
    devices = range(lax.axis_size(axis))
    route = [((i - distance) % len(devices), i) for i in devices]
    return lax.ppermute(block, axis, route)


def body(c_occ, c_vir, ints, blocks, screen, eps_occ, eps_vir):
    occ_count = c_occ.shape[1]
    vir_count = c_vir.shape[1]
    local_aux = ints.shape[1]

    def add_block(block_index, running):
        start_occ = blocks[block_index, 0] * SHELL
        start_vir = blocks[block_index, 1] * SHELL
        rows_occ = lax.dynamic_slice_in_dim(c_occ, start_occ, SHELL, 0)
        rows_vir = lax.dynamic_slice_in_dim(c_vir, start_vir, SHELL, 0).astype(jnp.float32)
        int_block = ints[block_index].reshape(local_aux, SHELL, SHELL)
        half_done = jnp.einsum(
            "pmn,mi->ipn", int_block, rows_occ, preferred_element_type=jnp.float32
        )
        vir_done = jnp.einsum("ipn,na->ipa", half_done, rows_vir, precision=lax.Precision.HIGHEST)
        return running + screen[block_index].astype(jnp.float32) * vir_done

    partial_sum = lax.fori_loop(
        0, ints.shape[0], add_block, jnp.zeros((occ_count, local_aux, vir_count), jnp.float32)
    )
    reduced = lax.psum_scatter(partial_sum, "grp", scatter_dimension=0, tiled=True)
    bmat = reduced.astype(jnp.bfloat16)
    pair_count = lax.axis_size("pair")
    grid_side = math.isqrt(pair_count)
    block_width = vir_count // grid_side
    pair_index = lax.axis_index("pair")
    row_block = pair_index // grid_side
    col_block = pair_index % grid_side
    pieces = bmat[0].reshape(local_aux, grid_side, block_width).transpose(1, 0, 2)
    to_rows = jnp.broadcast_to(pieces[:, None], (grid_side, grid_side, local_aux, block_width))
    to_cols = jnp.broadcast_to(pieces[None, :], (grid_side, grid_side, local_aux, block_width))
    outgoing = jnp.concatenate([to_rows, to_cols], axis=3).reshape(
        pair_count, local_aux, 2 * block_width
    )
    own_panel = lax.all_to_all(outgoing, "pair", split_axis=0, concat_axis=1, tiled=True)[0]
    row_energies = lax.dynamic_slice_in_dim(eps_vir, row_block * block_width, block_width, 0)
    col_energies = lax.dynamic_slice_in_dim(eps_vir, col_block * block_width, block_width, 0)
    grp_count = lax.axis_size("grp")
    grp_index = lax.axis_index("grp")
    positions = jnp.arange(occ_count, dtype=jnp.int32)
    own_onehot = (positions == grp_index).astype(jnp.float32)
    e_own = jnp.sum(own_onehot * eps_occ)
    scale_factor = 1.0 / (float(vir_count) * float(vir_count) * float(own_panel.shape[0]))
    contract = (((0,), (0,)), ((), ()))
    energy = jnp.zeros((occ_count, occ_count), jnp.float32)
    visiting = own_panel
    for offset in range(grp_count // 2 + 1):
        if offset > 0:
            visiting = from_behind(visiting, "grp", 1)
        peer_index = (grp_index - offset) % grp_count
        peer_onehot = (positions == peer_index).astype(jnp.float32)
        e_peer = jnp.sum(peer_onehot * eps_occ)
        forward_block = lax.dot_general(
            own_panel[:, :block_width],
            visiting[:, block_width:],
            contract,
            preferred_element_type=jnp.float32,
        )
        flipped = lax.dot_general(
            own_panel[:, block_width:],
            visiting[:, :block_width],
            contract,
            preferred_element_type=jnp.float32,
        ).T
        denominators = e_own + e_peer - row_energies[:, None] - col_energies[None, :]
        forward_part = (
            jnp.sum(forward_block * (2.0 * forward_block - flipped) / denominators) * scale_factor
        )
        energy = energy + forward_part * jnp.outer(own_onehot, peer_onehot)
        if 0 < offset < grp_count // 2:
            backward_part = (
                jnp.sum(flipped * (2.0 * flipped - forward_block) / denominators) * scale_factor
            )
            energy = energy + backward_part * jnp.outer(peer_onehot, own_onehot)
    pair_energy = lax.psum(energy, ("pair", "grp"))
    return (bmat, pair_energy)


def solution(mesh):
    return jax.shard_map(
        body,
        mesh=mesh,
        in_specs=(P(), P(), P("grp", "pair", None), P("grp", None), P("grp"), P(), P()),
        out_specs=(P("grp", "pair", None), P()),
        check_vma=False,
    )
```

profile of v0, /device:TPU:1, one launch (start us, length us, event | category | flops | bytes accessed | tf_op | source)
XLA Modules:
  0.0 473.3 jit_solution(13547373568077431913)
XLA Ops:
  7.2 37.0 %while.14 = (s32[]{:T(128)}, f32[8,32,2048]{2,1,0:T(8,128)S(1)}, s32[4]{0:T(128)}, s32[4,2]{0,1:T(2,128)}, bf16[768,8]{0,1:T(8,128)(2,1)}, /*index=5*/bf16[4,32,...) while((s32[]{:T(128)}, f32[8,32,2048]{2,1,0:T(8,128)S(1)}, ...), condition=%wide.region_1.0_spmd.clone, body=%wide.region_0.0_spmd.clone.sunk | while | flops 406323200 | bytes 5901071 | solution.py:34
  7.2 1.2 dynamic_slice.82
  9.1 1.3 constant_dynamic-slice_fusion.5
  11.7 1.0 constant_dynamic-slice_fusion.6
  12.7 0.5 squeeze.28
  13.2 0.9 fusion.82
  14.1 2.3 fusion.83
  16.5 1.2 dynamic_slice.82
  18.4 1.3 constant_dynamic-slice_fusion.5
  20.9 1.0 constant_dynamic-slice_fusion.6
  21.9 0.5 squeeze.28
  22.5 0.9 fusion.82
  23.4 2.3 fusion.83
  25.7 1.2 dynamic_slice.82
  27.6 1.3 constant_dynamic-slice_fusion.5
  30.2 1.0 constant_dynamic-slice_fusion.6
  31.2 0.5 squeeze.28
  31.7 0.9 fusion.82
  32.6 2.3 fusion.83
  35.0 1.2 dynamic_slice.82
  36.9 1.3 constant_dynamic-slice_fusion.5
  39.5 1.0 constant_dynamic-slice_fusion.6
  41.0 0.9 fusion.82
  41.9 2.3 fusion.83
  44.3 1.3 copy-done
  45.6 50.8 %reduce-scatter.2.cloned.1.call-done = f32[1,32,2048]{2,1,0:T(8,128)} async-done(((f32[8,32,2048]{2,1,0:T(8,128)}), f32[1,32,2048]{2,1,0:T(8,128)}) %reduce-scatter.2.cloned.1.call-update) | async-done | bytes 262160 | tf_op jit(solution)/shard_map/reduce_scatter | solution.py:37
  96.4 1.0 convert_element_type.74
  98.0 58.8 %all_to_all.4 = bf16[64,32,512]{2,1,0:T(8,128)(2,1)S(1)} all-to-all(bf16[64,32,512]{2,1,0:T(8,128)(2,1)S(1)} %bitcast.29), channel_id=1, replica_groups=mesh['pair'=64,'grp'=8] {'pair'}, dimensions={0} | all-to-all | bytes 4194304 | tf_op jit(solution)/shard_map/all_to_all | solution.py:51
  156.8 6.1 %collective-permute-start = (bf16[2048,512]{1,0:T(8,128)(2,1)S(1)}, bf16[2048,512]{1,0:T(8,128)(2,1)S(1)}, u32[]{:S(2)}, u32[]{:S(2)}) collective-permute-start(bf16[2048,512]{1,0:T(8,128)(2,1)S(1)} %bitcast.30), channel_id=1, source_target_pairs={{7,0},{0,1},{1,2},{2,3},{3,4},{4,5},{5,6},{6,7},{15,8},{8,9},{9,10... | collective-permute-start | bytes 6291464 | tf_op jit(solution)/shard_map/ppermute | solution.py:14
  162.9 23.2 %collective-permute-done = bf16[2048,512]{1,0:T(8,128)(2,1)S(1)} collective-permute-done((bf16[2048,512]{1,0:T(8,128)(2,1)S(1)}, bf16[2048,512]{1,0:T(8,128)(2,1)S(1)}, u32[]{:S(2)}, u32[]{:S(2)}) %collective-permute-start) | collective-permute-done | bytes 2097184 | tf_op jit(solution)/shard_map/ppermute | solution.py:14
  186.1 1.3 copy-done.3
  187.5 5.3 %collective-permute-start.1 = (bf16[2048,512]{1,0:T(8,128)(2,1)S(1)}, bf16[2048,512]{1,0:T(8,128)(2,1)}, u32[]{:S(2)}, u32[]{:S(2)}) collective-permute-start(bf16[2048,512]{1,0:T(8,128)(2,1)S(1)} %collective-permute-done), channel_id=1, source_target_pairs={{7,0},{0,1},{1,2},{2,3},{3,4},{4,5},{5,6},{6,7},{15,8},{8,9},{9,10... | collective-permute-start | bytes 6291464 | tf_op jit(solution)/shard_map/ppermute | solution.py:14
  192.8 40.3 %collective-permute-done.1 = bf16[2048,512]{1,0:T(8,128)(2,1)} collective-permute-done((bf16[2048,512]{1,0:T(8,128)(2,1)S(1)}, bf16[2048,512]{1,0:T(8,128)(2,1)}, u32[]{:S(2)}, u32[]{:S(2)}) %collective-permute-start.1) | collective-permute-done | bytes 2097184 | tf_op jit(solution)/shard_map/ppermute | solution.py:14
  233.0 5.4 %collective-permute-start.2 = (bf16[2048,512]{1,0:T(8,128)(2,1)}, bf16[2048,512]{1,0:T(8,128)(2,1)}, u32[]{:S(2)}, u32[]{:S(2)}) collective-permute-start(bf16[2048,512]{1,0:T(8,128)(2,1)} %collective-permute-done.1), channel_id=1, source_target_pairs={{7,0},{0,1},{1,2},{2,3},{3,4},{4,5},{5,6},{6,7},{15,8},{8,9},{9,10... | collective-permute-start | bytes 6291464 | tf_op jit(solution)/shard_map/ppermute | solution.py:14
  238.5 0.7 fusion.66
  245.7 0.8 broadcast_subtract_fusion.4
  246.6 56.5 %collective-permute-done.2 = bf16[2048,512]{1,0:T(8,128)(2,1)} collective-permute-done((bf16[2048,512]{1,0:T(8,128)(2,1)}, bf16[2048,512]{1,0:T(8,128)(2,1)}, u32[]{:S(2)}, u32[]{:S(2)}) %collective-permute-start.2) | collective-permute-done | bytes 2097184 | tf_op jit(solution)/shard_map/ppermute | solution.py:14
  303.1 5.3 %collective-permute-start.3 = (bf16[2048,512]{1,0:T(8,128)(2,1)}, bf16[2048,512]{1,0:T(8,128)(2,1)}, u32[]{:S(2)}, u32[]{:S(2)}) collective-permute-start(bf16[2048,512]{1,0:T(8,128)(2,1)} %collective-permute-done.2), channel_id=1, source_target_pairs={{7,0},{0,1},{1,2},{2,3},{3,4},{4,5},{5,6},{6,7},{15,8},{8,9},{9,10... | collective-permute-start | bytes 6291464 | tf_op jit(solution)/shard_map/ppermute | solution.py:14
  308.3 1.1 fusion.45
  310.1 1.8 fusion.21
  312.5 1.7 fusion.17
  314.2 1.7 fusion.19
  315.9 1.7 fusion.15
  317.6 2.5 fusion.59
  323.8 24.6 %collective-permute-done.3 = bf16[2048,512]{1,0:T(8,128)(2,1)} collective-permute-done((bf16[2048,512]{1,0:T(8,128)(2,1)}, bf16[2048,512]{1,0:T(8,128)(2,1)}, u32[]{:S(2)}, u32[]{:S(2)}) %collective-permute-start.3) | collective-permute-done | bytes 2097184 | tf_op jit(solution)/shard_map/ppermute | solution.py:14
  348.4 1.7 fusion.9
  350.1 2.3 fusion.54
  353.1 113.3 %psum.7 = f32[8,8]{1,0:T(8,128)} all-reduce(f32[8,8]{1,0:T(8,128)S(1)} %multiply_add_fusion), channel_id=1, replica_groups=mesh['pair'=64,'grp'=8] {'pair','grp'}, use_global_device_ids=true, to_apply=%region_17.18 | all-reduce | flops 64 | bytes 512 | tf_op jit(solution)/shard_map/psum | solution.py:91
  (22 shorter events, 1.8 us)
Async XLA Ops:
  7.2 89.2 %reduce-scatter.2.cloned.1.call-start = ((), (), s32[]{:S(2)}) async-start(), calls=%async_computation.2 | async-start | bytes 2359296 | tf_op jit(solution)/shard_map/reduce_scatter | solution.py:37
  44.2 1.4 copy-start
  97.4 0.7 copy-start.1
  98.0 140.5 %copy-start.2 = (f32[8]{0:T(128)S(1)}, f32[8]{0:T(128)}, u32[]{:S(2)}) copy-start(f32[8]{0:T(128)} %param.14) | copy-start | bytes 100
  156.8 29.3 %collective-permute-start = (bf16[2048,512]{1,0:T(8,128)(2,1)S(1)}, bf16[2048,512]{1,0:T(8,128)(2,1)S(1)}, u32[]{:S(2)}, u32[]{:S(2)}) collective-permute-start(bf16[2048,512]{1,0:T(8,128)(2,1)S(1)} %bitcast.30), channel_id=1, source_target_pairs={{7,0},{0,1},{1,2},{2,3},{3,4},{4,5},{5,6},{6,7},{15,8},{8,9},{9,10... | collective-permute-start | bytes 6291464 | tf_op jit(solution)/shard_map/ppermute | solution.py:14
  186.1 1.3 copy-start.3
  187.5 45.5 %collective-permute-start.1 = (bf16[2048,512]{1,0:T(8,128)(2,1)S(1)}, bf16[2048,512]{1,0:T(8,128)(2,1)}, u32[]{:S(2)}, u32[]{:S(2)}) collective-permute-start(bf16[2048,512]{1,0:T(8,128)(2,1)S(1)} %collective-permute-done), channel_id=1, source_target_pairs={{7,0},{0,1},{1,2},{2,3},{3,4},{4,5},{5,6},{6,7},{15,8},{8,9},{9,10... | collective-permute-start | bytes 6291464 | tf_op jit(solution)/shard_map/ppermute | solution.py:14
  233.0 70.0 %collective-permute-start.2 = (bf16[2048,512]{1,0:T(8,128)(2,1)}, bf16[2048,512]{1,0:T(8,128)(2,1)}, u32[]{:S(2)}, u32[]{:S(2)}) collective-permute-start(bf16[2048,512]{1,0:T(8,128)(2,1)} %collective-permute-done.1), channel_id=1, source_target_pairs={{7,0},{0,1},{1,2},{2,3},{3,4},{4,5},{5,6},{6,7},{15,8},{8,9},{9,10... | collective-permute-start | bytes 6291464 | tf_op jit(solution)/shard_map/ppermute | solution.py:14
  303.1 45.3 %collective-permute-start.3 = (bf16[2048,512]{1,0:T(8,128)(2,1)}, bf16[2048,512]{1,0:T(8,128)(2,1)}, u32[]{:S(2)}, u32[]{:S(2)}) collective-permute-start(bf16[2048,512]{1,0:T(8,128)(2,1)} %collective-permute-done.2), channel_id=1, source_target_pairs={{7,0},{0,1},{1,2},{2,3},{3,4},{4,5},{5,6},{6,7},{15,8},{8,9},{9,10... | collective-permute-start | bytes 6291464 | tf_op jit(solution)/shard_map/ppermute | solution.py:14
  310.1 1.9 copy-start.4
Sparse Core Ops, SparseCore 0:
  45.7 50.6 reduce-scatter.1
where the time goes:
time: 475 us; the launch traced here: 473 us
  waiting for transfers between devices  195 us (41%)
  blocking collectives  172 us (36%)
  matrix products  28 us (6%)
  between operations  25.7 us (5%)
  starting transfers between devices  22.1 us (5%)
  local copies, waits for them, and re-layouts  19.5 us (4%)
  loops' own time  7.63 us (2%)
    ppermute x4, waiting for transfers between devices, from_behind(): return lax.ppermute(block, axis, route)  145 us
    psum x1, blocking collectives, body(): pair_energy = lax.psum(energy, ('pair', 'grp'))  113 us
    all_to_all x1, blocking collectives, body(): lax.all_to_all(outgoing, 'pair', split_axis=0, concat_axis=1, tiled=True)[0]  58.8 us
    reduce_scatter x1, waiting for transfers between devices, body(): lax.psum_scatter(partial_sum, 'grp', scatter_dimension=0, tiled=True)  50.8 us
    ppermute x4, starting transfers between devices, from_behind(): return lax.ppermute(block, axis, route)  22 us
  transfers between devices with their start and end apart: 5, of which 5 were waited for; matrix products, arithmetic and copies ran while one was open for 3% of the time, Pallas kernels for 0%

commit v1 on v0

v1 whole, which is shorter than its diff:
```python
import jax
import jax.numpy as jnp
from jax import lax
from jax.sharding import Mesh, PartitionSpec as P

SHELL = 64
AXES = ("z", "x", "yl", "yh", "core")
PAIR = ("z", "x", "yl")
GRP = ("yh", "core")
TILES = 16
F32 = jnp.float32
BF16 = jnp.bfloat16


def split3(x):
    a = lax.reduce_precision(x, 8, 7)
    b = lax.reduce_precision(x - a, 8, 7)
    c = x - a - b
    return a.astype(BF16), b.astype(BF16), c.astype(BF16)


def half_transform(c_occ, ints, blocks, screen):
    nblk, rows, _ = ints.shape
    occ = c_occ.shape[1]
    coef = jnp.stack(
        [lax.dynamic_slice_in_dim(c_occ, blocks[b, 0] * SHELL, SHELL, 0) for b in range(nblk)]
    )
    coef = coef * screen.astype(BF16)[:, None, None]
    half = jnp.einsum(
        "bpmn,bmi->ibpn",
        ints.reshape(nblk, rows, SHELL, SHELL),
        coef,
        preferred_element_type=F32,
    )
    half = half.reshape(occ, nblk, rows // 2, 2 * SHELL).reshape(occ, -1, 128)
    where = jnp.broadcast_to(blocks[:, 1].astype(F32)[:, None, None], (nblk, 2, 128))
    where = jnp.broadcast_to(where.reshape(1, 2 * nblk, 128), (occ, 2 * nblk, 128))
    return jnp.concatenate([half, where], axis=1)


def transform(recv, c_vir, nblk, rows):
    sources = recv.shape[0]
    half = recv[:, : nblk * rows // 2].reshape(sources * nblk, rows, SHELL)
    shell = recv[:, nblk * rows // 2 :: 2, 0].reshape(sources * nblk)
    count = c_vir.shape[0] // SHELL
    onehot = (shell[None, :] == jnp.arange(count, dtype=F32)[:, None]).astype(F32)
    summed = jnp.einsum("nb,bpm->pnm", onehot, half, precision=lax.Precision.HIGHEST)
    summed = summed.reshape(rows, count * SHELL)
    terms = jnp.concatenate(split3(summed), axis=0)
    full = jnp.dot(terms, c_vir, preferred_element_type=F32)
    full = full[2 * rows :] + full[rows : 2 * rows] + full[:rows]
    return full.astype(BF16)


def outgoing(bmat):
    rows = bmat.shape[0]
    tiles = bmat.reshape(2, rows // 2, TILES, 128).transpose(2, 0, 1, 3)
    first = jnp.broadcast_to(tiles[:, None], (TILES, TILES, 2, rows // 2, 128))
    halves = bmat.reshape(2, 2, rows // 4, TILES, 2, 64).transpose(3, 4, 0, 2, 1, 5)
    halves = halves.reshape(TILES, 2, 2, rows // 4, 128)
    second = jnp.stack([jnp.roll(halves, -k, axis=0) for k in range(1, 9)], axis=1)
    second = second.reshape(TILES, TILES, 2, rows // 4, 128)
    return jnp.concatenate([first, second], axis=3).reshape(512, 3 * rows // 4, 128)


def energies(recv, eps_occ, eps_vir):
    occ = eps_occ.shape[0]
    rows = recv.shape[1] // 3
    recv = recv.reshape(-1, occ, 3 * rows, 128)
    chip = ((lax.axis_index("z") * 4 + lax.axis_index("x")) * 2 + lax.axis_index("yl")) * 4 + lax.axis_index("yh")
    tile, kind = chip // TILES, chip % TILES
    step, side = kind // 2 + 1, kind % 2
    core = lax.axis_index("core")

    x0, x1 = recv[:, :, :rows], recv[:, :, rows : 2 * rows]
    y0, y1 = recv[:, :, 2 * rows :, :64], recv[:, :, 2 * rows :, 64:]
    cross = jnp.einsum("piqa,pjqb->iajb", x0, y0, preferred_element_type=F32)
    cross = cross + jnp.einsum("piqa,pjqb->iajb", x1, y1, preferred_element_type=F32)

    own_i = kind // 2
    panel = recv[:, :, : 2 * rows]
    mine = lax.dynamic_index_in_dim(panel, own_i, 1, keepdims=False)
    others = lax.dynamic_slice_in_dim(panel, (kind % 2) * 4, 4, 1)
    selfs = jnp.einsum("pqa,pjqb->jab", mine, others, preferred_element_type=F32)

    cross = cross.reshape(occ, 2, 64, occ, 64)
    selfs = selfs.reshape(2, 2, 128, 128)
    give_cross = lax.dynamic_index_in_dim(cross, 1 - core, 1, keepdims=False)
    give_self = lax.dynamic_index_in_dim(selfs, 1 - core, 0, keepdims=False)
    give = jnp.concatenate([give_cross.reshape(-1, 128), give_self.reshape(-1, 128)], axis=0)
    got = lax.ppermute(give, "core", [(0, 1), (1, 0)])
    cross = lax.dynamic_index_in_dim(cross, core, 1, keepdims=False)
    split = occ * 64 * occ * 64 // 128
    cross = cross + got[:split].reshape(cross.shape)
    selfs = lax.dynamic_index_in_dim(selfs, core, 0, keepdims=False)
    selfs = selfs + got[split:].reshape(selfs.shape)

    eps_a = lax.dynamic_slice_in_dim(eps_vir, tile * 128 + core * 64, 64, 0)
    other = (tile + step) % TILES
    eps_b = lax.dynamic_slice_in_dim(eps_vir, other * 128 + side * 64, 64, 0)
    pair_sum = eps_occ[:, None] + eps_occ[None, :]
    denominators = pair_sum[:, None, :, None] - eps_a[None, :, None, None] - eps_b[None, None, None, :]
    flipped = cross.transpose(2, 1, 0, 3)
    terms = cross * (2.0 * cross - flipped) / denominators
    one_way = jnp.sum(terms, axis=(1, 3))
    weight = jnp.where(step == 8, 0.5, 1.0).astype(F32)
    energy = (one_way + one_way.T) * weight

    eps_t = lax.dynamic_slice_in_dim(eps_vir, tile * 128, 128, 0)
    first_j = (kind % 2) * 4 + core * 2
    e_pair = lax.dynamic_index_in_dim(eps_occ, own_i, 0, keepdims=False) + lax.dynamic_slice_in_dim(eps_occ, first_j, 2, 0)
    denominators = e_pair[:, None, None] - eps_t[None, :, None] - eps_t[None, None, :]
    self_sum = jnp.sum(selfs * (2.0 * selfs - selfs.transpose(0, 2, 1)) / denominators, axis=(1, 2))
    positions = jnp.arange(occ, dtype=jnp.int32)
    row = (positions == own_i).astype(F32)
    cols = (positions[None, :] == first_j + jnp.arange(2)[:, None]).astype(F32)
    return energy + row[:, None] * jnp.sum(cols * self_sum[:, None], axis=0)[None, :]


def sum_over(x, axes, count):
    got = lax.all_to_all(jnp.broadcast_to(x[None], (count,) + x.shape), axes, 0, 0, tiled=True)
    return jnp.sum(got, axis=0)


def body(c_occ, c_vir, ints, blocks, screen, eps_occ, eps_vir):
    nblk, rows, _ = ints.shape
    vir = c_vir.shape[1]
    sent = half_transform(c_occ, ints, blocks, screen)
    recv = lax.all_to_all(sent, GRP, 0, 0, tiled=True)
    bmat = transform(recv, c_vir, nblk, rows)
    panels = lax.all_to_all(outgoing(bmat), AXES, 0, 0, tiled=True)
    energy = energies(panels, eps_occ, eps_vir)
    scale = 1.0 / (float(vir) * float(vir) * float(rows * 64))
    energy = (energy * scale).reshape(1, -1)
    energy = sum_over(energy, ("z", "x"), 32)
    energy = sum_over(energy, ("yh", "yl", "core"), 16)
    occ = eps_occ.shape[0]
    return bmat[None], energy.reshape(occ, occ)


def solution(mesh):
    fine = Mesh(mesh.devices.reshape(8, 4, 2, 4, 2), AXES)
    return jax.shard_map(
        body,
        mesh=fine,
        in_specs=(P(), P(), P(GRP, PAIR, None), P(GRP, None), P(GRP), P(), P()),
        out_specs=(P(GRP, PAIR, None), P()),
        check_vma=False,
    )
```

time: 475 us -> 280 us (0.59)
  blocking collectives: 172 us -> 35.1 us
  waiting for transfers between devices: 195 us -> 79.8 us
  local copies, waits for them, and re-layouts: 19.5 us -> 100 us
  between operations: 25.7 us -> 3.69 us
  other arithmetic: 2.8 us -> 20.6 us
  matrix products: 28 us -> 12.9 us
  loops' own time: 7.63 us -> 0 us
    ppermute x4 -> x1, waiting for transfers between devices: 145 us -> 0.01 us  [energies(): got = lax.ppermute(give, 'core', [(0, 1), (1, 0)])]
    psum x1 -> x0, blocking collectives: 113 us -> none  [body(): pair_energy = lax.psum(energy, ('pair', 'grp'))]
    all_to_all x0 -> x2, waiting for transfers between devices: none -> 79.8 us  [the longest x1 74.6 us: body(): panels = lax.all_to_all(outgoing(bmat), AXES, 0, 0, tiled=True)]
    reduce_scatter x1 -> x0, waiting for transfers between devices: 50.8 us -> none  [body(): lax.psum_scatter(partial_sum, 'grp', scatter_dimension=0, tiled=True)]
    slice x0 -> x39, local copies, waits for them, and re-layouts: none -> 44.9 us  [the longest x31 30.9 us: outgoing(): jnp.roll(halves, -k, axis=0)]
    all_to_all x1 -> x2, blocking collectives: 58.8 us -> 35.1 us  [the longest x1 20.6 us: body(): recv = lax.all_to_all(sent, GRP, 0, 0, tiled=True)]
    all_to_all x0 -> x2, starting transfers between devices: none -> 23.2 us  [the longest x1 18.5 us: body(): panels = lax.all_to_all(outgoing(bmat), AXES, 0, 0, tiled=True)]
    ppermute x4 -> x1, starting transfers between devices: 22 us -> 2.41 us  [energies(): got = lax.ppermute(give, 'core', [(0, 1), (1, 0)])]
  transfers between devices with their start and end apart: 5 -> 3, of which waited for: 5 -> 2; matrix products, arithmetic and copies ran while one was open for 3% -> 4% of each run, Pallas kernels for 0% -> 0%
where the time goes in v1:
time: 280 us; the launch traced here: 278 us
  local copies, waits for them, and re-layouts  100 us (36%)
  waiting for transfers between devices  79.8 us (28%)
  blocking collectives  35.1 us (13%)
  starting transfers between devices  25.6 us (9%)
  other arithmetic  20.6 us (7%)
  matrix products  12.9 us (5%)
  between operations  3.69 us (1%)
    all_to_all x1, waiting for transfers between devices, body(): panels = lax.all_to_all(outgoing(bmat), AXES, 0, 0, tiled=True)  74.6 us
    slice x31, local copies, waits for them, and re-layouts, outgoing(): jnp.roll(halves, -k, axis=0)  30.9 us
    all_to_all x1, blocking collectives, body(): recv = lax.all_to_all(sent, GRP, 0, 0, tiled=True)  20.6 us
    unnamed x29, local copies, waits for them, and re-layouts  19.6 us
    all_to_all x1, starting transfers between devices, body(): panels = lax.all_to_all(outgoing(bmat), AXES, 0, 0, tiled=True)  18.5 us
    all_to_all x1, blocking collectives, sum_over(): lax.all_to_all(jnp.broadcast_to(x[None], (count,) + x.shape), axes, 0, 0,...  14.5 us
    dynamic_slice x1, local copies, waits for them, and re-layouts, energies(): cross = lax.dynamic_index_in_dim(cross, core, 1, keepdims=False)  9.91 us
    unnamed x8, other arithmetic  6.9 us
  transfers between devices with their start and end apart: 3, of which 2 were waited for; matrix products, arithmetic and copies ran while one was open for 4% of the time, Pallas kernels for 0%

profile of v1, /device:TPU:1, one launch (start us, length us, event | category | flops | bytes accessed | tf_op | source)
XLA Modules:
  0.0 277.8 jit_solution(14578517759239160012)
XLA Ops:
  0.7 1.5 fusion.54
  5.4 4.2 %reshape.175 = bf16[4,32,64,64]{3,2,1,0:T(8,128)(2,1)} reshape(bf16[4,32,4096]{2,1,0:T(8,128)(2,1)} %param.9) | data formatting | bytes 2097152 | tf_op jit(solution)/shard_map/reshape | solution.py:31
  9.8 2.0 convolution_bitcast_fusion
  12.7 1.2 reshape_reshape.3
  14.2 20.6 %all_to_all.20 = f32[8,72,128]{2,1,0:T(8,128)S(1)} all-to-all(f32[8,72,128]{2,1,0:T(8,128)S(1)} %pad_maximum_fusion.2), channel_id=1, replica_groups=mesh['z'=8,'x'=4,'yl'=2,'yh'=4,'core'=2] {'yh','core'}, dimensions={0} | all-to-all | bytes 589824 | tf_op jit(solution)/shard_map/all_to_all | solution.py:129
  35.5 1.9 reshape.176
  37.6 1.6 convolution_bitcast_fusion.1
  52.4 1.4 slice.176
  54.6 1.5 slice.180
  56.1 1.7 slice.178
  57.8 1.5 slice.184
  59.4 1.7 slice.182
  61.1 1.5 slice.188
  62.6 1.1 slice.186
  63.7 1.6 slice.192
  65.3 1.7 slice.190
  67.0 1.6 slice.196
  69.4 1.7 slice.200
  71.2 1.0 slice.204
  72.2 1.0 slice.202
  73.2 1.0 fusion.16
  80.1 2.2 pad_maximum_fusion
  82.4 18.5 %all-to-all-start.1 = ((bf16[512,24,128]{2,1,0:T(8,128)(2,1)}), bf16[512,24,128]{2,1,0:T(8,128)(2,1)}, u32[]{:S(2)}, u32[]{:S(2)}) async-start(bf16[512,24,128]{2,1,0:T(8,128)(2,1)} %pad_maximum_fusion), calls=%async_computation.1 | async-start | bytes 6291456 | tf_op jit(solution)/shard_map/all_to_all | solution.py:131
  101.0 74.6 %all-to-all-done.1 = bf16[512,24,128]{2,1,0:T(8,128)(2,1)} async-done(((bf16[512,24,128]{2,1,0:T(8,128)(2,1)}), bf16[512,24,128]{2,1,0:T(8,128)(2,1)}, u32[]{:S(2)}, u32[]{:S(2)}) %all-to-all-start.1) | async-done | bytes 3145760 | tf_op jit(solution)/shard_map/all_to_all | solution.py:131
  175.5 2.0 slice.236
  177.5 3.1 %fusion.51 = (bf16[64,8,8,128]{3,2,1,0:T(8,128)(2,1)}, bf16[64,8,8,128]{3,2,1,0:T(8,128)(2,1)}) fusion(bf16[64,8,24,128]{3,2,1,0:T(8,128)(2,1)} %bitcast.27), kind=kLoop, calls=%fused_computation.98 | loop fusion | bytes 4194304 | tf_op jit(solution)/shard_map/slice | solution.py:75
  180.5 3.5 %fusion.50 = (bf16[64,8,8,64]{3,2,1,0:T(8,128)(2,1)}, bf16[64,8,8,64]{3,2,1,0:T(8,128)(2,1)}) fusion(bf16[64,8,24,128]{3,2,1,0:T(8,128)(2,1)} %bitcast.27), kind=kLoop, calls=%fused_computation.97 | loop fusion | bytes 2097152 | tf_op jit(solution)/shard_map/slice | solution.py:76
  184.1 1.2 constant_dynamic-slice_fusion.2
  185.3 2.9 %copy.112 = bf16[64,8,8,64]{0,3,2,1:T(8,128)(2,1)} copy(bf16[64,8,8,64]{3,2,1,0:T(8,128)(2,1)} %get-tuple-element.5) | data formatting | bytes 1048576
  188.2 2.9 %copy.114 = bf16[64,8,8,64]{0,3,2,1:T(8,128)(2,1)} copy(bf16[64,8,8,64]{3,2,1,0:T(8,128)(2,1)} %get-tuple-element.4) | data formatting | bytes 1048576
  191.2 3.2 %fusion.5 = f32[8,128,8,64,1]{1,3,4,2,0:T(8,128)S(1)} fusion(bf16[64,8,8,128]{3,2,1,0:T(8,128)(2,1)} %get-tuple-element.7, bf16[64,8,8,64]{0,3,2,1:T(8,128)(2,1)} %copy.112), kind=kOutput, calls=%fused_computation.14 | convolution fusion | flops 536870912 | bytes 3670016 | tf_op jit(solution)/shard_map/piqa,pjqb->iajb/dot_general | solution.py:77
  194.4 2.9 %bitcast_add_fusion.1 = f32[8,128,8,64]{1,3,2,0:T(8,128)} fusion(f32[8,128,8,64,1]{1,3,4,2,0:T(8,128)S(1)} %fusion.5, bf16[64,8,8,128]{3,2,1,0:T(8,128)(2,1)S(1)} %copy-done.4, bf16[64,8,8,64]{0,3,2,1:T(8,128)(2,1)S(1)} %copy-done.3), kind=kOutput, calls=%fused_computation.5 | convolution fusion | flops 537395200 | bytes 5767168 | tf_op jit(solution)/shard_map/piqa,pjqb->iajb/dot_general | solution.py:78
  197.3 5.6 %reshape.181 = f32[8,2,64,8,64]{2,1,4,3,0:T(2,128)} reshape(f32[8,128,8,64]{1,3,2,0:T(8,128)} %bitcast_add_fusion.1) | data formatting | bytes 4194304 | tf_op jit(solution)/shard_map/reshape | solution.py:86
  202.9 2.5 fusion.3
  206.2 9.9 %constant_dynamic-slice_fusion.4 = (f32[8,1,64,8,64]{2,1,4,3,0:T(1,128)}, f32[8,1,64,8,64]{2,1,4,3,0:T(1,128)}) fusion(f32[8,2,64,8,64]{2,1,4,3,0:T(2,128)} %reshape.181, s32[]{:T(128)S(6)} %select_n.78, s32[]{:T(128)S(6)} %select_n.79), kind=kLoop, calls=%fused_computation.78 | loop fusion | bytes 4194312 | tf_op jit(solution)/shard_map/jit(dynamic_index_in_dim)/dynamic_slice | solution.py:92
  216.1 6.0 %copy.116 = f32[8,1,64,8,64]{4,3,2,0,1:T(8,128)} copy(f32[8,1,64,8,64]{2,1,4,3,0:T(1,128)} %get-tuple-element.3) | data formatting | bytes 2097152
  222.1 2.6 reshape.182
  224.7 2.3 pad_maximum_fusion.1
  227.0 2.4 collective-permute-start
  232.7 6.0 %copy.115 = f32[8,1,64,8,64]{4,3,2,0,1:T(8,128)} copy(f32[8,1,64,8,64]{2,1,4,3,0:T(1,128)} %get-tuple-element.2) | data formatting | bytes 2097152
  238.7 2.3 slice.237
  240.9 2.7 reshape.185
  243.6 2.4 bitcast_add_fusion
  246.1 1.7 fusion.2
  250.3 14.5 %all_to_all.21 = f32[32,1,64]{2,1,0:T(1,128)S(1)} all-to-all(f32[32,1,64]{2,1,0:T(1,128)S(1)} %broadcast_in_dim.22), channel_id=1, replica_groups=mesh['z'=8,'x'=4,'yl'=2,'yh'=4,'core'=2] {'z','x'}, dimensions={0} | all-to-all | bytes 16384 | tf_op jit(solution)/shard_map/all_to_all | solution.py:121
  265.4 4.6 %all-to-all-start.3 = ((f32[16,1,64]{2,1,0:T(1,128)}), f32[16,1,64]{2,1,0:T(1,128)S(1)}, u32[]{:S(2)}, u32[]{:S(2)}) async-start(f32[16,1,64]{2,1,0:T(1,128)} %broadcast_in_dim.23), calls=%async_computation.3 | async-start | bytes 16384 | tf_op jit(solution)/shard_map/all_to_all | solution.py:121
  270.1 1.8 fusion.58
  271.9 5.3 %all-to-all-done.3 = f32[16,1,64]{2,1,0:T(1,128)S(1)} async-done(((f32[16,1,64]{2,1,0:T(1,128)}), f32[16,1,64]{2,1,0:T(1,128)S(1)}, u32[]{:S(2)}, u32[]{:S(2)}) %all-to-all-start.3) | async-done | bytes 4128 | tf_op jit(solution)/shard_map/all_to_all | solution.py:121
  (98 shorter events, 31.2 us)
Async XLA Ops:
  0.6 38.8 %copy-start = (bf16[768,2048]{1,0:T(8,128)(2,1)S(1)}, bf16[768,2048]{1,0:T(8,128)(2,1)}, u32[]{:S(2)}) copy-start(bf16[768,2048]{1,0:T(8,128)(2,1)} %param.8) | copy-start | bytes 9437188
  0.6 9.0 %copy-start.11 = (s32[4]{0:T(128)S(1)}, s32[4]{0:T(128)}, u32[]{:S(2)}) copy-start(s32[4]{0:T(128)} %param.11) | copy-start | bytes 52
  0.7 9.0 %copy-start.9 = (bf16[768,8]{0,1:T(8,128)(2,1)S(1)}, bf16[768,8]{0,1:T(8,128)(2,1)}, u32[]{:S(2)}) copy-start(bf16[768,8]{0,1:T(8,128)(2,1)} %param.7) | copy-start | bytes 36868
  40.0 0.9 copy-start.1
  41.5 10.2 %copy-start.2 = (f32[96,2048]{1,0:T(8,128)S(1)}, f32[96,2048]{1,0:T(8,128)}, u32[]{:S(2)}) copy-start(f32[96,2048]{1,0:T(8,128)} %copy-done.1) | copy-start | bytes 2359300
  54.6 16.4 %copy-start.5 = (bf16[9,2,2,8,2,64]{5,4,3,2,1,0:T(2,128)(2,1)S(1)}, bf16[9,2,2,8,2,64]{5,4,3,2,1,0:T(2,128)(2,1)}, u32[]{:S(2)}) copy-start(bf16[9,2,2,8,2,64]{5,4,3,2,1,0:T(2,128)(2,1)} %slice.228) | copy-start | bytes 221188
  69.4 8.4 %copy-start.7 = (bf16[10,2,2,8,128]{4,3,2,1,0:T(8,128)(2,1)S(1)}, bf16[10,2,2,8,128]{4,3,2,1,0:T(8,128)(2,1)}, u32[]{:S(2)}) copy-start(bf16[10,2,2,8,128]{4,3,2,1,0:T(8,128)(2,1)} %slice.194) | copy-start | bytes 245764
  73.2 6.5 %copy-start.6 = (bf16[4,8,16,128]{3,1,2,0:T(8,128)(2,1)S(1)}, bf16[4,8,16,128]{3,1,2,0:T(8,128)(2,1)}, u32[]{:S(2)}) copy-start(bf16[4,8,16,128]{3,1,2,0:T(8,128)(2,1)} %fusion.57) | copy-start | bytes 393220
  82.4 93.2 %all-to-all-start.1 = ((bf16[512,24,128]{2,1,0:T(8,128)(2,1)}), bf16[512,24,128]{2,1,0:T(8,128)(2,1)}, u32[]{:S(2)}, u32[]{:S(2)}) async-start(bf16[512,24,128]{2,1,0:T(8,128)(2,1)} %pad_maximum_fusion), calls=%async_computation.1 | async-start | bytes 6291456 | tf_op jit(solution)/shard_map/all_to_all | solution.py:131
  191.2 3.2 %copy-start.3 = (bf16[64,8,8,64]{0,3,2,1:T(8,128)(2,1)S(1)}, bf16[64,8,8,64]{0,3,2,1:T(8,128)(2,1)}, u32[]{:S(2)}) copy-start(bf16[64,8,8,64]{0,3,2,1:T(8,128)(2,1)} %copy.114) | copy-start | bytes 1572868
  191.2 3.2 %copy-start.4 = (bf16[64,8,8,128]{3,2,1,0:T(8,128)(2,1)S(1)}, bf16[64,8,8,128]{3,2,1,0:T(8,128)(2,1)}, u32[]{:S(2)}) copy-start(bf16[64,8,8,128]{3,2,1,0:T(8,128)(2,1)} %get-tuple-element.6) | copy-start | bytes 3145732
  205.4 0.7 copy-start.8
  222.1 7.4 %copy-start.10 = (f32[8]{0:T(128)S(1)}, f32[8]{0:T(128)}, u32[]{:S(2)}) copy-start(f32[8]{0:T(128)} %param.12) | copy-start | bytes 100
  227.0 11.7 %collective-permute-start = (f32[2304,128]{1,0:T(8,128)}, f32[2304,128]{1,0:T(8,128)}, u32[]{:S(2)}, u32[]{:S(2)}) collective-permute-start(f32[2304,128]{1,0:T(8,128)} %pad_maximum_fusion.1), channel_id=1, source_target_pairs={{0,1},{1,0},{2,3},{3,2},{4,5},{5,4},{6,7},{7,6},{8,9},{9,8},{10,11... | collective-permute-start | bytes 3538952 | tf_op jit(solution)/shard_map/ppermute | solution.py:91
  265.4 11.7 %all-to-all-start.3 = ((f32[16,1,64]{2,1,0:T(1,128)}), f32[16,1,64]{2,1,0:T(1,128)S(1)}, u32[]{:S(2)}, u32[]{:S(2)}) async-start(f32[16,1,64]{2,1,0:T(1,128)} %broadcast_in_dim.23), calls=%async_computation.3 | async-start | bytes 16384 | tf_op jit(solution)/shard_map/all_to_all | solution.py:121

commit v2 on v1

v2 whole, which is shorter than its diff:
```python
import functools

import jax
import jax.numpy as jnp
from jax import lax
from jax.experimental import pallas as pl
from jax.experimental.pallas import tpu as pltpu
from jax.sharding import Mesh, PartitionSpec as P

SHELL = 64
SHELLS = 12
TILES = 16
AXES = ("z", "x", "yl", "yh", "core")
CHIPS = ("z", "x", "yl", "yh")
PAIR = ("z", "x", "yl")
GRP = ("yh", "core")
F32 = jnp.float32
BF16 = jnp.bfloat16
VMEM = pl.BlockSpec(memory_space=pltpu.VMEM)
SMEM = pl.BlockSpec(memory_space=pltpu.SMEM)
PARAMS = pltpu.CompilerParams(vmem_limit_bytes=40 * 1024 * 1024)
TRANSPOSED = (((0,), (0,)), ((), ()))


def lanes(shape):
    return lax.broadcasted_iota(jnp.int32, shape, 1)


def rows(shape):
    return lax.broadcasted_iota(jnp.int32, shape, 0)


def half_kernel(blocks, screen, c_occ, ints, out, spread, coef):
    block = pl.program_id(0)

    @pl.when(block == 0)
    def _():
        shape = (SHELL, 4096)
        spread[...] = (lanes(shape) // SHELL == rows(shape)).astype(F32).astype(BF16)

    start = pl.multiple_of(blocks[block, 0] * SHELL, SHELL)
    own = c_occ[pl.ds(start, SHELL), :]
    wide = lax.dot_general(own, spread[...], TRANSPOSED, preferred_element_type=F32)
    coef[...] = wide * screen[block].astype(F32)

    def step(t, sums):
        at = pl.multiple_of(t * 128, 128)
        tile = ints[0, :, pl.ds(at, 128)].astype(F32)
        weights = coef[:, pl.ds(at, 128)]
        return tuple(sums[i] + tile * weights[i : i + 1] for i in range(8))

    sums = lax.fori_loop(0, 32, step, (jnp.zeros((32, 128), F32),) * 8, unroll=8)
    left = lanes((32, 128)) < SHELL
    full = [s + pltpu.roll(s, SHELL, 1) for s in sums]
    shell = blocks[block, 1].astype(F32)
    put = pl.multiple_of(block * 16, 16)
    for yh in range(4):
        both = jnp.where(left, full[2 * yh], full[2 * yh + 1])
        for core in range(2):
            d = yh * 2 + core
            out[d, pl.ds(put, 16), :] = both[core * 16 : core * 16 + 16]
            out[d, 64:72, :] = jnp.where(rows((8, 128)) == block, shell, out[d, 64:72, :])


def half_transform(c_occ, ints, blocks, screen):
    count = ints.shape[0]
    return pl.pallas_call(
        half_kernel,
        out_shape=jax.ShapeDtypeStruct((8, 72, 128), F32),
        grid=(count,),
        in_specs=[
            SMEM,
            SMEM,
            pl.BlockSpec(c_occ.shape, lambda b: (0, 0)),
            pl.BlockSpec((1,) + ints.shape[1:], lambda b: (b, 0, 0)),
        ],
        out_specs=pl.BlockSpec((8, 72, 128), lambda b: (0, 0, 0)),
        scratch_shapes=[pltpu.VMEM((SHELL, 4096), BF16), pltpu.VMEM((8, 4096), F32)],
        compiler_params=PARAMS,
        name="half",
    )(blocks, screen, c_occ, ints)


def rounded(x):
    return x.astype(BF16).astype(F32)


def transform_kernel(recv, c_vir, bmat, out, terms, sides):
    left = lanes((16, 128)) < SHELL
    sums = [jnp.zeros((16, 128), F32) for _ in range(SHELLS)]
    for source in range(8):
        for b in range(4):
            data = recv[source, b * 16 : b * 16 + 16, :]
            shell = recv[source, 64 + b : 65 + b, :]
            for n in range(SHELLS):
                sums[n] = sums[n] + jnp.where(shell == float(n), data, 0.0)
    for m in range(SHELLS // 2):
        one, two = sums[2 * m], sums[2 * m + 1]
        pair = (
            jnp.where(left, one, pltpu.roll(two, SHELL, 1)),
            jnp.where(left, pltpu.roll(one, SHELL, 1), two),
        )
        for i in range(2):
            value = pair[i]
            for term in range(3):
                part = rounded(value)
                terms[term * 32 + i * 16 : term * 32 + i * 16 + 16, m * 128 : m * 128 + 128] = part.astype(BF16)
                value = value - part
    for q in range(TILES // 2):
        got = jnp.dot(terms[...], c_vir[:, q * 256 : q * 256 + 256], preferred_element_type=F32)
        full = (got[64:96] + got[32:64]) + got[0:32]
        bmat[:, q * 256 : q * 256 + 256] = full.astype(BF16)
        for t in range(2):
            one, two = full[0:16, t * 128 : t * 128 + 128], full[16:32, t * 128 : t * 128 + 128]
            tile = q * 2 + t
            sides[tile * 2] = jnp.where(left, one, pltpu.roll(two, SHELL, 1)).astype(BF16)
            sides[tile * 2 + 1] = jnp.where(left, pltpu.roll(one, SHELL, 1), two).astype(BF16)
    for r in range(TILES):
        for kind in range(TILES):
            other = (r + kind // 2 + 1) % TILES
            out[r * TILES + kind, 0:32, :] = bmat[:, r * 128 : r * 128 + 128]
            out[r * TILES + kind, 32:48, :] = sides[other * 2 + kind % 2]


def transform(recv, c_vir):
    return pl.pallas_call(
        transform_kernel,
        out_shape=(
            jax.ShapeDtypeStruct((32, c_vir.shape[1]), BF16),
            jax.ShapeDtypeStruct((256, 48, 128), BF16),
        ),
        in_specs=[VMEM, VMEM],
        out_specs=(VMEM, VMEM),
        scratch_shapes=[pltpu.VMEM((96, c_vir.shape[0]), BF16), pltpu.VMEM((32, 16, 128), BF16)],
        compiler_params=PARAMS,
        name="transform",
    )(recv, c_vir)


def gram_kernel(place, panels, keep, give, wide, all_t, all_s):
    core, side, own = place[4], place[3], place[5]
    for i in range(8):
        wide[:, i * 128 : i * 128 + 128] = panels[:, (i // 2) * 3 + i % 2].reshape(1024, 128)
    for p in range(4):
        thin = panels[:, p * 3 + 2].reshape(1024, 128)
        all_t[p * 128 : p * 128 + 128, :] = lax.dot_general(thin, wide[...], TRANSPOSED, preferred_element_type=F32)
    mine = panels[:, (own // 2) * 3 + own % 2].reshape(1024, 128)
    others = wide[:, pl.ds(pl.multiple_of(side * 512, 512), 512)]
    all_s[...] = lax.dot_general(mine, others, TRANSPOSED, preferred_element_type=F32)
    for which, target in ((core, keep), (1 - core, give)):
        for j in range(8):
            at = pl.multiple_of(j * 64 + which * 32, 32)
            target[j * 32 : j * 32 + 32, :] = all_t[pl.ds(at, 32), :]
        for q in range(4):
            at = pl.multiple_of(which * 256, 256)
            target[256:288, q * 256 : q * 256 + 256] = all_s[q * 32 : q * 32 + 32, pl.ds(at, 256)]


def gram(place, panels):
    shape = jax.ShapeDtypeStruct((288, 1024), F32)
    return pl.pallas_call(
        gram_kernel,
        out_shape=(shape, shape),
        in_specs=[SMEM, VMEM],
        out_specs=(VMEM, VMEM),
        scratch_shapes=[
            pltpu.VMEM((1024, 1024), BF16),
            pltpu.VMEM((512, 1024), F32),
            pltpu.VMEM((128, 512), F32),
        ],
        compiler_params=PARAMS,
        name="gram",
    )(place, panels.reshape(64, 12, 16, 128))


def energy_kernel(scale, place, eps_occ, keep, got, eps_vir, out, parts):
    tile, other, step, side, core, own = (place[n] for n in range(6))
    row_a = eps_vir[pl.ds(tile, 1), :]
    row_b = eps_vir[pl.ds(other, 1), :]
    first = side * 64 + core * 32
    col_b = jnp.sum(jnp.where(lanes((32, 128)) == rows((32, 128)) + first, row_b, 0.0), axis=1, keepdims=True)
    weight = jnp.where(step == 8, 1.0, 2.0)
    for i in range(8):
        for j in range(i, 8):
            there = slice(j * 32, j * 32 + 32), slice(i * 128, i * 128 + 128)
            here = slice(i * 32, i * 32 + 32), slice(j * 128, j * 128 + 128)
            one = keep[there] + got[there]
            two = keep[here] + got[here]
            denominators = (eps_occ[i] + eps_occ[j] - row_a) - col_b
            terms = (one * one + two * two - one * two) / denominators
            part = jnp.sum(terms, axis=0, keepdims=True) * weight
            parts[i * 8 + j : i * 8 + j + 1, :] = part
            parts[j * 8 + i : j * 8 + i + 1, :] = part
    square = (128, 128)
    eye = lanes(square) == rows(square)
    col_a = jnp.sum(jnp.where(eye, row_a, 0.0), axis=1, keepdims=True)
    for m in range(2):
        j = side * 4 + core * 2 + m
        block = jnp.concatenate(
            [
                keep[256:288, q * 256 + m * 128 : q * 256 + m * 128 + 128]
                + got[256:288, q * 256 + m * 128 : q * 256 + m * 128 + 128]
                for q in range(4)
            ],
            axis=0,
        )
        denominators = (eps_occ[own] + eps_occ[j] - row_a) - col_a
        terms = block * (2.0 * block - block.T) / denominators
        at = pl.ds(own * 8 + j, 1)
        parts[at, :] = parts[at, :] + jnp.sum(terms, axis=0, keepdims=True)
    column = jnp.sum(parts[...], axis=1, keepdims=True) * scale
    out[...] = jnp.sum(jnp.where(lanes((64, 128)) == rows((64, 128)), column, 0.0), axis=0, keepdims=True)


def energies(scale, place, eps_occ, keep, got, eps_vir):
    return pl.pallas_call(
        functools.partial(energy_kernel, scale),
        out_shape=jax.ShapeDtypeStruct((1, 128), F32),
        in_specs=[SMEM, SMEM, VMEM, VMEM, VMEM],
        out_specs=VMEM,
        scratch_shapes=[pltpu.VMEM((64, 128), F32)],
        compiler_params=PARAMS,
        name="energies",
    )(place, eps_occ, keep, got, eps_vir.reshape(-1, 128))


def sum_over(x, axes, count):
    got = lax.all_to_all(jnp.broadcast_to(x[None], (count,) + x.shape), axes, 0, 0, tiled=True)
    return jnp.sum(got, axis=0)


def position():
    chip = lax.axis_index(CHIPS)
    tile, kind = chip // TILES, chip % TILES
    step, side = kind // 2 + 1, kind % 2
    return jnp.stack([tile, (tile + step) % TILES, step, side, lax.axis_index("core"), kind // 2])


def body(c_occ, c_vir, ints, blocks, screen, eps_occ, eps_vir):
    vir, occ = c_vir.shape[1], c_occ.shape[1]
    place = position()
    core = lax.axis_index("core")
    swap = [(0, 1), (1, 0)]
    sent = half_transform(c_occ, ints, blocks, screen)
    recv = lax.all_to_all(sent, GRP, 0, 0, tiled=True)
    two, operand = transform(recv, c_vir)
    panels = lax.all_to_all(operand, CHIPS, 0, 0, tiled=True)

    two = two.reshape(2, 16, vir)
    mine = lax.dynamic_index_in_dim(two, core, 0, keepdims=False)
    others = lax.ppermute(lax.dynamic_index_in_dim(two, 1 - core, 0, keepdims=False), "core", swap)
    bmat = jnp.where(core == 0, jnp.stack([mine, others]), jnp.stack([others, mine]))

    keep, give = gram(place, panels)
    got = lax.ppermute(give, "core", swap)
    scale = 1.0 / (float(vir) * float(vir) * 2048.0)
    energy = energies(scale, place, eps_occ, keep, got, eps_vir)
    energy = sum_over(energy, ("z", "x"), 32)
    energy = sum_over(energy, ("yh", "yl", "core"), 16)
    return bmat.reshape(1, 32, vir), energy[:, : occ * occ].reshape(occ, occ)


def solution(mesh):
    fine = Mesh(mesh.devices.reshape(8, 4, 2, 4, 2), AXES)
    return jax.shard_map(
        body,
        mesh=fine,
        in_specs=(P(), P(), P(GRP, PAIR, None), P(GRP, None), P(GRP), P(), P()),
        out_specs=(P(GRP, PAIR, None), P()),
        check_vma=False,
    )
```

time: 280 us -> 170 us (0.61)
  local copies, waits for them, and re-layouts: 100 us -> 13.7 us
  other arithmetic: 20.6 us -> 0.71 us
  blocking collectives: 35.1 us -> 20.6 us
  matrix products: 12.9 us -> 0 us
  starting transfers between devices: 25.6 us -> 35.9 us
  Pallas kernels: 0 us -> 9.11 us
  waiting for transfers between devices: 79.8 us -> 88.1 us
  between operations: 3.69 us -> 0.82 us
    slice x39 -> x1, local copies, waits for them, and re-layouts: 44.9 us -> 0.02 us  [body(): return (bmat.reshape(1, 32, vir), energy[:, :occ * occ].reshape(occ, occ))]
    reshape x9 -> x1, local copies, waits for them, and re-layouts: 18.3 us -> 0.68 us  [body(): return (bmat.reshape(1, 32, vir), energy[:, :occ * occ].reshape(occ, occ))]
    all_to_all x1 -> x0, blocking collectives: 14.5 us -> none  [sum_over(): lax.all_to_all(jnp.broadcast_to(x[None], (count,) + x.shape), axes, 0, 0,...]
    dynamic_slice x7 -> x1, local copies, waits for them, and re-layouts: 13.3 us -> 0.02 us  [body(): mine = lax.dynamic_index_in_dim(two, core, 0, keepdims=False)]
    dot_general x6 -> x0, matrix products: 12.9 us -> none  [the longest x1 3.19 us: energies(): cross = jnp.einsum('piqa,pjqb->iajb', x0, y0, preferred_element_type=F32)]
    all_to_all x1 -> x2, waiting for transfers between devices: 5.26 us -> 14.8 us  [sum_over(): lax.all_to_all(jnp.broadcast_to(x[None], (count,) + x.shape), axes, 0, 0,...]
    pallas_call x0 -> x4, Pallas kernels: none -> 9.11 us  [the longest x1 3.4 us: half_transform(): pl.pallas_call(half_kernel, out_shape=jax.ShapeDtypeStruct((8, 72, 128),...]
    unnamed x29 -> x22, local copies, waits for them, and re-layouts: 19.6 us -> 11.6 us
  transfers between devices with their start and end apart: 3 -> 5, of which waited for: 2 -> 4; matrix products, arithmetic and copies ran while one was open for 4% -> 1% of each run, Pallas kernels for 0% -> 1%
where the time goes in v2:
time: 170 us; the launch traced here: 169 us
  waiting for transfers between devices  88.1 us (52%)
  starting transfers between devices  35.9 us (21%)
  blocking collectives  20.6 us (12%)
  local copies, waits for them, and re-layouts  13.7 us (8%)
  Pallas kernels  9.11 us (5%)
    all_to_all x1, waiting for transfers between devices, body(): panels = lax.all_to_all(operand, CHIPS, 0, 0, tiled=True)  72.6 us
    all_to_all x1, blocking collectives, body(): recv = lax.all_to_all(sent, GRP, 0, 0, tiled=True)  20.6 us
    all_to_all x1, starting transfers between devices, body(): panels = lax.all_to_all(operand, CHIPS, 0, 0, tiled=True)  17.9 us
    all_to_all x2, waiting for transfers between devices, sum_over(): lax.all_to_all(jnp.broadcast_to(x[None], (count,) + x.shape), axes, 0, 0,...  14.8 us
    all_to_all x2, starting transfers between devices, sum_over(): lax.all_to_all(jnp.broadcast_to(x[None], (count,) + x.shape), axes, 0, 0,...  12 us
    unnamed x22, local copies, waits for them, and re-layouts  11.6 us
    ppermute x1, starting transfers between devices, body(): got = lax.ppermute(give, 'core', swap)  4.13 us
    pallas_call x1, Pallas kernels, half_transform(): pl.pallas_call(half_kernel, out_shape=jax.ShapeDtypeStruct((8, 72, 128),...  3.4 us
  transfers between devices with their start and end apart: 5, of which 4 were waited for; matrix products, arithmetic and copies ran while one was open for 1% of the time, Pallas kernels for 1%

profile of v2, /device:TPU:1, one launch (start us, length us, event | category | flops | bytes accessed | tf_op | source)
XLA Modules:
  0.0 168.9 jit_solution(13808700857741473578)
XLA Ops:
  0.6 0.8 copy.13.blocks
  1.4 0.9 copy.14.c_occ
  2.3 0.0 copy-start.6
  2.3 1.2 copy-done.6
  3.5 0.0 copy-start.8
  3.5 0.7 copy-done.8
  4.2 3.4 %half.1 = f32[8,72,128]{2,1,0:T(8,128)S(1)} custom-call(s32[4,2]{1,0:T(4,128)S(1)} %copy.13.blocks, s32[4]{0:T(128)S(1)} %copy-done.8, bf16[768,8]{1,0:T(8,128)(2,1)S(1)} %copy.14.c_occ, bf16[4,32,4096]{2,1,0:T(8,128)(2,1)S(1)} %copy-done.6), custom_call_target="tpu_custom_call" | custom-call | tf_op jit(solution)/shard_map/half/pallas_call | solution.py:67
  7.6 20.6 %all_to_all.20.recv = f32[8,72,128]{2,1,0:T(8,128)S(1)} all-to-all(f32[8,72,128]{2,1,0:T(8,128)S(1)} %half.1), channel_id=1, replica_groups=mesh['z'=8,'x'=4,'yl'=2,'yh'=4,'core'=2] {'yh','core'}, dimensions={0} | all-to-all | bytes 589824 | tf_op jit(solution)/shard_map/all_to_all | solution.py:245
  28.2 0.0 copy-start.1
  28.2 1.9 %copy-done.1 = bf16[768,2048]{1,0:T(8,128)(2,1)S(1)} copy-done((bf16[768,2048]{1,0:T(8,128)(2,1)S(1)}, bf16[768,2048]{1,0:T(8,128)(2,1)}, u32[]{:S(2)}) %copy-start.1) | copy-done | bytes 3145752
  30.1 1.4 transform.1
  31.5 0.0 copy-start
  31.5 1.6 copy-done
  33.1 17.9 %all-to-all-start.1 = ((bf16[256,48,128]{2,1,0:T(8,128)(2,1)}), bf16[256,48,128]{2,1,0:T(8,128)(2,1)S(1)}, u32[]{:S(2)}, u32[]{:S(2)}) async-start(bf16[256,48,128]{2,1,0:T(8,128)(2,1)} %copy-done), calls=%async_computation.1 | async-start | bytes 6291456 | tf_op jit(solution)/shard_map/all_to_all | solution.py:247
  51.0 0.0 copy-start.7
  51.0 0.0 copy-start.9
  51.1 0.1 stack.42.place
  51.2 72.6 %all-to-all-done.1 = bf16[256,48,128]{2,1,0:T(8,128)(2,1)S(1)} async-done(((bf16[256,48,128]{2,1,0:T(8,128)(2,1)}), bf16[256,48,128]{2,1,0:T(8,128)(2,1)S(1)}, u32[]{:S(2)}, u32[]{:S(2)}) %all-to-all-start.1) | async-done | bytes 3145760 | tf_op jit(solution)/shard_map/all_to_all | solution.py:247
  123.7 3.3 %gram.1 = (f32[288,1024]{1,0:T(8,128)S(1)}, f32[288,1024]{1,0:T(8,128)}) custom-call(s32[6]{0:T(128)S(1)} %stack.42.place, bf16[64,12,16,128]{3,2,1,0:T(8,128)(2,1)S(1)} %bitcast.17), custom_call_target="tpu_custom_call" | custom-call | tf_op jit(solution)/shard_map/gram/pallas_call | solution.py:161
  127.1 0.0 copy-start.2
  127.1 1.0 copy-done.2
  128.1 4.1 %collective-permute-start.1 = (f32[288,1024]{1,0:T(8,128)}, f32[288,1024]{1,0:T(8,128)S(1)}, u32[]{:S(2)}, u32[]{:S(2)}) collective-permute-start(f32[288,1024]{1,0:T(8,128)} %get-tuple-element.9), channel_id=1, source_target_pairs={{0,1},{1,0},{2,3},{3,2},{4,5},{5,4},{6,7},{7,6},{8,9},{9,8},{10,11... | collective-permute-start | bytes 3538952 | tf_op jit(solution)/shard_map/ppermute | solution.py:255
  132.3 1.9 %collective-permute-start = (bf16[16,2048]{1,0:T(8,128)(2,1)S(1)}, bf16[16,2048]{1,0:T(8,128)(2,1)S(1)}, u32[]{:S(2)}, u32[]{:S(2)}) collective-permute-start(bf16[16,2048]{1,0:T(8,128)(2,1)S(1)} %get-tuple-element.11), channel_id=1, source_target_pairs={{0,1},{1,0},{2,3},{3,2},{4,5},{5,4},{6,7},{7,6},{8,9},{9,8},{10,11... | collective-permute-start | bytes 196616 | tf_op jit(solution)/shard_map/ppermute | solution.py:251
  134.2 0.7 collective-permute-done.1.got
  134.9 0.0 copy-start.4
  134.9 1.0 copy-done.4
  135.9 0.0 copy-done.7
  135.9 0.0 copy-done.9
  135.9 0.0 copy-start.3
  135.9 1.3 copy-done.3
  137.2 0.0 copy-start.5
  137.2 1.3 copy-done.5
  138.5 1.0 energies.1
  139.5 0.6 broadcast_in_dim.7
  140.1 5.9 %all-to-all-start.2 = ((f32[32,1,128]{2,1,0:T(1,128)}), f32[32,1,128]{2,1,0:T(1,128)S(1)}, u32[]{:S(2)}, u32[]{:S(2)}) async-start(f32[32,1,128]{2,1,0:T(1,128)} %broadcast_in_dim.7), calls=%async_computation.2 | async-start | bytes 32768 | tf_op jit(solution)/shard_map/all_to_all | solution.py:228
  146.0 8.5 %all-to-all-done.2 = f32[32,1,128]{2,1,0:T(1,128)S(1)} async-done(((f32[32,1,128]{2,1,0:T(1,128)}), f32[32,1,128]{2,1,0:T(1,128)S(1)}, u32[]{:S(2)}, u32[]{:S(2)}) %all-to-all-start.2) | async-done | bytes 16416 | tf_op jit(solution)/shard_map/all_to_all | solution.py:228
  154.5 0.6 broadcast_in_dim.16
  155.1 6.1 %all-to-all-start.3 = ((f32[16,1,128]{2,1,0:T(1,128)}), f32[16,1,128]{2,1,0:T(1,128)S(1)}, u32[]{:S(2)}, u32[]{:S(2)}) async-start(f32[16,1,128]{2,1,0:T(1,128)} %broadcast_in_dim.16), calls=%async_computation.3 | async-start | bytes 16384 | tf_op jit(solution)/shard_map/all_to_all | solution.py:228
  161.2 0.0 collective-permute-done
  161.2 0.7 maximum_select_fusion
  161.9 6.3 %all-to-all-done.3 = f32[16,1,128]{2,1,0:T(1,128)S(1)} async-done(((f32[16,1,128]{2,1,0:T(1,128)}), f32[16,1,128]{2,1,0:T(1,128)S(1)}, u32[]{:S(2)}, u32[]{:S(2)}) %all-to-all-start.3) | async-done | bytes 8224 | tf_op jit(solution)/shard_map/all_to_all | solution.py:228
  168.3 0.7 reshape.48
  (4 shorter events, 0.1 us)
Async XLA Ops:
  2.3 1.2 copy-start.6
  3.5 0.7 copy-start.8
  28.2 1.9 %copy-start.1 = (bf16[768,2048]{1,0:T(8,128)(2,1)S(1)}, bf16[768,2048]{1,0:T(8,128)(2,1)}, u32[]{:S(2)}) copy-start(bf16[768,2048]{1,0:T(8,128)(2,1)} %c_vir.1) | copy-start | bytes 9437188
  31.5 1.6 copy-start
  33.1 90.6 %all-to-all-start.1 = ((bf16[256,48,128]{2,1,0:T(8,128)(2,1)}), bf16[256,48,128]{2,1,0:T(8,128)(2,1)S(1)}, u32[]{:S(2)}, u32[]{:S(2)}) async-start(bf16[256,48,128]{2,1,0:T(8,128)(2,1)} %copy-done), calls=%async_computation.1 | async-start | bytes 6291456 | tf_op jit(solution)/shard_map/all_to_all | solution.py:247
  51.0 84.9 %copy-start.7 = (f32[2048]{0:T(1024)S(1)}, f32[2048]{0:T(1024)}, u32[]{:S(2)}) copy-start(f32[2048]{0:T(1024)} %param.13) | copy-start | bytes 24580
  51.0 84.9 %copy-start.9 = (f32[8]{0:T(128)S(1)}, f32[8]{0:T(128)}, u32[]{:S(2)}) copy-start(f32[8]{0:T(128)} %eps_occ.1) | copy-start | bytes 100
  127.1 1.0 copy-start.2
  128.1 6.8 %collective-permute-start.1 = (f32[288,1024]{1,0:T(8,128)}, f32[288,1024]{1,0:T(8,128)S(1)}, u32[]{:S(2)}, u32[]{:S(2)}) collective-permute-start(f32[288,1024]{1,0:T(8,128)} %get-tuple-element.9), channel_id=1, source_target_pairs={{0,1},{1,0},{2,3},{3,2},{4,5},{5,4},{6,7},{7,6},{8,9},{9,8},{10,11... | collective-permute-start | bytes 3538952 | tf_op jit(solution)/shard_map/ppermute | solution.py:255
  132.3 28.9 %collective-permute-start = (bf16[16,2048]{1,0:T(8,128)(2,1)S(1)}, bf16[16,2048]{1,0:T(8,128)(2,1)S(1)}, u32[]{:S(2)}, u32[]{:S(2)}) collective-permute-start(bf16[16,2048]{1,0:T(8,128)(2,1)S(1)} %get-tuple-element.11), channel_id=1, source_target_pairs={{0,1},{1,0},{2,3},{3,2},{4,5},{5,4},{6,7},{7,6},{8,9},{9,8},{10,11... | collective-permute-start | bytes 196616 | tf_op jit(solution)/shard_map/ppermute | solution.py:251
  134.9 1.0 copy-start.4
  135.9 1.3 copy-start.3
  137.2 1.3 copy-start.5
  140.1 14.4 %all-to-all-start.2 = ((f32[32,1,128]{2,1,0:T(1,128)}), f32[32,1,128]{2,1,0:T(1,128)S(1)}, u32[]{:S(2)}, u32[]{:S(2)}) async-start(f32[32,1,128]{2,1,0:T(1,128)} %broadcast_in_dim.7), calls=%async_computation.2 | async-start | bytes 32768 | tf_op jit(solution)/shard_map/all_to_all | solution.py:228
  155.1 13.1 %all-to-all-start.3 = ((f32[16,1,128]{2,1,0:T(1,128)}), f32[16,1,128]{2,1,0:T(1,128)S(1)}, u32[]{:S(2)}, u32[]{:S(2)}) async-start(f32[16,1,128]{2,1,0:T(1,128)} %broadcast_in_dim.16), calls=%async_computation.3 | async-start | bytes 16384 | tf_op jit(solution)/shard_map/all_to_all | solution.py:228

commit v3 on v2

v3 whole, which is shorter than its diff:
```python
import functools

import jax
import jax.numpy as jnp
from jax import lax
from jax.experimental import pallas as pl
from jax.experimental.pallas import tpu as pltpu
from jax.sharding import Mesh, PartitionSpec as P

SHELL = 64
SHELLS = 12
TILES = 16
AXES = ("z", "x", "yl", "yh", "core")
CHIPS = ("z", "x", "yl", "yh")
PAIR = ("z", "x", "yl")
GRP = ("yh", "core")
F32 = jnp.float32
BF16 = jnp.bfloat16
VMEM = pl.BlockSpec(memory_space=pltpu.VMEM)
SMEM = pl.BlockSpec(memory_space=pltpu.SMEM)
HBM = pl.BlockSpec(memory_space=pltpu.HBM)
TRANSPOSED = (((0,), (0,)), ((), ()))


def lanes(shape):
    return lax.broadcasted_iota(jnp.int32, shape, 1)


def grant(mib):
    return pltpu.CompilerParams(vmem_limit_bytes=mib * 1024 * 1024)


def rows(shape):
    return lax.broadcasted_iota(jnp.int32, shape, 0)


def half_kernel(blocks, screen, c_occ, ints, out, held, spread, coef, sems):
    count = held.shape[0]
    for b in range(count):
        pltpu.make_async_copy(ints.at[b], held.at[b], sems.at[b]).start()
    shape = (SHELL, 4096)
    spread[...] = (lanes(shape) // SHELL == rows(shape)).astype(F32).astype(BF16)
    left = lanes((32, 128)) < SHELL

    @pl.loop(0, count)
    def _(block):
        first = blocks[0, block]
        at = pl.multiple_of((first // 2) * 128, 128)
        own = pltpu.roll(c_occ[:, pl.ds(at, 128)].astype(F32), (first % 2) * SHELL, 1)[:, :SHELL]
        wide = jnp.dot(own.astype(BF16), spread[...], preferred_element_type=F32)
        coef[...] = wide * screen[block].astype(F32)
        pltpu.make_async_copy(ints.at[block], held.at[block], sems.at[block]).wait()

        def step(t, sums):
            at = pl.multiple_of(t * 128, 128)
            tile = held[block, :, pl.ds(at, 128)].astype(F32)
            weights = coef[:, pl.ds(at, 128)]
            return tuple(sums[i] + tile * weights[i : i + 1] for i in range(8))

        sums = lax.fori_loop(0, 32, step, (jnp.zeros((32, 128), F32),) * 8, unroll=8)
        full = [s + pltpu.roll(s, SHELL, 1) for s in sums]
        shell = blocks[1, block].astype(F32)
        put = pl.multiple_of(block * 16, 16)
        for yh in range(4):
            both = jnp.where(left, full[2 * yh], full[2 * yh + 1])
            for core in range(2):
                d = yh * 2 + core
                out[d, pl.ds(put, 16), :] = both[core * 16 : core * 16 + 16]
                out[d, 64:72, :] = jnp.where(rows((8, 128)) == block, shell, out[d, 64:72, :])


def half_transform(c_occ, ints, blocks, screen):
    return pl.pallas_call(
        half_kernel,
        out_shape=jax.ShapeDtypeStruct((8, 72, 128), F32),
        in_specs=[SMEM, SMEM, VMEM, HBM],
        out_specs=VMEM,
        scratch_shapes=[
            pltpu.VMEM(ints.shape, BF16),
            pltpu.VMEM((SHELL, 4096), BF16),
            pltpu.VMEM((8, 4096), F32),
            pltpu.SemaphoreType.DMA((ints.shape[0],)),
        ],
        compiler_params=grant(6),
        name="half",
    )(blocks.T, screen, c_occ.T, ints)


def rounded(x):
    return x.astype(BF16).astype(F32)


def transform_kernel(recv, c_vir, bmat, wide, thin, held, terms, sides, sems):
    copies = []
    for q in range(TILES // 2):
        columns = pl.ds(q * 256, 256)
        copies.append(pltpu.make_async_copy(c_vir.at[:, columns], held.at[:, columns], sems.at[q]))
        copies[q].start()
    left = lanes((16, 128)) < SHELL
    sums = [jnp.zeros((16, 128), F32) for _ in range(SHELLS)]
    for source in range(8):
        for b in range(4):
            data = recv[source, b * 16 : b * 16 + 16, :]
            shell = recv[source, 64 + b : 65 + b, :]
            for n in range(SHELLS):
                sums[n] = sums[n] + jnp.where(shell == float(n), data, 0.0)
    for m in range(SHELLS // 2):
        one, two = sums[2 * m], sums[2 * m + 1]
        pair = (
            jnp.where(left, one, pltpu.roll(two, SHELL, 1)),
            jnp.where(left, pltpu.roll(one, SHELL, 1), two),
        )
        for i in range(2):
            value = pair[i]
            for term in range(3):
                part = rounded(value)
                terms[term * 32 + i * 16 : term * 32 + i * 16 + 16, m * 128 : m * 128 + 128] = part.astype(BF16)
                value = value - part
    for q in range(TILES // 2):
        copies[q].wait()
        got = jnp.dot(terms[...], held[:, q * 256 : q * 256 + 256], preferred_element_type=F32)
        full = (got[64:96] + got[32:64]) + got[0:32]
        bmat[:, q * 256 : q * 256 + 256] = full.astype(BF16)
        for t in range(2):
            one, two = full[0:16, t * 128 : t * 128 + 128], full[16:32, t * 128 : t * 128 + 128]
            tile = q * 2 + t
            sides[tile * 2] = jnp.where(left, one, pltpu.roll(two, SHELL, 1)).astype(BF16)
            sides[tile * 2 + 1] = jnp.where(left, pltpu.roll(one, SHELL, 1), two).astype(BF16)
    for r in range(TILES):
        for yh in range(4):
            wide[r * 4 + yh] = bmat[:, r * 128 : r * 128 + 128]
            for x in range(4):
                kind = x * 4 + yh
                other = (r + kind // 2 + 1) % TILES
                thin[((r // 2 * 4 + x) * 2 + r % 2) * 4 + yh] = sides[other * 2 + kind % 2]


def transform(recv, c_vir):
    return pl.pallas_call(
        transform_kernel,
        out_shape=(
            jax.ShapeDtypeStruct((32, c_vir.shape[1]), BF16),
            jax.ShapeDtypeStruct((64, 32, 128), BF16),
            jax.ShapeDtypeStruct((256, 16, 128), BF16),
        ),
        in_specs=[VMEM, HBM],
        out_specs=(VMEM, VMEM, VMEM),
        scratch_shapes=[
            pltpu.VMEM(c_vir.shape, BF16),
            pltpu.VMEM((96, c_vir.shape[0]), BF16),
            pltpu.VMEM((32, 16, 128), BF16),
            pltpu.SemaphoreType.DMA((TILES // 2,)),
        ],
        compiler_params=grant(10),
        name="transform",
    )(recv, c_vir)


def gram_kernel(place, tiles, sides, _, keep, give, wide, all_t, all_s):
    core, side, own = place[4], place[3], place[5]
    mine = []
    for x in range(4):
        for i in range(8):
            wide[x * 256 : x * 256 + 256, i * 128 : i * 128 + 128] = tiles[x, :, i].reshape(256, 128)
        mine.append(tiles[x, :, own].reshape(256, 128))
    for p in range(4):
        thin = jnp.concatenate([sides[:, x, :, p].reshape(256, 128) for x in range(4)], axis=0)
        all_t[p * 128 : p * 128 + 128, :] = lax.dot_general(thin, wide[...], TRANSPOSED, preferred_element_type=F32)
    mine = jnp.concatenate(mine, axis=0)
    others = wide[:, pl.ds(pl.multiple_of(side * 512, 512), 512)]
    all_s[...] = lax.dot_general(mine, others, TRANSPOSED, preferred_element_type=F32)
    for which, target in ((core, keep), (1 - core, give)):
        for j in range(8):
            at = pl.multiple_of(j * 64 + which * 32, 32)
            target[j * 32 : j * 32 + 32, :] = all_t[pl.ds(at, 32), :]
        for q in range(4):
            at = pl.multiple_of(which * 256, 256)
            target[256:288, q * 256 : q * 256 + 256] = all_s[q * 32 : q * 32 + 32, pl.ds(at, 256)]


def gram(place, tiles, sides, after):
    shape = jax.ShapeDtypeStruct((288, 1024), F32)
    return pl.pallas_call(
        gram_kernel,
        out_shape=(shape, shape),
        in_specs=[SMEM, VMEM, VMEM, HBM],
        out_specs=(VMEM, VMEM),
        scratch_shapes=[
            pltpu.VMEM((1024, 1024), BF16),
            pltpu.VMEM((512, 1024), F32),
            pltpu.VMEM((128, 512), F32),
        ],
        compiler_params=grant(16),
        name="gram",
    )(place, tiles.reshape(4, 16, 8, 16, 128), sides.reshape(8, 4, 2, 4, 16, 128), after)


def energy_kernel(scale, place, eps_occ, keep, got, eps_vir, out, parts):
    tile, other, step, side, core, own = (place[n] for n in range(6))
    row_a = eps_vir[pl.ds(tile, 1), :]
    row_b = eps_vir[pl.ds(other, 1), :]
    first = side * 64 + core * 32
    col_b = jnp.sum(jnp.where(lanes((32, 128)) == rows((32, 128)) + first, row_b, 0.0), axis=1, keepdims=True)
    weight = jnp.where(step == 8, 1.0, 2.0)
    for i in range(8):
        for j in range(i, 8):
            there = slice(j * 32, j * 32 + 32), slice(i * 128, i * 128 + 128)
            here = slice(i * 32, i * 32 + 32), slice(j * 128, j * 128 + 128)
            one = keep[there] + got[there]
            two = keep[here] + got[here]
            denominators = (eps_occ[i] + eps_occ[j] - row_a) - col_b
            terms = (one * one + two * two - one * two) / denominators
            part = jnp.sum(terms, axis=0, keepdims=True) * weight
            parts[i * 8 + j : i * 8 + j + 1, :] = part
            parts[j * 8 + i : j * 8 + i + 1, :] = part
    square = (128, 128)
    eye = lanes(square) == rows(square)
    col_a = jnp.sum(jnp.where(eye, row_a, 0.0), axis=1, keepdims=True)
    for m in range(2):
        j = side * 4 + core * 2 + m
        block = jnp.concatenate(
            [
                keep[256:288, q * 256 + m * 128 : q * 256 + m * 128 + 128]
                + got[256:288, q * 256 + m * 128 : q * 256 + m * 128 + 128]
                for q in range(4)
            ],
            axis=0,
        )
        denominators = (eps_occ[own] + eps_occ[j] - row_a) - col_a
        terms = block * (2.0 * block - block.T) / denominators
        at = pl.ds(own * 8 + j, 1)
        parts[at, :] = parts[at, :] + jnp.sum(terms, axis=0, keepdims=True)
    column = jnp.sum(parts[...], axis=1, keepdims=True) * scale
    row = jnp.sum(jnp.where(lanes((64, 128)) == rows((64, 128)), column, 0.0), axis=0, keepdims=True)
    out[...] = jnp.broadcast_to(row[None], out.shape)


def energies(scale, place, eps_occ, keep, got, eps_vir):
    return pl.pallas_call(
        functools.partial(energy_kernel, scale),
        out_shape=jax.ShapeDtypeStruct((32, 1, 128), F32),
        in_specs=[SMEM, SMEM, VMEM, VMEM, VMEM],
        out_specs=VMEM,
        scratch_shapes=[pltpu.VMEM((64, 128), F32)],
        compiler_params=grant(6),
        name="energies",
    )(place, eps_occ, keep, got, eps_vir.reshape(-1, 128))


def position():
    z, x, yl, yh, core = (lax.axis_index(axis) for axis in AXES)
    tile, kind = z * 2 + yl, x * 4 + yh
    step, side = lax.shift_right_logical(kind, 1) + 1, kind & 1
    return jnp.stack([tile, (tile + step) & (TILES - 1), step, side, core, lax.shift_right_logical(kind, 1)])


def again_kernel(got, out):
    out[...] = jnp.broadcast_to(jnp.sum(got[...], axis=0)[None], out.shape)


def last_kernel(got, out):
    row = jnp.broadcast_to(jnp.sum(got[...], axis=0), (8, 128))
    place = rows((8, 128))
    square = row
    for i in range(1, 8):
        square = jnp.where(place == i, pltpu.roll(row, 128 - 8 * i, 1), square)
    out[...] = square[:, :8]


def body(c_occ, c_vir, ints, blocks, screen, eps_occ, eps_vir):
    vir, occ = c_vir.shape[1], c_occ.shape[1]
    place = position()
    core = lax.axis_index("core")
    swap = [(0, 1), (1, 0)]
    sent = half_transform(c_occ, ints, blocks, screen)
    recv = lax.all_to_all(sent, GRP, 0, 0, tiled=True)
    two, wide, thin = transform(recv, c_vir)
    tiles = lax.all_to_all(wide, ("z", "yl", "yh"), 0, 0, tiled=True)
    tiles = lax.all_gather(tiles, "x")
    sides = lax.all_to_all(thin, CHIPS, 0, 0, tiled=True)

    two = two.reshape(2, 16, vir)
    mine = lax.dynamic_index_in_dim(two, core, 0, keepdims=False)
    others = lax.ppermute(lax.dynamic_index_in_dim(two, 1 - core, 0, keepdims=False), "core", swap)
    bmat = jnp.where(core == 0, jnp.stack([mine, others]), jnp.stack([others, mine]))

    keep, give = gram(place, tiles, sides, others)
    got = lax.ppermute(give, "core", swap)
    scale = 1.0 / (float(vir) * float(vir) * 2048.0)
    energy = energies(scale, place, eps_occ, keep, got, eps_vir)
    energy = lax.all_to_all(energy, ("z", "x"), 0, 0, tiled=True)
    energy = pl.pallas_call(again_kernel, out_shape=jax.ShapeDtypeStruct((16, 1, 128), F32), name="again")(energy)
    energy = lax.all_to_all(energy, ("yh", "yl", "core"), 0, 0, tiled=True)
    energy = pl.pallas_call(last_kernel, out_shape=jax.ShapeDtypeStruct((occ, occ), F32), name="last")(energy)
    return bmat.reshape(1, 32, vir), energy


def solution(mesh):
    fine = Mesh(mesh.devices.reshape(8, 4, 2, 4, 2), AXES)
    return jax.shard_map(
        body,
        mesh=fine,
        in_specs=(P(), P(), P(GRP, PAIR, None), P(GRP, None), P(GRP), P(), P()),
        out_specs=(P(GRP, PAIR, None), P()),
        check_vma=False,
    )
```

time: 170 us -> 168 us (0.988)
  waiting for transfers between devices: 88.1 us -> 44.1 us
  blocking collectives: 20.6 us -> 51.1 us
  between operations: 0.82 us -> 14.1 us
  Pallas kernels: 9.11 us -> 15.2 us
  local copies, waits for them, and re-layouts: 13.7 us -> 8.04 us
  starting transfers between devices: 35.9 us -> 33.8 us
    all_to_all x3, waiting for transfers between devices: 87.4 us -> 37.5 us  [the longest x1 22.7 us: body(): sides = lax.all_to_all(thin, CHIPS, 0, 0, tiled=True)]
    all_to_all x0 -> x1, blocking collectives: none -> 30.5 us  [body(): tiles = lax.all_to_all(wide, ('z', 'yl', 'yh'), 0, 0, tiled=True)]
    unnamed x22 -> x20, local copies, waits for them, and re-layouts: 11.6 us -> 7.95 us
    pallas_call x1, Pallas kernels: 1.41 us -> 5.05 us  [transform(): pl.pallas_call(transform_kernel, out_shape=(jax.ShapeDtypeStruct((32, c_v...]
    all_gather x0 -> x1, waiting for transfers between devices: none -> 3.28 us  [body(): tiles = lax.all_gather(tiles, 'x')]
    pallas_call x0 -> x2, Pallas kernels: none -> 2.73 us  [the longest x1 1.38 us: body(): pl.pallas_call(last_kernel, out_shape=jax.ShapeDtypeStruct((occ, occ), F3...]
    all_to_all x3, starting transfers between devices: 29.9 us -> 28 us  [the longest x1 11.6 us: body(): sides = lax.all_to_all(thin, CHIPS, 0, 0, tiled=True)]
    ppermute x1, waiting for transfers between devices: 0.71 us -> 2.45 us  [body(): got = lax.ppermute(give, 'core', swap)]
  transfers between devices with their start and end apart: 5 -> 6, of which waited for: 4 -> 6; matrix products, arithmetic and copies ran while one was open for 1% -> 0% of each run, Pallas kernels for 1% -> 0%
where the time goes in v3:
time: 168 us; the launch traced here: 167 us
  blocking collectives  51.1 us (30%)
  waiting for transfers between devices  44.1 us (26%)
  starting transfers between devices  33.8 us (20%)
  Pallas kernels  15.2 us (9%)
  between operations  14.1 us (8%)
  local copies, waits for them, and re-layouts  8.04 us (5%)
    all_to_all x1, blocking collectives, body(): tiles = lax.all_to_all(wide, ('z', 'yl', 'yh'), 0, 0, tiled=True)  30.5 us
    all_to_all x1, waiting for transfers between devices, body(): sides = lax.all_to_all(thin, CHIPS, 0, 0, tiled=True)  22.7 us
    all_to_all x1, blocking collectives, body(): recv = lax.all_to_all(sent, GRP, 0, 0, tiled=True)  20.6 us
    all_to_all x1, starting transfers between devices, body(): sides = lax.all_to_all(thin, CHIPS, 0, 0, tiled=True)  11.6 us
    all_to_all x1, waiting for transfers between devices, body(): energy = lax.all_to_all(energy, ('z', 'x'), 0, 0, tiled=True)  8.5 us
    all_to_all x1, starting transfers between devices, body(): energy = lax.all_to_all(energy, ('yh', 'yl', 'core'), 0, 0, tiled=True)  8.31 us
    all_to_all x1, starting transfers between devices, body(): energy = lax.all_to_all(energy, ('z', 'x'), 0, 0, tiled=True)  8.06 us
    unnamed x20, local copies, waits for them, and re-layouts  7.95 us
  transfers between devices with their start and end apart: 6, of which 6 were waited for; matrix products, arithmetic and copies ran while one was open for 0% of the time, Pallas kernels for 0%

profile of v3, /device:TPU:1, one launch (start us, length us, event | category | flops | bytes accessed | tf_op | source)
XLA Modules:
  0.0 167.0 jit_solution(11520284611985920072)
XLA Ops:
  7.2 0.0 all-gather.3.cloned.1.call-start
  7.2 0.0 copy-start.2
  7.2 1.2 copy-done.2
  8.4 0.0 copy-start.3
  8.4 0.7 copy-done.3
  9.1 0.0 copy-start.5
  9.1 0.7 copy-done.5
  9.8 0.0 copy-start.6
  9.8 0.7 copy-done.6
  10.5 3.5 %half.1 = f32[8,72,128]{2,1,0:T(8,128)S(1)} custom-call(s32[2,4]{1,0:T(2,128)S(1)} %bitcast.22, s32[4]{0:T(128)S(1)} %copy-done.6, bf16[8,768]{1,0:T(8,128)(2,1)S(1)} %bitcast.20, bf16[4,32,4096]{2,1,0:T(8,128)(2,1)S(1)} %copy-done.2), custom_call_target="tpu_custom_call" | custom-call | tf_op jit(solution)/shard_map/half/pallas_call | solution.py:73
  14.0 20.6 %all_to_all.25.recv = f32[8,72,128]{2,1,0:T(8,128)S(1)} all-to-all(f32[8,72,128]{2,1,0:T(8,128)S(1)} %half.1), channel_id=1, replica_groups=mesh['z'=8,'x'=4,'yl'=2,'yh'=4,'core'=2] {'yh','core'}, dimensions={0} | all-to-all | bytes 589824 | tf_op jit(solution)/shard_map/all_to_all | solution.py:276
  34.6 0.0 copy-start
  34.6 1.9 %copy-done = bf16[768,2048]{1,0:T(8,128)(2,1)S(1)} copy-done((bf16[768,2048]{1,0:T(8,128)(2,1)S(1)}, bf16[768,2048]{1,0:T(8,128)(2,1)}, u32[]{:S(2)}) %copy-start) | copy-done | bytes 3145752
  36.5 5.1 %transform.1 = (bf16[32,2048]{1,0:T(8,128)(2,1)S(1)}, bf16[64,32,128]{2,1,0:T(8,128)(2,1)S(1)}, bf16[256,16,128]{2,1,0:T(8,128)(2,1)}) custom-call(f32[8,72,128]{2,1,0:T(8,128)S(1)} %all_to_all.25.recv, bf16[768,2048]{1,0:T(8,128)(2,1)S(1)} %copy-done), custom_call_target="tpu_custom_call" | custom-call | tf_op jit(solution)/shard_map/transform/pallas_call | solution.py:139
  41.6 30.5 %all_to_all.26 = bf16[64,32,128]{2,1,0:T(8,128)(2,1)} all-to-all(bf16[64,32,128]{2,1,0:T(8,128)(2,1)S(1)} %get-tuple-element.8), channel_id=1, replica_groups=mesh['z'=8,'x'=4,'yl'=2,'yh'=4,'core'=2] {'z','yl','yh'}, dimensions={0} | all-to-all | bytes 1048576 | tf_op jit(solution)/shard_map/all_to_all | solution.py:278
  72.0 0.0 all-gather.3.cloned.1.call-update
  72.1 11.6 %all-to-all-start.2 = ((bf16[256,16,128]{2,1,0:T(8,128)(2,1)}), bf16[256,16,128]{2,1,0:T(8,128)(2,1)S(1)}, u32[]{:S(2)}, u32[]{:S(2)}) async-start(bf16[256,16,128]{2,1,0:T(8,128)(2,1)} %get-tuple-element.9), calls=%async_computation.2 | async-start | bytes 2097152 | tf_op jit(solution)/shard_map/all_to_all | solution.py:280
  83.7 3.2 %collective-permute-start = (bf16[16,2048]{1,0:T(8,128)(2,1)S(1)}, bf16[16,2048]{1,0:T(8,128)(2,1)S(1)}, u32[]{:S(2)}, u32[]{:S(2)}) collective-permute-start(bf16[16,2048]{1,0:T(8,128)(2,1)S(1)} %get-tuple-element.13), channel_id=1, source_target_pairs={{0,1},{1,0},{2,3},{3,2},{4,5},{5,4},{6,7},{7,6},{8,9},{9,8},{10,11... | collective-permute-start | bytes 196616 | tf_op jit(solution)/shard_map/ppermute | solution.py:284
  86.9 0.1 stack.42.place
  87.0 0.8 collective-permute-done._
  87.8 22.7 %all-to-all-done.2 = bf16[256,16,128]{2,1,0:T(8,128)(2,1)S(1)} async-done(((bf16[256,16,128]{2,1,0:T(8,128)(2,1)}), bf16[256,16,128]{2,1,0:T(8,128)(2,1)S(1)}, u32[]{:S(2)}, u32[]{:S(2)}) %all-to-all-start.2) | async-done | bytes 1048608 | tf_op jit(solution)/shard_map/all_to_all | solution.py:280
  110.5 3.3 %all-gather.3.cloned.1.call-done = bf16[256,32,128]{2,1,0:T(8,128)(2,1)} async-done(((bf16[64,32,128]{2,1,0:T(8,128)(2,1)}), bf16[256,32,128]{2,1,0:T(8,128)(2,1)}) %all-gather.3.cloned.1.call-update) | async-done | bytes 2097168 | tf_op jit(solution)/shard_map/all_gather | solution.py:279
  113.7 0.0 copy-start.1
  113.8 1.6 copy-done.1
  115.3 0.0 copy-start.4
  115.3 0.0 copy-start.7
  115.3 2.3 %gram.1 = (f32[288,1024]{1,0:T(8,128)S(1)}, f32[288,1024]{1,0:T(8,128)S(1)}) custom-call(s32[6]{0:T(128)S(1)} %stack.42.place, bf16[4,16,8,16,128]{4,3,2,1,0:T(8,128)(2,1)S(1)} %bitcast.17, bf16[8,4,2,4,16,128]{5,4,3,2,1,0:T(8,128)(2,1)S(1)} %bitcast.16, bf16[16,2048]{1,0:T(8,128)(2,1)S(1)} %collective-permute-done._), custom_call_target="tpu_custom_call" | custom-call | tf_op jit(solution)/shard_map/gram/pallas_call | solution.py:183
  117.7 2.6 %collective-permute-start.1 = (f32[288,1024]{1,0:T(8,128)S(1)}, f32[288,1024]{1,0:T(8,128)S(1)}, u32[]{:S(2)}, u32[]{:S(2)}) collective-permute-start(f32[288,1024]{1,0:T(8,128)S(1)} %get-tuple-element.11), channel_id=1, source_target_pairs={{0,1},{1,0},{2,3},{3,2},{4,5},{5,4},{6,7},{7,6},{8,9},{9,8},{10,11... | collective-permute-start | bytes 3538952 | tf_op jit(solution)/shard_map/ppermute | solution.py:288
  120.2 2.5 %collective-permute-done.1.got = f32[288,1024]{1,0:T(8,128)S(1)} collective-permute-done((f32[288,1024]{1,0:T(8,128)S(1)}, f32[288,1024]{1,0:T(8,128)S(1)}, u32[]{:S(2)}, u32[]{:S(2)}) %collective-permute-start.1) | collective-permute-done | bytes 1179680 | tf_op jit(solution)/shard_map/ppermute | solution.py:288
  122.7 0.0 copy-done.4
  122.7 0.0 copy-done.7
  122.7 1.6 energies.1
  124.3 8.1 %all-to-all-start.3 = ((f32[32,1,128]{2,1,0:T(1,128)}), f32[32,1,128]{2,1,0:T(1,128)S(1)}, u32[]{:S(2)}, u32[]{:S(2)}) async-start(f32[32,1,128]{2,1,0:T(1,128)} %energies.1), calls=%async_computation.3 | async-start | bytes 32768 | tf_op jit(solution)/shard_map/all_to_all | solution.py:291
  132.4 8.5 %all-to-all-done.3.got = f32[32,1,128]{2,1,0:T(1,128)S(1)} async-done(((f32[32,1,128]{2,1,0:T(1,128)}), f32[32,1,128]{2,1,0:T(1,128)S(1)}, u32[]{:S(2)}, u32[]{:S(2)}) %all-to-all-start.3) | async-done | bytes 16416 | tf_op jit(solution)/shard_map/all_to_all | solution.py:291
  140.9 0.0 copy-start.8
  140.9 0.6 copy-done.8
  141.5 1.4 again.1
  142.8 8.3 %all-to-all-start.4 = ((f32[16,1,128]{2,1,0:T(1,128)}), f32[16,1,128]{2,1,0:T(1,128)S(1)}, u32[]{:S(2)}, u32[]{:S(2)}) async-start(f32[16,1,128]{2,1,0:T(1,128)} %again.1), calls=%async_computation.4 | async-start | bytes 16384 | tf_op jit(solution)/shard_map/all_to_all | solution.py:293
  151.1 0.7 maximum_select_fusion
  151.8 6.4 %all-to-all-done.4.got = f32[16,1,128]{2,1,0:T(1,128)S(1)} async-done(((f32[16,1,128]{2,1,0:T(1,128)}), f32[16,1,128]{2,1,0:T(1,128)S(1)}, u32[]{:S(2)}, u32[]{:S(2)}) %all-to-all-start.4) | async-done | bytes 8224 | tf_op jit(solution)/shard_map/all_to_all | solution.py:293
  158.2 0.0 copy-start.9
  158.2 0.6 copy-done.9
  158.8 1.4 last.1
  (1 shorter events, 0.0 us)
Async XLA Ops:
  7.2 106.6 %all-gather.3.cloned.1.call-start = ((), (), s32[]{:S(2)}) async-start(), calls=%async_computation.5 | async-start | bytes 2621440 | tf_op jit(solution)/shard_map/all_gather | solution.py:279
  7.2 1.2 copy-start.2
  8.4 0.7 copy-start.3
  9.1 0.7 copy-start.5
  9.8 0.7 copy-start.6
  34.6 1.9 %copy-start = (bf16[768,2048]{1,0:T(8,128)(2,1)S(1)}, bf16[768,2048]{1,0:T(8,128)(2,1)}, u32[]{:S(2)}) copy-start(bf16[768,2048]{1,0:T(8,128)(2,1)} %c_vir.1) | copy-start | bytes 9437188
  72.1 38.4 %all-to-all-start.2 = ((bf16[256,16,128]{2,1,0:T(8,128)(2,1)}), bf16[256,16,128]{2,1,0:T(8,128)(2,1)S(1)}, u32[]{:S(2)}, u32[]{:S(2)}) async-start(bf16[256,16,128]{2,1,0:T(8,128)(2,1)} %get-tuple-element.9), calls=%async_computation.2 | async-start | bytes 2097152 | tf_op jit(solution)/shard_map/all_to_all | solution.py:280
  83.7 4.1 %collective-permute-start = (bf16[16,2048]{1,0:T(8,128)(2,1)S(1)}, bf16[16,2048]{1,0:T(8,128)(2,1)S(1)}, u32[]{:S(2)}, u32[]{:S(2)}) collective-permute-start(bf16[16,2048]{1,0:T(8,128)(2,1)S(1)} %get-tuple-element.13), channel_id=1, source_target_pairs={{0,1},{1,0},{2,3},{3,2},{4,5},{5,4},{6,7},{7,6},{8,9},{9,8},{10,11... | collective-permute-start | bytes 196616 | tf_op jit(solution)/shard_map/ppermute | solution.py:284
  113.7 1.6 copy-start.1
  115.3 7.4 %copy-start.4 = (f32[2048]{0:T(1024)S(1)}, f32[2048]{0:T(1024)}, u32[]{:S(2)}) copy-start(f32[2048]{0:T(1024)} %param.13) | copy-start | bytes 24580
  115.3 7.4 %copy-start.7 = (f32[8]{0:T(128)S(1)}, f32[8]{0:T(128)}, u32[]{:S(2)}) copy-start(f32[8]{0:T(128)} %eps_occ.1) | copy-start | bytes 100
  117.7 5.0 %collective-permute-start.1 = (f32[288,1024]{1,0:T(8,128)S(1)}, f32[288,1024]{1,0:T(8,128)S(1)}, u32[]{:S(2)}, u32[]{:S(2)}) collective-permute-start(f32[288,1024]{1,0:T(8,128)S(1)} %get-tuple-element.11), channel_id=1, source_target_pairs={{0,1},{1,0},{2,3},{3,2},{4,5},{5,4},{6,7},{7,6},{8,9},{9,8},{10,11... | collective-permute-start | bytes 3538952 | tf_op jit(solution)/shard_map/ppermute | solution.py:288
  124.3 16.6 %all-to-all-start.3 = ((f32[32,1,128]{2,1,0:T(1,128)}), f32[32,1,128]{2,1,0:T(1,128)S(1)}, u32[]{:S(2)}, u32[]{:S(2)}) async-start(f32[32,1,128]{2,1,0:T(1,128)} %energies.1), calls=%async_computation.3 | async-start | bytes 32768 | tf_op jit(solution)/shard_map/all_to_all | solution.py:291
  140.9 0.6 copy-start.8
  142.8 15.3 %all-to-all-start.4 = ((f32[16,1,128]{2,1,0:T(1,128)}), f32[16,1,128]{2,1,0:T(1,128)S(1)}, u32[]{:S(2)}, u32[]{:S(2)}) async-start(f32[16,1,128]{2,1,0:T(1,128)} %again.1), calls=%async_computation.4 | async-start | bytes 16384 | tf_op jit(solution)/shard_map/all_to_all | solution.py:293
  158.2 0.6 copy-start.9
Sparse Core Ops, SparseCore 0:
  72.2 41.5 all-gather.2

commit v4 on v3

--- a/solution.py
+++ b/solution.py
@@ -81,7 +81,7 @@
             pltpu.VMEM((8, 4096), F32),
             pltpu.SemaphoreType.DMA((ints.shape[0],)),
         ],
-        compiler_params=grant(6),
+        compiler_params=grant(62),
         name="half",
     )(blocks.T, screen, c_occ.T, ints)
 
@@ -151,22 +151,27 @@
             pltpu.VMEM((32, 16, 128), BF16),
             pltpu.SemaphoreType.DMA((TILES // 2,)),
         ],
-        compiler_params=grant(10),
+        compiler_params=grant(61),
         name="transform",
     )(recv, c_vir)
 
 
-def gram_kernel(place, tiles, sides, _, keep, give, wide, all_t, all_s):
-    core, side, own = place[4], place[3], place[5]
-    mine = []
-    for x in range(4):
+def gram_kernel(place, here, below, above, low, high, sides, _, keep, give, wide, thin, all_t, all_s):
+    core, side, own, x = place[4], place[3], place[5], place[6]
+    first = 0
+    for away, tiles in ((0, here), (3, below), (1, above), (2, low), (2, high)):
+        count = tiles.shape[0] * 16
         for i in range(8):
-            wide[x * 256 : x * 256 + 256, i * 128 : i * 128 + 128] = tiles[x, :, i].reshape(256, 128)
-        mine.append(tiles[x, :, own].reshape(256, 128))
+            wide[first : first + count, i * 128 : i * 128 + 128] = tiles[:, i].reshape(count, 128)
+        z = 4 if tiles is high else 0
+        for p in range(4):
+            rows_z = sides[z : z + count // 32, (x + away) & 3, :, p]
+            thin[first : first + count, p * 128 : p * 128 + 128] = rows_z.reshape(count, 128)
+        first += count
     for p in range(4):
-        thin = jnp.concatenate([sides[:, x, :, p].reshape(256, 128) for x in range(4)], axis=0)
-        all_t[p * 128 : p * 128 + 128, :] = lax.dot_general(thin, wide[...], TRANSPOSED, preferred_element_type=F32)
-    mine = jnp.concatenate(mine, axis=0)
+        part = lax.dot_general(thin[:, p * 128 : p * 128 + 128], wide[...], TRANSPOSED, preferred_element_type=F32)
+        all_t[p * 128 : p * 128 + 128, :] = part
+    mine = wide[:, pl.ds(pl.multiple_of(own * 128, 128), 128)]
     others = wide[:, pl.ds(pl.multiple_of(side * 512, 512), 512)]
     all_s[...] = lax.dot_general(mine, others, TRANSPOSED, preferred_element_type=F32)
     for which, target in ((core, keep), (1 - core, give)):
@@ -178,21 +183,23 @@
             target[256:288, q * 256 : q * 256 + 256] = all_s[q * 32 : q * 32 + 32, pl.ds(at, 256)]
 
 
-def gram(place, tiles, sides, after):
+def gram(place, here, below, above, low, high, sides, after):
     shape = jax.ShapeDtypeStruct((288, 1024), F32)
+    tiles = (block.reshape(-1, 8, 16, 128) for block in (here, below, above, low, high))
     return pl.pallas_call(
         gram_kernel,
         out_shape=(shape, shape),
-        in_specs=[SMEM, VMEM, VMEM, HBM],
+        in_specs=[SMEM] + [VMEM] * 6 + [HBM],
         out_specs=(VMEM, VMEM),
         scratch_shapes=[
             pltpu.VMEM((1024, 1024), BF16),
+            pltpu.VMEM((1024, 512), BF16),
             pltpu.VMEM((512, 1024), F32),
             pltpu.VMEM((128, 512), F32),
         ],
         compiler_params=grant(16),
         name="gram",
-    )(place, tiles.reshape(4, 16, 8, 16, 128), sides.reshape(8, 4, 2, 4, 16, 128), after)
+    )(place, *tiles, sides.reshape(8, 4, 2, 4, 16, 128), after)
 
 
 def energy_kernel(scale, place, eps_occ, keep, got, eps_vir, out, parts):
@@ -251,7 +258,7 @@
     z, x, yl, yh, core = (lax.axis_index(axis) for axis in AXES)
     tile, kind = z * 2 + yl, x * 4 + yh
     step, side = lax.shift_right_logical(kind, 1) + 1, kind & 1
-    return jnp.stack([tile, (tile + step) & (TILES - 1), step, side, core, lax.shift_right_logical(kind, 1)])
+    return jnp.stack([tile, (tile + step) & (TILES - 1), step, side, core, lax.shift_right_logical(kind, 1), x])
 
 
 def again_kernel(got, out):
@@ -265,6 +272,17 @@
     for i in range(1, 8):
         square = jnp.where(place == i, pltpu.roll(row, 128 - 8 * i, 1), square)
     out[...] = square[:, :8]
+
+
+def small(kernel, shape, name):
+    return pl.pallas_call(
+        kernel,
+        out_shape=jax.ShapeDtypeStruct(shape, F32),
+        in_specs=[VMEM],
+        out_specs=VMEM,
+        compiler_params=grant(2),
+        name=name,
+    )
 
 
 def body(c_occ, c_vir, ints, blocks, screen, eps_occ, eps_vir):
@@ -275,8 +293,11 @@
     sent = half_transform(c_occ, ints, blocks, screen)
     recv = lax.all_to_all(sent, GRP, 0, 0, tiled=True)
     two, wide, thin = transform(recv, c_vir)
-    tiles = lax.all_to_all(wide, ("z", "yl", "yh"), 0, 0, tiled=True)
-    tiles = lax.all_gather(tiles, "x")
+    here = lax.all_to_all(wide, ("z", "yl", "yh"), 0, 0, tiled=True)
+    up = [(i, (i + 1) % 4) for i in range(4)]
+    down = [(i, (i + 3) % 4) for i in range(4)]
+    below, above = lax.ppermute(here, "x", up), lax.ppermute(here, "x", down)
+    low, high = lax.ppermute(above[:32], "x", down), lax.ppermute(below[32:], "x", up)
     sides = lax.all_to_all(thin, CHIPS, 0, 0, tiled=True)
 
     two = two.reshape(2, 16, vir)
@@ -284,14 +305,14 @@
     others = lax.ppermute(lax.dynamic_index_in_dim(two, 1 - core, 0, keepdims=False), "core", swap)
     bmat = jnp.where(core == 0, jnp.stack([mine, others]), jnp.stack([others, mine]))
 
-    keep, give = gram(place, tiles, sides, others)
+    keep, give = gram(place, here, below, above, low, high, sides, others)
     got = lax.ppermute(give, "core", swap)
     scale = 1.0 / (float(vir) * float(vir) * 2048.0)
     energy = energies(scale, place, eps_occ, keep, got, eps_vir)
     energy = lax.all_to_all(energy, ("z", "x"), 0, 0, tiled=True)
-    energy = pl.pallas_call(again_kernel, out_shape=jax.ShapeDtypeStruct((16, 1, 128), F32), name="again")(energy)
+    energy = small(again_kernel, (16, 1, 128), "again")(energy)
     energy = lax.all_to_all(energy, ("yh", "yl", "core"), 0, 0, tiled=True)
-    energy = pl.pallas_call(last_kernel, out_shape=jax.ShapeDtypeStruct((occ, occ), F32), name="last")(energy)
+    energy = small(last_kernel, (occ, occ), "last")(energy)
     return bmat.reshape(1, 32, vir), energy
 
 

time: 168 us -> 157 us (0.935)
  starting transfers between devices: 33.8 us -> 48.2 us
  between operations: 14.1 us -> 0.78 us
  waiting for transfers between devices: 44.1 us -> 36.5 us
  local copies, waits for them, and re-layouts: 8.04 us -> 2.37 us
    all_to_all x1, waiting for transfers between devices: 22.7 us -> 0.01 us  [body(): sides = lax.all_to_all(thin, CHIPS, 0, 0, tiled=True)]
    ppermute x0 -> x4, waiting for transfers between devices: none -> 18.2 us  [the longest x2 18.2 us: body(): below, above = (lax.ppermute(here, 'x', up), lax.ppermute(here, 'x', down))]
    ppermute x0 -> x4, starting transfers between devices: none -> 10.6 us  [the longest x2 5.28 us: body(): below, above = (lax.ppermute(here, 'x', up), lax.ppermute(here, 'x', down))]
    unnamed x20 -> x4, local copies, waits for them, and re-layouts: 7.95 us -> 0.01 us
    all_gather x1 -> x0, waiting for transfers between devices: 3.28 us -> none  [body(): tiles = lax.all_gather(tiles, 'x')]
    ppermute x1, starting transfers between devices: 2.56 us -> 5.13 us  [body(): got = lax.ppermute(give, 'core', swap)]
  transfers between devices with their start and end apart: 6 -> 9, of which waited for: 6 -> 5; matrix products, arithmetic and copies ran while one was open for 0% -> 2% of each run, Pallas kernels for 0% -> 0%
where the time goes in v4:
time: 157 us; the launch traced here: 156 us
  blocking collectives  51.5 us (33%)
  starting transfers between devices  48.2 us (31%)
  waiting for transfers between devices  36.5 us (23%)
  Pallas kernels  16.1 us (10%)
  local copies, waits for them, and re-layouts  2.37 us (2%)
    all_to_all x1, blocking collectives, body(): here = lax.all_to_all(wide, ('z', 'yl', 'yh'), 0, 0, tiled=True)  29.3 us
    all_to_all x1, blocking collectives, body(): recv = lax.all_to_all(sent, GRP, 0, 0, tiled=True)  22.2 us
    ppermute x2, waiting for transfers between devices, body(): below, above = (lax.ppermute(here, 'x', up), lax.ppermute(here, 'x', down))  18.2 us
    all_to_all x1, starting transfers between devices, body(): sides = lax.all_to_all(thin, CHIPS, 0, 0, tiled=True)  11.6 us
    all_to_all x1, starting transfers between devices, body(): energy = lax.all_to_all(energy, ('yh', 'yl', 'core'), 0, 0, tiled=True)  8.85 us
    all_to_all x1, waiting for transfers between devices, body(): energy = lax.all_to_all(energy, ('z', 'x'), 0, 0, tiled=True)  8.5 us
    all_to_all x1, starting transfers between devices, body(): energy = lax.all_to_all(energy, ('z', 'x'), 0, 0, tiled=True)  7.62 us
    all_to_all x1, waiting for transfers between devices, body(): energy = lax.all_to_all(energy, ('yh', 'yl', 'core'), 0, 0, tiled=True)  6.34 us
  transfers between devices with their start and end apart: 9, of which 5 were waited for; matrix products, arithmetic and copies ran while one was open for 2% of the time, Pallas kernels for 0%

profile of v4, /device:TPU:1, one launch (start us, length us, event | category | flops | bytes accessed | tf_op | source)
XLA Modules:
  0.0 156.1 jit_solution(17736079518818950572)
XLA Ops:
  0.6 5.0 %half.1 = f32[8,72,128]{2,1,0:T(8,128)} custom-call(s32[2,4]{1,0:T(2,128)} %bitcast.32, s32[4]{0:T(128)} %screen.1, bf16[8,768]{1,0:T(8,128)(2,1)} %bitcast.31, bf16[4,32,4096]{2,1,0:T(8,128)(2,1)} %ints.1), custom_call_target="tpu_custom_call" | custom-call | tf_op jit(solution)/shard_map/half/pallas_call | solution.py:73
  5.6 22.2 %all_to_all.25.recv = f32[8,72,128]{2,1,0:T(8,128)} all-to-all(f32[8,72,128]{2,1,0:T(8,128)} %half.1), channel_id=1, replica_groups=mesh['z'=8,'x'=4,'yl'=2,'yh'=4,'core'=2] {'yh','core'}, dimensions={0} | all-to-all | bytes 589824 | tf_op jit(solution)/shard_map/all_to_all | solution.py:294
  27.8 5.8 %transform.1 = (bf16[32,2048]{1,0:T(8,128)(2,1)}, bf16[64,32,128]{2,1,0:T(8,128)(2,1)}, bf16[256,16,128]{2,1,0:T(8,128)(2,1)}) custom-call(f32[8,72,128]{2,1,0:T(8,128)} %all_to_all.25.recv, bf16[768,2048]{1,0:T(8,128)(2,1)} %c_vir.1), custom_call_target="tpu_custom_call" | custom-call | tf_op jit(solution)/shard_map/transform/pallas_call | solution.py:139
  33.6 29.3 %all_to_all.26 = bf16[64,32,128]{2,1,0:T(8,128)(2,1)S(1)} all-to-all(bf16[64,32,128]{2,1,0:T(8,128)(2,1)} %get-tuple-element.8), channel_id=1, replica_groups=mesh['z'=8,'x'=4,'yl'=2,'yh'=4,'core'=2] {'z','yl','yh'}, dimensions={0} | all-to-all | bytes 1048576 | tf_op jit(solution)/shard_map/all_to_all | solution.py:296
  62.9 11.6 %all-to-all-start.2 = ((bf16[256,16,128]{2,1,0:T(8,128)(2,1)}), bf16[256,16,128]{2,1,0:T(8,128)(2,1)S(1)}, u32[]{:S(2)}, u32[]{:S(2)}) async-start(bf16[256,16,128]{2,1,0:T(8,128)(2,1)} %get-tuple-element.9), calls=%async_computation.2 | async-start | bytes 2097152 | tf_op jit(solution)/shard_map/all_to_all | solution.py:301
  74.5 2.9 %collective-permute-start.2 = (bf16[64,32,128]{2,1,0:T(8,128)(2,1)S(1)}, bf16[64,32,128]{2,1,0:T(8,128)(2,1)S(1)}, u32[]{:S(2)}, u32[]{:S(2)}) collective-permute-start(bf16[64,32,128]{2,1,0:T(8,128)(2,1)S(1)} %all_to_all.26), channel_id=1, source_target_pairs={{0,48},{16,0},{32,16},{48,32},{1,49},{17,1},{33,17},{49,33},{2,50}... | collective-permute-start | bytes 1572872 | tf_op jit(solution)/shard_map/ppermute | solution.py:299
  77.3 2.4 %collective-permute-start.1 = (bf16[64,32,128]{2,1,0:T(8,128)(2,1)S(1)}, bf16[64,32,128]{2,1,0:T(8,128)(2,1)S(1)}, u32[]{:S(2)}, u32[]{:S(2)}) collective-permute-start(bf16[64,32,128]{2,1,0:T(8,128)(2,1)S(1)} %all_to_all.26), channel_id=1, source_target_pairs={{0,16},{16,32},{32,48},{48,0},{1,17},{17,33},{33,49},{49,1},{2,18}... | collective-permute-start | bytes 1572872 | tf_op jit(solution)/shard_map/ppermute | solution.py:299
  79.8 18.2 %collective-permute-done.2 = bf16[64,32,128]{2,1,0:T(8,128)(2,1)S(1)} collective-permute-done((bf16[64,32,128]{2,1,0:T(8,128)(2,1)S(1)}, bf16[64,32,128]{2,1,0:T(8,128)(2,1)S(1)}, u32[]{:S(2)}, u32[]{:S(2)}) %collective-permute-start.2) | collective-permute-done | bytes 524320 | tf_op jit(solution)/shard_map/ppermute | solution.py:299
  98.0 3.3 %collective-permute-start.3 = (bf16[32,32,128]{2,1,0:T(8,128)(2,1)S(1)}, bf16[32,32,128]{2,1,0:T(8,128)(2,1)S(1)}, u32[]{:S(2)}, u32[]{:S(2)}) collective-permute-start(bf16[32,32,128]{2,1,0:T(8,128)(2,1)S(1)} %slice.8), channel_id=1, source_target_pairs={{0,48},{16,0},{32,16},{48,32},{1,49},{17,1},{33,17},{49,33},{2,50}... | collective-permute-start | bytes 786440 | tf_op jit(solution)/shard_map/ppermute | solution.py:300
  101.2 0.0 collective-permute-done.1
  101.3 0.7 slice.9
  102.0 2.0 %collective-permute-start.4 = (bf16[32,32,128]{2,1,0:T(8,128)(2,1)}, bf16[32,32,128]{2,1,0:T(8,128)(2,1)S(1)}, u32[]{:S(2)}, u32[]{:S(2)}) collective-permute-start(bf16[32,32,128]{2,1,0:T(8,128)(2,1)} %slice.9), channel_id=1, source_target_pairs={{0,16},{16,32},{32,48},{48,0},{1,17},{17,33},{33,49},{49,1},{2,18}... | collective-permute-start | bytes 786440 | tf_op jit(solution)/shard_map/ppermute | solution.py:300
  104.0 1.5 constant_dynamic-slice_fusion
  105.5 4.5 %collective-permute-start = (bf16[16,2048]{1,0:T(8,128)(2,1)}, bf16[16,2048]{1,0:T(8,128)(2,1)S(1)}, u32[]{:S(2)}, u32[]{:S(2)}) collective-permute-start(bf16[16,2048]{1,0:T(8,128)(2,1)} %get-tuple-element.13), channel_id=1, source_target_pairs={{0,1},{1,0},{2,3},{3,2},{4,5},{5,4},{6,7},{7,6},{8,9},{9,8},{10,11... | collective-permute-start | bytes 196616 | tf_op jit(solution)/shard_map/ppermute | solution.py:305
  110.1 0.1 stack.46.place
  110.1 1.0 collective-permute-done._
  111.1 0.0 collective-permute-done.3
  111.1 0.0 collective-permute-done.4
  111.1 0.0 all-to-all-done.2
  111.1 0.0 copy-start
  111.2 0.0 copy-start.1
  111.2 2.5 %gram.1 = (f32[288,1024]{1,0:T(8,128)S(1)}, f32[288,1024]{1,0:T(8,128)S(1)}) custom-call(s32[7]{0:T(128)S(1)} %stack.46.place, bf16[16,8,16,128]{3,2,1,0:T(8,128)(2,1)S(1)} %bitcast.22, bf16[16,8,16,128]{3,2,1,0:T(8,128)(2,1)S(1)} %bitcast.24, bf16[16,8,16,128]{3,2,1,0:T(8,128)(2,1)S(1)} %bitcast.23, bf16[8,8,16,128]{3,2,1,0:T(8,128)(2,1)S(1)} %bitcast.26, ...), custom_call_target="tpu_custom_call" | custom-call | tf_op jit(solution)/shard_map/gram/pallas_call | solution.py:189
  113.6 5.1 %collective-permute-start.5 = (f32[288,1024]{1,0:T(8,128)S(1)}, f32[288,1024]{1,0:T(8,128)S(1)}, u32[]{:S(2)}, u32[]{:S(2)}) collective-permute-start(f32[288,1024]{1,0:T(8,128)S(1)} %get-tuple-element.11), channel_id=1, source_target_pairs={{0,1},{1,0},{2,3},{3,2},{4,5},{5,4},{6,7},{7,6},{8,9},{9,8},{10,11... | collective-permute-start | bytes 3538952 | tf_op jit(solution)/shard_map/ppermute | solution.py:309
  118.8 2.5 %collective-permute-done.5.got = f32[288,1024]{1,0:T(8,128)S(1)} collective-permute-done((f32[288,1024]{1,0:T(8,128)S(1)}, f32[288,1024]{1,0:T(8,128)S(1)}, u32[]{:S(2)}, u32[]{:S(2)}) %collective-permute-start.5) | collective-permute-done | bytes 1179680 | tf_op jit(solution)/shard_map/ppermute | solution.py:309
  121.2 0.0 copy-done
  121.2 0.0 copy-done.1
  121.2 1.6 %energies.1 = f32[32,1,128]{2,1,0:T(1,128)} custom-call(s32[7]{0:T(128)S(1)} %stack.46.place, f32[8]{0:T(128)S(1)} %copy-done.1, f32[288,1024]{1,0:T(8,128)S(1)} %get-tuple-element.10.keep, f32[288,1024]{1,0:T(8,128)S(1)} %collective-permute-done.5.got, f32[16,128]{1,0:T(8,128)S(1)} %bitcast.28), custom_call_target="tpu_custom_call" | custom-call | tf_op jit(solution)/shard_map/energies/pallas_call | solution.py:246
  122.8 7.6 %all-to-all-start.3 = ((f32[32,1,128]{2,1,0:T(1,128)}), f32[32,1,128]{2,1,0:T(1,128)S(1)}, u32[]{:S(2)}, u32[]{:S(2)}) async-start(f32[32,1,128]{2,1,0:T(1,128)} %energies.1), calls=%async_computation.3 | async-start | bytes 32768 | tf_op jit(solution)/shard_map/all_to_all | solution.py:312
  130.5 8.5 %all-to-all-done.3.got = f32[32,1,128]{2,1,0:T(1,128)S(1)} async-done(((f32[32,1,128]{2,1,0:T(1,128)}), f32[32,1,128]{2,1,0:T(1,128)S(1)}, u32[]{:S(2)}, u32[]{:S(2)}) %all-to-all-start.3) | async-done | bytes 16416 | tf_op jit(solution)/shard_map/all_to_all | solution.py:312
  139.0 0.6 again.1
  139.6 8.8 %all-to-all-start.4 = ((f32[16,1,128]{2,1,0:T(1,128)}), f32[16,1,128]{2,1,0:T(1,128)S(1)}, u32[]{:S(2)}, u32[]{:S(2)}) async-start(f32[16,1,128]{2,1,0:T(1,128)} %again.1), calls=%async_computation.4 | async-start | bytes 16384 | tf_op jit(solution)/shard_map/all_to_all | solution.py:314
  148.4 0.7 maximum_select_fusion
  149.1 6.3 %all-to-all-done.4.got = f32[16,1,128]{2,1,0:T(1,128)S(1)} async-done(((f32[16,1,128]{2,1,0:T(1,128)}), f32[16,1,128]{2,1,0:T(1,128)S(1)}, u32[]{:S(2)}, u32[]{:S(2)}) %all-to-all-start.4) | async-done | bytes 8224 | tf_op jit(solution)/shard_map/all_to_all | solution.py:314
  155.5 0.7 last.1
  (1 shorter events, 0.0 us)
Async XLA Ops:
  62.9 48.3 %all-to-all-start.2 = ((bf16[256,16,128]{2,1,0:T(8,128)(2,1)}), bf16[256,16,128]{2,1,0:T(8,128)(2,1)S(1)}, u32[]{:S(2)}, u32[]{:S(2)}) async-start(bf16[256,16,128]{2,1,0:T(8,128)(2,1)} %get-tuple-element.9), calls=%async_computation.2 | async-start | bytes 2097152 | tf_op jit(solution)/shard_map/all_to_all | solution.py:301
  74.5 23.5 %collective-permute-start.2 = (bf16[64,32,128]{2,1,0:T(8,128)(2,1)S(1)}, bf16[64,32,128]{2,1,0:T(8,128)(2,1)S(1)}, u32[]{:S(2)}, u32[]{:S(2)}) collective-permute-start(bf16[64,32,128]{2,1,0:T(8,128)(2,1)S(1)} %all_to_all.26), channel_id=1, source_target_pairs={{0,48},{16,0},{32,16},{48,32},{1,49},{17,1},{33,17},{49,33},{2,50}... | collective-permute-start | bytes 1572872 | tf_op jit(solution)/shard_map/ppermute | solution.py:299
  77.3 23.9 %collective-permute-start.1 = (bf16[64,32,128]{2,1,0:T(8,128)(2,1)S(1)}, bf16[64,32,128]{2,1,0:T(8,128)(2,1)S(1)}, u32[]{:S(2)}, u32[]{:S(2)}) collective-permute-start(bf16[64,32,128]{2,1,0:T(8,128)(2,1)S(1)} %all_to_all.26), channel_id=1, source_target_pairs={{0,16},{16,32},{32,48},{48,0},{1,17},{17,33},{33,49},{49,1},{2,18}... | collective-permute-start | bytes 1572872 | tf_op jit(solution)/shard_map/ppermute | solution.py:299
  98.0 13.2 %collective-permute-start.3 = (bf16[32,32,128]{2,1,0:T(8,128)(2,1)S(1)}, bf16[32,32,128]{2,1,0:T(8,128)(2,1)S(1)}, u32[]{:S(2)}, u32[]{:S(2)}) collective-permute-start(bf16[32,32,128]{2,1,0:T(8,128)(2,1)S(1)} %slice.8), channel_id=1, source_target_pairs={{0,48},{16,0},{32,16},{48,32},{1,49},{17,1},{33,17},{49,33},{2,50}... | collective-permute-start | bytes 786440 | tf_op jit(solution)/shard_map/ppermute | solution.py:300
  102.0 9.1 %collective-permute-start.4 = (bf16[32,32,128]{2,1,0:T(8,128)(2,1)}, bf16[32,32,128]{2,1,0:T(8,128)(2,1)S(1)}, u32[]{:S(2)}, u32[]{:S(2)}) collective-permute-start(bf16[32,32,128]{2,1,0:T(8,128)(2,1)} %slice.9), channel_id=1, source_target_pairs={{0,16},{16,32},{32,48},{48,0},{1,17},{17,33},{33,49},{49,1},{2,18}... | collective-permute-start | bytes 786440 | tf_op jit(solution)/shard_map/ppermute | solution.py:300
  105.5 5.6 %collective-permute-start = (bf16[16,2048]{1,0:T(8,128)(2,1)}, bf16[16,2048]{1,0:T(8,128)(2,1)S(1)}, u32[]{:S(2)}, u32[]{:S(2)}) collective-permute-start(bf16[16,2048]{1,0:T(8,128)(2,1)} %get-tuple-element.13), channel_id=1, source_target_pairs={{0,1},{1,0},{2,3},{3,2},{4,5},{5,4},{6,7},{7,6},{8,9},{9,8},{10,11... | collective-permute-start | bytes 196616 | tf_op jit(solution)/shard_map/ppermute | solution.py:305
  111.1 10.1 %copy-start = (f32[2048]{0:T(1024)S(1)}, f32[2048]{0:T(1024)}, u32[]{:S(2)}) copy-start(f32[2048]{0:T(1024)} %param.13) | copy-start | bytes 24580
  111.2 10.1 %copy-start.1 = (f32[8]{0:T(128)S(1)}, f32[8]{0:T(128)}, u32[]{:S(2)}) copy-start(f32[8]{0:T(128)} %eps_occ.1) | copy-start | bytes 100
  113.6 7.6 %collective-permute-start.5 = (f32[288,1024]{1,0:T(8,128)S(1)}, f32[288,1024]{1,0:T(8,128)S(1)}, u32[]{:S(2)}, u32[]{:S(2)}) collective-permute-start(f32[288,1024]{1,0:T(8,128)S(1)} %get-tuple-element.11), channel_id=1, source_target_pairs={{0,1},{1,0},{2,3},{3,2},{4,5},{5,4},{6,7},{7,6},{8,9},{9,8},{10,11... | collective-permute-start | bytes 3538952 | tf_op jit(solution)/shard_map/ppermute | solution.py:309
  122.8 16.1 %all-to-all-start.3 = ((f32[32,1,128]{2,1,0:T(1,128)}), f32[32,1,128]{2,1,0:T(1,128)S(1)}, u32[]{:S(2)}, u32[]{:S(2)}) async-start(f32[32,1,128]{2,1,0:T(1,128)} %energies.1), calls=%async_computation.3 | async-start | bytes 32768 | tf_op jit(solution)/shard_map/all_to_all | solution.py:312
  139.6 15.9 %all-to-all-start.4 = ((f32[16,1,128]{2,1,0:T(1,128)}), f32[16,1,128]{2,1,0:T(1,128)S(1)}, u32[]{:S(2)}, u32[]{:S(2)}) async-start(f32[16,1,128]{2,1,0:T(1,128)} %again.1), calls=%async_computation.4 | async-start | bytes 16384 | tf_op jit(solution)/shard_map/all_to_all | solution.py:314

commit v5 on v4

--- a/solution.py
+++ b/solution.py
@@ -92,10 +92,10 @@
 
 def transform_kernel(recv, c_vir, bmat, wide, thin, held, terms, sides, sems):
     copies = []
-    for q in range(TILES // 2):
-        columns = pl.ds(q * 256, 256)
-        copies.append(pltpu.make_async_copy(c_vir.at[:, columns], held.at[:, columns], sems.at[q]))
-        copies[q].start()
+    for m in range(SHELLS // 2):
+        part = pl.ds(m * 128, 128)
+        copies.append(pltpu.make_async_copy(c_vir.at[part], held.at[part], sems.at[m]))
+        copies[m].start()
     left = lanes((16, 128)) < SHELL
     sums = [jnp.zeros((16, 128), F32) for _ in range(SHELLS)]
     for source in range(8):
@@ -116,8 +116,9 @@
                 part = rounded(value)
                 terms[term * 32 + i * 16 : term * 32 + i * 16 + 16, m * 128 : m * 128 + 128] = part.astype(BF16)
                 value = value - part
+    for copy in copies:
+        copy.wait()
     for q in range(TILES // 2):
-        copies[q].wait()
         got = jnp.dot(terms[...], held[:, q * 256 : q * 256 + 256], preferred_element_type=F32)
         full = (got[64:96] + got[32:64]) + got[0:32]
         bmat[:, q * 256 : q * 256 + 256] = full.astype(BF16)
@@ -149,14 +150,14 @@
             pltpu.VMEM(c_vir.shape, BF16),
             pltpu.VMEM((96, c_vir.shape[0]), BF16),
             pltpu.VMEM((32, 16, 128), BF16),
-            pltpu.SemaphoreType.DMA((TILES // 2,)),
+            pltpu.SemaphoreType.DMA((SHELLS // 2,)),
         ],
         compiler_params=grant(61),
         name="transform",
     )(recv, c_vir)
 
 
-def gram_kernel(place, here, below, above, low, high, sides, _, keep, give, wide, thin, all_t, all_s):
+def gram_kernel(place, here, below, above, low, high, sides, two, keep, give, wide, thin, all_t, all_s):
     core, side, own, x = place[4], place[3], place[5], place[6]
     first = 0
     for away, tiles in ((0, here), (3, below), (1, above), (2, low), (2, high)):
@@ -181,15 +182,17 @@
         for q in range(4):
             at = pl.multiple_of(which * 256, 256)
             target[256:288, q * 256 : q * 256 + 256] = all_s[q * 32 : q * 32 + 32, pl.ds(at, 256)]
-
-
-def gram(place, here, below, above, low, high, sides, after):
-    shape = jax.ShapeDtypeStruct((288, 1024), F32)
+    at = pl.multiple_of((1 - core) * 16, 16)
+    for q in range(2):
+        give[288 + q * 16 : 304 + q * 16, :] = two[pl.ds(at, 16), q * 1024 : q * 1024 + 1024].astype(F32)
+
+
+def gram(place, here, below, above, low, high, sides, two):
     tiles = (block.reshape(-1, 8, 16, 128) for block in (here, below, above, low, high))
     return pl.pallas_call(
         gram_kernel,
-        out_shape=(shape, shape),
-        in_specs=[SMEM] + [VMEM] * 6 + [HBM],
+        out_shape=(jax.ShapeDtypeStruct((288, 1024), F32), jax.ShapeDtypeStruct((320, 1024), F32)),
+        in_specs=[SMEM] + [VMEM] * 7,
         out_specs=(VMEM, VMEM),
         scratch_shapes=[
             pltpu.VMEM((1024, 1024), BF16),
@@ -199,10 +202,10 @@
         ],
         compiler_params=grant(16),
         name="gram",
-    )(place, *tiles, sides.reshape(8, 4, 2, 4, 16, 128), after)
-
-
-def energy_kernel(scale, place, eps_occ, keep, got, eps_vir, out, parts):
+    )(place, *tiles, sides.reshape(8, 4, 2, 4, 16, 128), two)
+
+
+def energy_kernel(scale, place, eps_occ, keep, got, eps_vir, mine, out, bmat, parts):
     tile, other, step, side, core, own = (place[n] for n in range(6))
     row_a = eps_vir[pl.ds(tile, 1), :]
     row_b = eps_vir[pl.ds(other, 1), :]
@@ -240,18 +243,23 @@
     column = jnp.sum(parts[...], axis=1, keepdims=True) * scale
     row = jnp.sum(jnp.where(lanes((64, 128)) == rows((64, 128)), column, 0.0), axis=0, keepdims=True)
     out[...] = jnp.broadcast_to(row[None], out.shape)
-
-
-def energies(scale, place, eps_occ, keep, got, eps_vir):
+    here = pl.ds(pl.multiple_of(core * 16, 16), 16)
+    bmat[here, :] = mine[here, :]
+    there = pl.ds(pl.multiple_of((1 - core) * 16, 16), 16)
+    for q in range(2):
+        bmat[there, q * 1024 : q * 1024 + 1024] = got[288 + q * 16 : 304 + q * 16, :].astype(BF16)
+
+
+def energies(scale, place, eps_occ, keep, got, eps_vir, two):
     return pl.pallas_call(
         functools.partial(energy_kernel, scale),
-        out_shape=jax.ShapeDtypeStruct((32, 1, 128), F32),
-        in_specs=[SMEM, SMEM, VMEM, VMEM, VMEM],
-        out_specs=VMEM,
+        out_shape=(jax.ShapeDtypeStruct((256, 1, 128), F32), jax.ShapeDtypeStruct(two.shape, BF16)),
+        in_specs=[SMEM, SMEM, VMEM, VMEM, VMEM, VMEM],
+        out_specs=(VMEM, VMEM),
         scratch_shapes=[pltpu.VMEM((64, 128), F32)],
-        compiler_params=grant(6),
+        compiler_params=grant(8),
         name="energies",
-    )(place, eps_occ, keep, got, eps_vir.reshape(-1, 128))
+    )(place, eps_occ, keep, got, eps_vir.reshape(-1, 128), two)
 
 
 def position():
@@ -259,10 +267,6 @@
     tile, kind = z * 2 + yl, x * 4 + yh
     step, side = lax.shift_right_logical(kind, 1) + 1, kind & 1
     return jnp.stack([tile, (tile + step) & (TILES - 1), step, side, core, lax.shift_right_logical(kind, 1), x])
-
-
-def again_kernel(got, out):
-    out[...] = jnp.broadcast_to(jnp.sum(got[...], axis=0)[None], out.shape)
 
 
 def last_kernel(got, out):
@@ -288,8 +292,6 @@
 def body(c_occ, c_vir, ints, blocks, screen, eps_occ, eps_vir):
     vir, occ = c_vir.shape[1], c_occ.shape[1]
     place = position()
-    core = lax.axis_index("core")
-    swap = [(0, 1), (1, 0)]
     sent = half_transform(c_occ, ints, blocks, screen)
     recv = lax.all_to_all(sent, GRP, 0, 0, tiled=True)
     two, wide, thin = transform(recv, c_vir)
@@ -300,19 +302,12 @@
     low, high = lax.ppermute(above[:32], "x", down), lax.ppermute(below[32:], "x", up)
     sides = lax.all_to_all(thin, CHIPS, 0, 0, tiled=True)
 
-    two = two.reshape(2, 16, vir)
-    mine = lax.dynamic_index_in_dim(two, core, 0, keepdims=False)
-    others = lax.ppermute(lax.dynamic_index_in_dim(two, 1 - core, 0, keepdims=False), "core", swap)
-    bmat = jnp.where(core == 0, jnp.stack([mine, others]), jnp.stack([others, mine]))
-
-    keep, give = gram(place, here, below, above, low, high, sides, others)
-    got = lax.ppermute(give, "core", swap)
+    keep, give = gram(place, here, below, above, low, high, sides, two)
+    got = lax.ppermute(give, "core", [(0, 1), (1, 0)])
     scale = 1.0 / (float(vir) * float(vir) * 2048.0)
-    energy = energies(scale, place, eps_occ, keep, got, eps_vir)
-    energy = lax.all_to_all(energy, ("z", "x"), 0, 0, tiled=True)
-    energy = small(again_kernel, (16, 1, 128), "again")(energy)
-    energy = lax.all_to_all(energy, ("yh", "yl", "core"), 0, 0, tiled=True)
-    energy = small(last_kernel, (occ, occ), "last")(energy)
+    energy, bmat = energies(scale, place, eps_occ, keep, got, eps_vir, two)
+    energy = lax.all_to_all(energy, CHIPS, 0, 0, tiled=True)
+    energy = lax.psum(small(last_kernel, (occ, occ), "last")(energy), "core")
     return bmat.reshape(1, 32, vir), energy
 
 

time: 157 us -> 156 us (level)
  blocking collectives: 51.5 us -> 84.5 us
  starting transfers between devices: 48.2 us -> 28 us
  waiting for transfers between devices: 36.5 us -> 27.2 us
  Pallas kernels: 16.1 us -> 14.1 us
    all_to_all x0 -> x1, blocking collectives: none -> 28.3 us  [body(): energy = lax.all_to_all(energy, CHIPS, 0, 0, tiled=True)]
    all_to_all x2 -> x0, starting transfers between devices: 16.5 us -> none  [the longest x1 8.85 us: body(): energy = lax.all_to_all(energy, ('yh', 'yl', 'core'), 0, 0, tiled=True)]
    all_to_all x2 -> x0, waiting for transfers between devices: 14.8 us -> none  [the longest x1 8.5 us: body(): energy = lax.all_to_all(energy, ('z', 'x'), 0, 0, tiled=True)]
    psum x0 -> x1, blocking collectives: none -> 4.72 us  [body(): energy = lax.psum(small(last_kernel, (occ, occ), 'last')(energy), 'core')]
    ppermute x1, waiting for transfers between devices: 0.01 us -> 4.18 us  [body(): lax.ppermute(below[32:], 'x', up)]
    ppermute x2 -> x1, starting transfers between devices: 9.63 us -> 5.77 us  [body(): got = lax.ppermute(give, 'core', [(0, 1), (1, 0)])]
    ppermute x1, waiting for transfers between devices: 0.01 us -> 2.22 us  [body(): lax.ppermute(above[:32], 'x', down)]
    pallas_call x4 -> x3, Pallas kernels: 5.38 us -> 4.33 us  [the longest x1 2.46 us: gram(): pl.pallas_call(gram_kernel, out_shape=(jax.ShapeDtypeStruct((288, 1024),...]
  transfers between devices with their start and end apart: 9 -> 6, of which waited for: 5 -> 4; matrix products, arithmetic and copies ran while one was open for 2% -> 1% of each run, Pallas kernels for 0% -> 0%
where the time goes in v5:
time: 156 us; the launch traced here: 155 us
  blocking collectives  84.5 us (54%)
  starting transfers between devices  28 us (18%)
  waiting for transfers between devices  27.2 us (17%)
  Pallas kernels  14.1 us (9%)
    all_to_all x1, blocking collectives, body(): here = lax.all_to_all(wide, ('z', 'yl', 'yh'), 0, 0, tiled=True)  29.3 us
    all_to_all x1, blocking collectives, body(): energy = lax.all_to_all(energy, CHIPS, 0, 0, tiled=True)  28.3 us
    all_to_all x1, blocking collectives, body(): recv = lax.all_to_all(sent, GRP, 0, 0, tiled=True)  22.2 us
    ppermute x2, waiting for transfers between devices, body(): below, above = (lax.ppermute(here, 'x', up), lax.ppermute(here, 'x', down))  18.2 us
    all_to_all x1, starting transfers between devices, body(): sides = lax.all_to_all(thin, CHIPS, 0, 0, tiled=True)  11.7 us
    ppermute x1, starting transfers between devices, body(): got = lax.ppermute(give, 'core', [(0, 1), (1, 0)])  5.77 us
    ppermute x2, starting transfers between devices, body(): below, above = (lax.ppermute(here, 'x', up), lax.ppermute(here, 'x', down))  5.28 us
    pallas_call x1, Pallas kernels, half_transform(): pl.pallas_call(half_kernel, out_shape=jax.ShapeDtypeStruct((8, 72, 128),...  4.95 us
  transfers between devices with their start and end apart: 6, of which 4 were waited for; matrix products, arithmetic and copies ran while one was open for 1% of the time, Pallas kernels for 0%

profile of v5, /device:TPU:1, one launch (start us, length us, event | category | flops | bytes accessed | tf_op | source)
XLA Modules:
  0.0 155.4 jit_solution(8625696273530781665)
XLA Ops:
  0.6 5.0 %half.1 = f32[8,72,128]{2,1,0:T(8,128)} custom-call(s32[2,4]{1,0:T(2,128)} %bitcast.25, s32[4]{0:T(128)} %screen.1, bf16[8,768]{1,0:T(8,128)(2,1)} %bitcast.24, bf16[4,32,4096]{2,1,0:T(8,128)(2,1)} %ints.1), custom_call_target="tpu_custom_call" | custom-call | tf_op jit(solution)/shard_map/half/pallas_call | solution.py:73
  5.6 22.2 %all_to_all.20.recv = f32[8,72,128]{2,1,0:T(8,128)} all-to-all(f32[8,72,128]{2,1,0:T(8,128)} %half.1), channel_id=1, replica_groups=mesh['z'=8,'x'=4,'yl'=2,'yh'=4,'core'=2] {'yh','core'}, dimensions={0} | all-to-all | bytes 589824 | tf_op jit(solution)/shard_map/all_to_all | solution.py:296
  27.8 4.8 %transform.1 = (bf16[32,2048]{1,0:T(8,128)(2,1)}, bf16[64,32,128]{2,1,0:T(8,128)(2,1)}, bf16[256,16,128]{2,1,0:T(8,128)(2,1)}) custom-call(f32[8,72,128]{2,1,0:T(8,128)} %all_to_all.20.recv, bf16[768,2048]{1,0:T(8,128)(2,1)} %c_vir.1), custom_call_target="tpu_custom_call" | custom-call | tf_op jit(solution)/shard_map/transform/pallas_call | solution.py:140
  32.6 29.3 %all_to_all.21 = bf16[64,32,128]{2,1,0:T(8,128)(2,1)S(1)} all-to-all(bf16[64,32,128]{2,1,0:T(8,128)(2,1)} %get-tuple-element.9), channel_id=1, replica_groups=mesh['z'=8,'x'=4,'yl'=2,'yh'=4,'core'=2] {'z','yl','yh'}, dimensions={0} | all-to-all | bytes 1048576 | tf_op jit(solution)/shard_map/all_to_all | solution.py:298
  61.9 0.0 copy-start
  61.9 11.7 %all-to-all-start.2 = ((bf16[256,16,128]{2,1,0:T(8,128)(2,1)}), bf16[256,16,128]{2,1,0:T(8,128)(2,1)S(1)}, u32[]{:S(2)}, u32[]{:S(2)}) async-start(bf16[256,16,128]{2,1,0:T(8,128)(2,1)} %get-tuple-element.10), calls=%async_computation.2 | async-start | bytes 2097152 | tf_op jit(solution)/shard_map/all_to_all | solution.py:303
  73.6 2.9 %collective-permute-start.1 = (bf16[64,32,128]{2,1,0:T(8,128)(2,1)S(1)}, bf16[64,32,128]{2,1,0:T(8,128)(2,1)S(1)}, u32[]{:S(2)}, u32[]{:S(2)}) collective-permute-start(bf16[64,32,128]{2,1,0:T(8,128)(2,1)S(1)} %all_to_all.21), channel_id=1, source_target_pairs={{0,48},{16,0},{32,16},{48,32},{1,49},{17,1},{33,17},{49,33},{2,50}... | collective-permute-start | bytes 1572872 | tf_op jit(solution)/shard_map/ppermute | solution.py:301
  76.5 2.4 %collective-permute-start = (bf16[64,32,128]{2,1,0:T(8,128)(2,1)S(1)}, bf16[64,32,128]{2,1,0:T(8,128)(2,1)S(1)}, u32[]{:S(2)}, u32[]{:S(2)}) collective-permute-start(bf16[64,32,128]{2,1,0:T(8,128)(2,1)S(1)} %all_to_all.21), channel_id=1, source_target_pairs={{0,16},{16,32},{32,48},{48,0},{1,17},{17,33},{33,49},{49,1},{2,18}... | collective-permute-start | bytes 1572872 | tf_op jit(solution)/shard_map/ppermute | solution.py:301
  78.9 18.2 %collective-permute-done.1 = bf16[64,32,128]{2,1,0:T(8,128)(2,1)S(1)} collective-permute-done((bf16[64,32,128]{2,1,0:T(8,128)(2,1)S(1)}, bf16[64,32,128]{2,1,0:T(8,128)(2,1)S(1)}, u32[]{:S(2)}, u32[]{:S(2)}) %collective-permute-start.1) | collective-permute-done | bytes 524320 | tf_op jit(solution)/shard_map/ppermute | solution.py:301
  97.1 3.2 %collective-permute-start.2 = (bf16[32,32,128]{2,1,0:T(8,128)(2,1)S(1)}, bf16[32,32,128]{2,1,0:T(8,128)(2,1)S(1)}, u32[]{:S(2)}, u32[]{:S(2)}) collective-permute-start(bf16[32,32,128]{2,1,0:T(8,128)(2,1)S(1)} %slice.8), channel_id=1, source_target_pairs={{0,48},{16,0},{32,16},{48,32},{1,49},{17,1},{33,17},{49,33},{2,50}... | collective-permute-start | bytes 786440 | tf_op jit(solution)/shard_map/ppermute | solution.py:302
  100.4 0.0 collective-permute-done
  100.4 0.7 slice.9
  101.1 2.0 %collective-permute-start.3 = (bf16[32,32,128]{2,1,0:T(8,128)(2,1)}, bf16[32,32,128]{2,1,0:T(8,128)(2,1)S(1)}, u32[]{:S(2)}, u32[]{:S(2)}) collective-permute-start(bf16[32,32,128]{2,1,0:T(8,128)(2,1)} %slice.9), channel_id=1, source_target_pairs={{0,16},{16,32},{32,48},{48,0},{1,17},{17,33},{33,49},{49,1},{2,18}... | collective-permute-start | bytes 786440 | tf_op jit(solution)/shard_map/ppermute | solution.py:302
  103.2 0.1 stack.31.place
  103.2 2.2 %collective-permute-done.2 = bf16[32,32,128]{2,1,0:T(8,128)(2,1)S(1)} collective-permute-done((bf16[32,32,128]{2,1,0:T(8,128)(2,1)S(1)}, bf16[32,32,128]{2,1,0:T(8,128)(2,1)S(1)}, u32[]{:S(2)}, u32[]{:S(2)}) %collective-permute-start.2) | collective-permute-done | bytes 262176 | tf_op jit(solution)/shard_map/ppermute | solution.py:302
  105.5 4.2 %collective-permute-done.3 = bf16[32,32,128]{2,1,0:T(8,128)(2,1)S(1)} collective-permute-done((bf16[32,32,128]{2,1,0:T(8,128)(2,1)}, bf16[32,32,128]{2,1,0:T(8,128)(2,1)S(1)}, u32[]{:S(2)}, u32[]{:S(2)}) %collective-permute-start.3) | collective-permute-done | bytes 262176 | tf_op jit(solution)/shard_map/ppermute | solution.py:302
  109.6 0.0 all-to-all-done.2
  109.6 0.0 copy-done
  109.6 0.0 copy-start.1
  109.7 0.0 copy-start.2
  109.7 2.5 %gram.1 = (f32[288,1024]{1,0:T(8,128)S(1)}, f32[320,1024]{1,0:T(8,128)S(1)}) custom-call(s32[7]{0:T(128)S(1)} %stack.31.place, bf16[16,8,16,128]{3,2,1,0:T(8,128)(2,1)S(1)} %bitcast.18, bf16[16,8,16,128]{3,2,1,0:T(8,128)(2,1)S(1)} %bitcast.20, bf16[16,8,16,128]{3,2,1,0:T(8,128)(2,1)S(1)} %bitcast.19, bf16[8,8,16,128]{3,2,1,0:T(8,128)(2,1)S(1)} %bitcast.21, ...), custom_call_target="tpu_custom_call" | custom-call | tf_op jit(solution)/shard_map/gram/pallas_call | solution.py:192
  112.1 5.8 %collective-permute-start.4 = (f32[320,1024]{1,0:T(8,128)S(1)}, f32[320,1024]{1,0:T(8,128)S(1)}, u32[]{:S(2)}, u32[]{:S(2)}) collective-permute-start(f32[320,1024]{1,0:T(8,128)S(1)} %get-tuple-element.13), channel_id=1, source_target_pairs={{0,1},{1,0},{2,3},{3,2},{4,5},{5,4},{6,7},{7,6},{8,9},{9,8},{10,11... | collective-permute-start | bytes 3932168 | tf_op jit(solution)/shard_map/ppermute | solution.py:306
  117.9 2.6 %collective-permute-done.4.got = f32[320,1024]{1,0:T(8,128)S(1)} collective-permute-done((f32[320,1024]{1,0:T(8,128)S(1)}, f32[320,1024]{1,0:T(8,128)S(1)}, u32[]{:S(2)}, u32[]{:S(2)}) %collective-permute-start.4) | collective-permute-done | bytes 1310752 | tf_op jit(solution)/shard_map/ppermute | solution.py:306
  120.6 0.0 copy-done.1
  120.6 0.0 copy-done.2
  120.6 1.5 energies.1
  122.1 28.3 %all_to_all.22.got = f32[256,1,128]{2,1,0:T(1,128)S(1)} all-to-all(f32[256,1,128]{2,1,0:T(1,128)S(1)} %get-tuple-element.15), channel_id=1, replica_groups=mesh['z'=8,'x'=4,'yl'=2,'yh'=4,'core'=2] {'z','x','yl','yh'}, dimensions={0} | all-to-all | bytes 262144 | tf_op jit(solution)/shard_map/all_to_all | solution.py:309
  150.4 0.3 last.1
  150.7 4.7 %psum.7 = f32[8,8]{1,0:T(8,128)} all-reduce(f32[8,8]{1,0:T(8,128)S(1)} %last.1), channel_id=1, replica_groups=mesh['z'=8,'x'=4,'yl'=2,'yh'=4,'core'=2] {'core'}, use_global_device_ids=true, to_apply=%region_0.0 | all-reduce | flops 64 | bytes 512 | tf_op jit(solution)/shard_map/psum | solution.py:310
  (1 shorter events, 0.0 us)
Async XLA Ops:
  61.9 47.8 %copy-start = (bf16[32,2048]{1,0:T(8,128)(2,1)S(1)}, bf16[32,2048]{1,0:T(8,128)(2,1)}, u32[]{:S(2)}) copy-start(bf16[32,2048]{1,0:T(8,128)(2,1)} %get-tuple-element.11.two.mine) | copy-start | bytes 393220
  61.9 47.7 %all-to-all-start.2 = ((bf16[256,16,128]{2,1,0:T(8,128)(2,1)}), bf16[256,16,128]{2,1,0:T(8,128)(2,1)S(1)}, u32[]{:S(2)}, u32[]{:S(2)}) async-start(bf16[256,16,128]{2,1,0:T(8,128)(2,1)} %get-tuple-element.10), calls=%async_computation.2 | async-start | bytes 2097152 | tf_op jit(solution)/shard_map/all_to_all | solution.py:303
  73.6 23.5 %collective-permute-start.1 = (bf16[64,32,128]{2,1,0:T(8,128)(2,1)S(1)}, bf16[64,32,128]{2,1,0:T(8,128)(2,1)S(1)}, u32[]{:S(2)}, u32[]{:S(2)}) collective-permute-start(bf16[64,32,128]{2,1,0:T(8,128)(2,1)S(1)} %all_to_all.21), channel_id=1, source_target_pairs={{0,48},{16,0},{32,16},{48,32},{1,49},{17,1},{33,17},{49,33},{2,50}... | collective-permute-start | bytes 1572872 | tf_op jit(solution)/shard_map/ppermute | solution.py:301
  76.5 23.9 %collective-permute-start = (bf16[64,32,128]{2,1,0:T(8,128)(2,1)S(1)}, bf16[64,32,128]{2,1,0:T(8,128)(2,1)S(1)}, u32[]{:S(2)}, u32[]{:S(2)}) collective-permute-start(bf16[64,32,128]{2,1,0:T(8,128)(2,1)S(1)} %all_to_all.21), channel_id=1, source_target_pairs={{0,16},{16,32},{32,48},{48,0},{1,17},{17,33},{33,49},{49,1},{2,18}... | collective-permute-start | bytes 1572872 | tf_op jit(solution)/shard_map/ppermute | solution.py:301
  97.1 8.3 %collective-permute-start.2 = (bf16[32,32,128]{2,1,0:T(8,128)(2,1)S(1)}, bf16[32,32,128]{2,1,0:T(8,128)(2,1)S(1)}, u32[]{:S(2)}, u32[]{:S(2)}) collective-permute-start(bf16[32,32,128]{2,1,0:T(8,128)(2,1)S(1)} %slice.8), channel_id=1, source_target_pairs={{0,48},{16,0},{32,16},{48,32},{1,49},{17,1},{33,17},{49,33},{2,50}... | collective-permute-start | bytes 786440 | tf_op jit(solution)/shard_map/ppermute | solution.py:302
  101.1 8.5 %collective-permute-start.3 = (bf16[32,32,128]{2,1,0:T(8,128)(2,1)}, bf16[32,32,128]{2,1,0:T(8,128)(2,1)S(1)}, u32[]{:S(2)}, u32[]{:S(2)}) collective-permute-start(bf16[32,32,128]{2,1,0:T(8,128)(2,1)} %slice.9), channel_id=1, source_target_pairs={{0,16},{16,32},{32,48},{48,0},{1,17},{17,33},{33,49},{49,1},{2,18}... | collective-permute-start | bytes 786440 | tf_op jit(solution)/shard_map/ppermute | solution.py:302
  109.6 10.9 %copy-start.1 = (f32[2048]{0:T(1024)S(1)}, f32[2048]{0:T(1024)}, u32[]{:S(2)}) copy-start(f32[2048]{0:T(1024)} %param.13) | copy-start | bytes 24580
  109.7 10.9 %copy-start.2 = (f32[8]{0:T(128)S(1)}, f32[8]{0:T(128)}, u32[]{:S(2)}) copy-start(f32[8]{0:T(128)} %eps_occ.1) | copy-start | bytes 100
  112.1 8.4 %collective-permute-start.4 = (f32[320,1024]{1,0:T(8,128)S(1)}, f32[320,1024]{1,0:T(8,128)S(1)}, u32[]{:S(2)}, u32[]{:S(2)}) collective-permute-start(f32[320,1024]{1,0:T(8,128)S(1)} %get-tuple-element.13), channel_id=1, source_target_pairs={{0,1},{1,0},{2,3},{3,2},{4,5},{5,4},{6,7},{7,6},{8,9},{9,8},{10,11... | collective-permute-start | bytes 3932168 | tf_op jit(solution)/shard_map/ppermute | solution.py:306

commit v6 on v5

--- a/solution.py
+++ b/solution.py
@@ -10,6 +10,7 @@
 SHELL = 64
 SHELLS = 12
 TILES = 16
+CHUNKS = 3
 AXES = ("z", "x", "yl", "yh", "core")
 CHIPS = ("z", "x", "yl", "yh")
 PAIR = ("z", "x", "yl")
@@ -40,21 +41,24 @@
         pltpu.make_async_copy(ints.at[b], held.at[b], sems.at[b]).start()
     shape = (SHELL, 4096)
     spread[...] = (lanes(shape) // SHELL == rows(shape)).astype(F32).astype(BF16)
+    own = []
+    for b in range(count):
+        first = blocks[0, b]
+        at = pl.multiple_of((first // 2) * 128, 128)
+        shell = pltpu.roll(c_occ[:, pl.ds(at, 128)].astype(F32), (first % 2) * SHELL, 1)[:, :SHELL]
+        own.append(shell * screen[b].astype(F32))
+    own = jnp.concatenate(own, axis=0).astype(BF16)
+    coef[...] = jnp.dot(own, spread[...], preferred_element_type=F32).reshape(count, 8, 4096)
     left = lanes((32, 128)) < SHELL
 
     @pl.loop(0, count)
     def _(block):
-        first = blocks[0, block]
-        at = pl.multiple_of((first // 2) * 128, 128)
-        own = pltpu.roll(c_occ[:, pl.ds(at, 128)].astype(F32), (first % 2) * SHELL, 1)[:, :SHELL]
-        wide = jnp.dot(own.astype(BF16), spread[...], preferred_element_type=F32)
-        coef[...] = wide * screen[block].astype(F32)
         pltpu.make_async_copy(ints.at[block], held.at[block], sems.at[block]).wait()
 
         def step(t, sums):
             at = pl.multiple_of(t * 128, 128)
             tile = held[block, :, pl.ds(at, 128)].astype(F32)
-            weights = coef[:, pl.ds(at, 128)]
+            weights = coef[block, :, pl.ds(at, 128)]
             return tuple(sums[i] + tile * weights[i : i + 1] for i in range(8))
 
         sums = lax.fori_loop(0, 32, step, (jnp.zeros((32, 128), F32),) * 8, unroll=8)
@@ -78,10 +82,10 @@
         scratch_shapes=[
             pltpu.VMEM(ints.shape, BF16),
             pltpu.VMEM((SHELL, 4096), BF16),
-            pltpu.VMEM((8, 4096), F32),
+            pltpu.VMEM((ints.shape[0], 8, 4096), F32),
             pltpu.SemaphoreType.DMA((ints.shape[0],)),
         ],
-        compiler_params=grant(62),
+        compiler_params=grant(54),
         name="half",
     )(blocks.T, screen, c_occ.T, ints)
 
@@ -90,12 +94,24 @@
     return x.astype(BF16).astype(F32)
 
 
-def transform_kernel(recv, c_vir, bmat, wide, thin, held, terms, sides, sems):
+def finish(q, full, left, bmat, sides):
+    bmat[:, q * 256 : q * 256 + 256] = full.astype(BF16)
+    for t in range(2):
+        one, two = full[0:16, t * 128 : t * 128 + 128], full[16:32, t * 128 : t * 128 + 128]
+        tile = q * 2 + t
+        sides[tile * 2] = jnp.where(left, one, pltpu.roll(two, SHELL, 1)).astype(BF16)
+        sides[tile * 2 + 1] = jnp.where(left, pltpu.roll(one, SHELL, 1), two).astype(BF16)
+
+
+def transform_kernel(recv_at, c_vir, bmat, wide, thin, recv, held, terms, sides, total, sems):
+    arrive = pltpu.make_async_copy(recv_at, recv, sems.at[CHUNKS])
+    arrive.start()
     copies = []
-    for m in range(SHELLS // 2):
-        part = pl.ds(m * 128, 128)
+    for m in range(CHUNKS):
+        part = pl.ds(m * 256, 256)
         copies.append(pltpu.make_async_copy(c_vir.at[part], held.at[part], sems.at[m]))
         copies[m].start()
+    arrive.wait()
     left = lanes((16, 128)) < SHELL
     sums = [jnp.zeros((16, 128), F32) for _ in range(SHELLS)]
     for source in range(8):
@@ -116,17 +132,18 @@
                 part = rounded(value)
                 terms[term * 32 + i * 16 : term * 32 + i * 16 + 16, m * 128 : m * 128 + 128] = part.astype(BF16)
                 value = value - part
-    for copy in copies:
-        copy.wait()
-    for q in range(TILES // 2):
-        got = jnp.dot(terms[...], held[:, q * 256 : q * 256 + 256], preferred_element_type=F32)
-        full = (got[64:96] + got[32:64]) + got[0:32]
-        bmat[:, q * 256 : q * 256 + 256] = full.astype(BF16)
-        for t in range(2):
-            one, two = full[0:16, t * 128 : t * 128 + 128], full[16:32, t * 128 : t * 128 + 128]
-            tile = q * 2 + t
-            sides[tile * 2] = jnp.where(left, one, pltpu.roll(two, SHELL, 1)).astype(BF16)
-            sides[tile * 2 + 1] = jnp.where(left, pltpu.roll(one, SHELL, 1), two).astype(BF16)
+    for m in range(CHUNKS):
+        copies[m].wait()
+        some = terms[:, m * 256 : m * 256 + 256]
+        for q in range(TILES // 2):
+            columns = slice(q * 256, q * 256 + 256)
+            got = jnp.dot(some, held[m * 256 : m * 256 + 256, columns], preferred_element_type=F32)
+            if m < CHUNKS - 1:
+                total[:, columns] = got if m == 0 else total[:, columns] + got
+                continue
+            got = total[:, columns] + got
+            full = (got[64:96] + got[32:64]) + got[0:32]
+            finish(q, full, left, bmat, sides)
     for r in range(TILES):
         for yh in range(4):
             wide[r * 4 + yh] = bmat[:, r * 128 : r * 128 + 128]
@@ -144,17 +161,37 @@
             jax.ShapeDtypeStruct((64, 32, 128), BF16),
             jax.ShapeDtypeStruct((256, 16, 128), BF16),
         ),
-        in_specs=[VMEM, HBM],
+        in_specs=[HBM, HBM],
         out_specs=(VMEM, VMEM, VMEM),
         scratch_shapes=[
+            pltpu.VMEM(recv.shape, F32),
             pltpu.VMEM(c_vir.shape, BF16),
             pltpu.VMEM((96, c_vir.shape[0]), BF16),
             pltpu.VMEM((32, 16, 128), BF16),
-            pltpu.SemaphoreType.DMA((SHELLS // 2,)),
+            pltpu.VMEM((96, c_vir.shape[1]), F32),
+            pltpu.SemaphoreType.DMA((CHUNKS + 1,)),
         ],
-        compiler_params=grant(61),
+        compiler_params=grant(52),
         name="transform",
     )(recv, c_vir)
+
+
+def onward_kernel(below, above, low, high):
+    low[...] = above[0:32]
+    high[...] = below[32:64]
+
+
+def onward(below, above):
+    half = jax.ShapeDtypeStruct((32,) + below.shape[1:], BF16)
+    return pl.pallas_call(
+        onward_kernel,
+        out_shape=(half, half),
+        in_specs=[VMEM, VMEM],
+        out_specs=(VMEM, VMEM),
+        compiler_params=grant(4),
+        cost_estimate=pl.CostEstimate(flops=1 << 35, bytes_accessed=1 << 21, transcendentals=0),
+        name="onward",
+    )(below, above)
 
 
 def gram_kernel(place, here, below, above, low, high, sides, two, keep, give, wide, thin, all_t, all_s):
@@ -299,7 +336,8 @@
     up = [(i, (i + 1) % 4) for i in range(4)]
     down = [(i, (i + 3) % 4) for i in range(4)]
     below, above = lax.ppermute(here, "x", up), lax.ppermute(here, "x", down)
-    low, high = lax.ppermute(above[:32], "x", down), lax.ppermute(below[32:], "x", up)
+    low, high = onward(below, above)
+    low, high = lax.ppermute(low, "x", down), lax.ppermute(high, "x", up)
     sides = lax.all_to_all(thin, CHIPS, 0, 0, tiled=True)
 
     keep, give = gram(place, here, below, above, low, high, sides, two)

time: 156 us -> 144 us (0.923)
  blocking collectives: 84.5 us -> 78.8 us
  waiting for transfers between devices: 27.2 us -> 22.8 us
    ppermute x2, waiting for transfers between devices: 18.2 us -> 0.01 us  [body(): below, above = (lax.ppermute(here, 'x', up), lax.ppermute(here, 'x', down))]
    all_to_all x1, waiting for transfers between devices: 0.01 us -> 9.75 us  [body(): sides = lax.all_to_all(thin, CHIPS, 0, 0, tiled=True)]
    all_to_all x1, blocking collectives: 28.3 us -> 22.9 us  [body(): energy = lax.all_to_all(energy, CHIPS, 0, 0, tiled=True)]
    ppermute x2, waiting for transfers between devices: 6.4 us -> 10.4 us  [body(): low, high = (lax.ppermute(low, 'x', down), lax.ppermute(high, 'x', up))]
  transfers between devices with their start and end apart: 6 -> 6, of which waited for: 4 -> 4; matrix products, arithmetic and copies ran while one was open for 1% -> 0% of each run, Pallas kernels for 0% -> 1%
where the time goes in v6:
time: 144 us
  blocking collectives  78.8 us (55%)
  starting transfers between devices  28.6 us (20%)
  waiting for transfers between devices  22.8 us (16%)
  Pallas kernels  12.7 us (9%)
    all_to_all x1, blocking collectives, body(): here = lax.all_to_all(wide, ('z', 'yl', 'yh'), 0, 0, tiled=True)  29.7 us
    all_to_all x1, blocking collectives, body(): energy = lax.all_to_all(energy, CHIPS, 0, 0, tiled=True)  22.9 us
    all_to_all x1, blocking collectives, body(): recv = lax.all_to_all(sent, GRP, 0, 0, tiled=True)  21.5 us
    all_to_all x1, starting transfers between devices, body(): sides = lax.all_to_all(thin, CHIPS, 0, 0, tiled=True)  11.5 us
    ppermute x2, waiting for transfers between devices, body(): low, high = (lax.ppermute(low, 'x', down), lax.ppermute(high, 'x', up))  10.4 us
    all_to_all x1, waiting for transfers between devices, body(): sides = lax.all_to_all(thin, CHIPS, 0, 0, tiled=True)  9.75 us
    ppermute x2, starting transfers between devices, body(): below, above = (lax.ppermute(here, 'x', up), lax.ppermute(here, 'x', down))  6.29 us
    ppermute x1, starting transfers between devices, body(): got = lax.ppermute(give, 'core', [(0, 1), (1, 0)])  5.57 us
  transfers between devices with their start and end apart: 6, of which 4 were waited for; matrix products, arithmetic and copies ran while one was open for 0% of the time, Pallas kernels for 1%

profile of v6, /device:TPU:1, one launch (start us, length us, event | category | flops | bytes accessed | tf_op | source)
XLA Modules:
  0.0 143.8 jit_solution(16882570162754016794)
XLA Ops:
  0.6 4.2 %half.1 = f32[8,72,128]{2,1,0:T(8,128)} custom-call(s32[2,4]{1,0:T(2,128)} %bitcast.25, s32[4]{0:T(128)} %screen.1, bf16[8,768]{1,0:T(8,128)(2,1)} %bitcast.24, bf16[4,32,4096]{2,1,0:T(8,128)(2,1)} %ints.1), custom_call_target="tpu_custom_call" | custom-call | tf_op jit(solution)/shard_map/half/pallas_call | solution.py:77
  4.9 21.5 %all_to_all.20.recv_at = f32[8,72,128]{2,1,0:T(8,128)S(1)} all-to-all(f32[8,72,128]{2,1,0:T(8,128)} %half.1), channel_id=1, replica_groups=mesh['z'=8,'x'=4,'yl'=2,'yh'=4,'core'=2] {'yh','core'}, dimensions={0} | all-to-all | bytes 589824 | tf_op jit(solution)/shard_map/all_to_all | solution.py:333
  26.4 3.4 %transform.1 = (bf16[32,2048]{1,0:T(8,128)(2,1)S(1)}, bf16[64,32,128]{2,1,0:T(8,128)(2,1)S(1)}, bf16[256,16,128]{2,1,0:T(8,128)(2,1)}) custom-call(f32[8,72,128]{2,1,0:T(8,128)S(1)} %all_to_all.20.recv_at, bf16[768,2048]{1,0:T(8,128)(2,1)} %c_vir.1), custom_call_target="tpu_custom_call" | custom-call | tf_op jit(solution)/shard_map/transform/pallas_call | solution.py:157
  29.8 29.7 %all_to_all.21 = bf16[64,32,128]{2,1,0:T(8,128)(2,1)S(1)} all-to-all(bf16[64,32,128]{2,1,0:T(8,128)(2,1)S(1)} %get-tuple-element.11), channel_id=1, replica_groups=mesh['z'=8,'x'=4,'yl'=2,'yh'=4,'core'=2] {'z','yl','yh'}, dimensions={0} | all-to-all | bytes 1048576 | tf_op jit(solution)/shard_map/all_to_all | solution.py:335
  59.5 4.4 %collective-permute-start.1 = (bf16[64,32,128]{2,1,0:T(8,128)(2,1)S(1)}, bf16[64,32,128]{2,1,0:T(8,128)(2,1)S(1)}, u32[]{:S(2)}, u32[]{:S(2)}) collective-permute-start(bf16[64,32,128]{2,1,0:T(8,128)(2,1)S(1)} %all_to_all.21), channel_id=1, source_target_pairs={{0,48},{16,0},{32,16},{48,32},{1,49},{17,1},{33,17},{49,33},{2,50}... | collective-permute-start | bytes 1572872 | tf_op jit(solution)/shard_map/ppermute | solution.py:338
  63.9 1.9 %collective-permute-start = (bf16[64,32,128]{2,1,0:T(8,128)(2,1)S(1)}, bf16[64,32,128]{2,1,0:T(8,128)(2,1)S(1)}, u32[]{:S(2)}, u32[]{:S(2)}) collective-permute-start(bf16[64,32,128]{2,1,0:T(8,128)(2,1)S(1)} %all_to_all.21), channel_id=1, source_target_pairs={{0,16},{16,32},{32,48},{48,0},{1,17},{17,33},{33,49},{49,1},{2,18}... | collective-permute-start | bytes 1572872 | tf_op jit(solution)/shard_map/ppermute | solution.py:338
  65.8 11.5 %all-to-all-start.2 = ((bf16[256,16,128]{2,1,0:T(8,128)(2,1)}), bf16[256,16,128]{2,1,0:T(8,128)(2,1)S(1)}, u32[]{:S(2)}, u32[]{:S(2)}) async-start(bf16[256,16,128]{2,1,0:T(8,128)(2,1)} %get-tuple-element.14), calls=%async_computation.2 | async-start | bytes 2097152 | tf_op jit(solution)/shard_map/all_to_all | solution.py:341
  77.3 0.0 collective-permute-done.1.above
  77.3 0.0 collective-permute-done.below
  77.3 0.7 onward.1
  78.1 2.8 %collective-permute-start.2 = (bf16[32,32,128]{2,1,0:T(8,128)(2,1)}, bf16[32,32,128]{2,1,0:T(8,128)(2,1)S(1)}, u32[]{:S(2)}, u32[]{:S(2)}) collective-permute-start(bf16[32,32,128]{2,1,0:T(8,128)(2,1)} %get-tuple-element.12), channel_id=1, source_target_pairs={{0,48},{16,0},{32,16},{48,32},{1,49},{17,1},{33,17},{49,33},{2,50}... | collective-permute-start | bytes 786440 | tf_op jit(solution)/shard_map/ppermute | solution.py:340
  80.9 2.4 %collective-permute-start.3 = (bf16[32,32,128]{2,1,0:T(8,128)(2,1)S(1)}, bf16[32,32,128]{2,1,0:T(8,128)(2,1)S(1)}, u32[]{:S(2)}, u32[]{:S(2)}) collective-permute-start(bf16[32,32,128]{2,1,0:T(8,128)(2,1)S(1)} %get-tuple-element.13), channel_id=1, source_target_pairs={{0,16},{16,32},{32,48},{48,0},{1,17},{17,33},{33,49},{49,1},{2,18}... | collective-permute-start | bytes 786440 | tf_op jit(solution)/shard_map/ppermute | solution.py:340
  83.4 0.1 stack.31.place
  83.5 5.2 %collective-permute-done.2 = bf16[32,32,128]{2,1,0:T(8,128)(2,1)S(1)} collective-permute-done((bf16[32,32,128]{2,1,0:T(8,128)(2,1)}, bf16[32,32,128]{2,1,0:T(8,128)(2,1)S(1)}, u32[]{:S(2)}, u32[]{:S(2)}) %collective-permute-start.2) | collective-permute-done | bytes 262176 | tf_op jit(solution)/shard_map/ppermute | solution.py:340
  88.7 5.2 %collective-permute-done.3 = bf16[32,32,128]{2,1,0:T(8,128)(2,1)S(1)} collective-permute-done((bf16[32,32,128]{2,1,0:T(8,128)(2,1)S(1)}, bf16[32,32,128]{2,1,0:T(8,128)(2,1)S(1)}, u32[]{:S(2)}, u32[]{:S(2)}) %collective-permute-start.3) | collective-permute-done | bytes 262176 | tf_op jit(solution)/shard_map/ppermute | solution.py:340
  93.9 9.8 %all-to-all-done.2 = bf16[256,16,128]{2,1,0:T(8,128)(2,1)S(1)} async-done(((bf16[256,16,128]{2,1,0:T(8,128)(2,1)}), bf16[256,16,128]{2,1,0:T(8,128)(2,1)S(1)}, u32[]{:S(2)}, u32[]{:S(2)}) %all-to-all-start.2) | async-done | bytes 1048608 | tf_op jit(solution)/shard_map/all_to_all | solution.py:341
  103.6 0.0 copy-start
  103.6 0.0 copy-start.1
  103.6 2.5 %gram.1 = (f32[288,1024]{1,0:T(8,128)S(1)}, f32[320,1024]{1,0:T(8,128)S(1)}) custom-call(s32[7]{0:T(128)S(1)} %stack.31.place, bf16[16,8,16,128]{3,2,1,0:T(8,128)(2,1)S(1)} %bitcast.18, bf16[16,8,16,128]{3,2,1,0:T(8,128)(2,1)S(1)} %bitcast.20, bf16[16,8,16,128]{3,2,1,0:T(8,128)(2,1)S(1)} %bitcast.19, bf16[8,8,16,128]{3,2,1,0:T(8,128)(2,1)S(1)} %bitcast.21, ...), custom_call_target="tpu_custom_call" | custom-call | tf_op jit(solution)/shard_map/gram/pallas_call | solution.py:229
  106.1 5.6 %collective-permute-start.4 = (f32[320,1024]{1,0:T(8,128)S(1)}, f32[320,1024]{1,0:T(8,128)S(1)}, u32[]{:S(2)}, u32[]{:S(2)}) collective-permute-start(f32[320,1024]{1,0:T(8,128)S(1)} %get-tuple-element.17), channel_id=1, source_target_pairs={{0,1},{1,0},{2,3},{3,2},{4,5},{5,4},{6,7},{7,6},{8,9},{9,8},{10,11... | collective-permute-start | bytes 3932168 | tf_op jit(solution)/shard_map/ppermute | solution.py:344
  111.7 2.6 %collective-permute-done.4.got = f32[320,1024]{1,0:T(8,128)S(1)} collective-permute-done((f32[320,1024]{1,0:T(8,128)S(1)}, f32[320,1024]{1,0:T(8,128)S(1)}, u32[]{:S(2)}, u32[]{:S(2)}) %collective-permute-start.4) | collective-permute-done | bytes 1310752 | tf_op jit(solution)/shard_map/ppermute | solution.py:344
  114.3 0.0 copy-done
  114.3 0.0 copy-done.1
  114.3 1.5 %energies.1 = (f32[256,1,128]{2,1,0:T(1,128)S(1)}, bf16[32,2048]{1,0:T(8,128)(2,1)}) custom-call(s32[7]{0:T(128)S(1)} %stack.31.place, f32[8]{0:T(128)S(1)} %copy-done.1, f32[288,1024]{1,0:T(8,128)S(1)} %get-tuple-element.16.keep, f32[320,1024]{1,0:T(8,128)S(1)} %collective-permute-done.4.got, f32[16,128]{1,0:T(8,128)S(1)} %bitcast.23, ...), custom_call_target="tpu_custom_call" | custom-call | tf_op jit(solution)/shard_map/energies/pallas_call | solution.py:291
  115.8 22.9 %all_to_all.22.got = f32[256,1,128]{2,1,0:T(1,128)S(1)} all-to-all(f32[256,1,128]{2,1,0:T(1,128)S(1)} %get-tuple-element.19), channel_id=1, replica_groups=mesh['z'=8,'x'=4,'yl'=2,'yh'=4,'core'=2] {'z','x','yl','yh'}, dimensions={0} | all-to-all | bytes 262144 | tf_op jit(solution)/shard_map/all_to_all | solution.py:347
  138.7 0.3 last.1
  139.0 4.7 %psum.7 = f32[8,8]{1,0:T(8,128)} all-reduce(f32[8,8]{1,0:T(8,128)S(1)} %last.1), channel_id=1, replica_groups=mesh['z'=8,'x'=4,'yl'=2,'yh'=4,'core'=2] {'core'}, use_global_device_ids=true, to_apply=%region_0.0 | all-reduce | flops 64 | bytes 512 | tf_op jit(solution)/shard_map/psum | solution.py:348
Async XLA Ops:
  59.5 17.8 %collective-permute-start.1 = (bf16[64,32,128]{2,1,0:T(8,128)(2,1)S(1)}, bf16[64,32,128]{2,1,0:T(8,128)(2,1)S(1)}, u32[]{:S(2)}, u32[]{:S(2)}) collective-permute-start(bf16[64,32,128]{2,1,0:T(8,128)(2,1)S(1)} %all_to_all.21), channel_id=1, source_target_pairs={{0,48},{16,0},{32,16},{48,32},{1,49},{17,1},{33,17},{49,33},{2,50}... | collective-permute-start | bytes 1572872 | tf_op jit(solution)/shard_map/ppermute | solution.py:338
  63.9 13.4 %collective-permute-start = (bf16[64,32,128]{2,1,0:T(8,128)(2,1)S(1)}, bf16[64,32,128]{2,1,0:T(8,128)(2,1)S(1)}, u32[]{:S(2)}, u32[]{:S(2)}) collective-permute-start(bf16[64,32,128]{2,1,0:T(8,128)(2,1)S(1)} %all_to_all.21), channel_id=1, source_target_pairs={{0,16},{16,32},{32,48},{48,0},{1,17},{17,33},{33,49},{49,1},{2,18}... | collective-permute-start | bytes 1572872 | tf_op jit(solution)/shard_map/ppermute | solution.py:338
  65.8 37.8 %all-to-all-start.2 = ((bf16[256,16,128]{2,1,0:T(8,128)(2,1)}), bf16[256,16,128]{2,1,0:T(8,128)(2,1)S(1)}, u32[]{:S(2)}, u32[]{:S(2)}) async-start(bf16[256,16,128]{2,1,0:T(8,128)(2,1)} %get-tuple-element.14), calls=%async_computation.2 | async-start | bytes 2097152 | tf_op jit(solution)/shard_map/all_to_all | solution.py:341
  78.1 10.6 %collective-permute-start.2 = (bf16[32,32,128]{2,1,0:T(8,128)(2,1)}, bf16[32,32,128]{2,1,0:T(8,128)(2,1)S(1)}, u32[]{:S(2)}, u32[]{:S(2)}) collective-permute-start(bf16[32,32,128]{2,1,0:T(8,128)(2,1)} %get-tuple-element.12), channel_id=1, source_target_pairs={{0,48},{16,0},{32,16},{48,32},{1,49},{17,1},{33,17},{49,33},{2,50}... | collective-permute-start | bytes 786440 | tf_op jit(solution)/shard_map/ppermute | solution.py:340
  80.9 12.9 %collective-permute-start.3 = (bf16[32,32,128]{2,1,0:T(8,128)(2,1)S(1)}, bf16[32,32,128]{2,1,0:T(8,128)(2,1)S(1)}, u32[]{:S(2)}, u32[]{:S(2)}) collective-permute-start(bf16[32,32,128]{2,1,0:T(8,128)(2,1)S(1)} %get-tuple-element.13), channel_id=1, source_target_pairs={{0,16},{16,32},{32,48},{48,0},{1,17},{17,33},{33,49},{49,1},{2,18}... | collective-permute-start | bytes 786440 | tf_op jit(solution)/shard_map/ppermute | solution.py:340
  103.6 10.7 %copy-start = (f32[2048]{0:T(1024)S(1)}, f32[2048]{0:T(1024)}, u32[]{:S(2)}) copy-start(f32[2048]{0:T(1024)} %param.13) | copy-start | bytes 24580
  103.6 10.7 %copy-start.1 = (f32[8]{0:T(128)S(1)}, f32[8]{0:T(128)}, u32[]{:S(2)}) copy-start(f32[8]{0:T(128)} %eps_occ.1) | copy-start | bytes 100
  106.1 8.2 %collective-permute-start.4 = (f32[320,1024]{1,0:T(8,128)S(1)}, f32[320,1024]{1,0:T(8,128)S(1)}, u32[]{:S(2)}, u32[]{:S(2)}) collective-permute-start(f32[320,1024]{1,0:T(8,128)S(1)} %get-tuple-element.17), channel_id=1, source_target_pairs={{0,1},{1,0},{2,3},{3,2},{4,5},{5,4},{6,7},{7,6},{8,9},{9,8},{10,11... | collective-permute-start | bytes 3932168 | tf_op jit(solution)/shard_map/ppermute | solution.py:344

commit v7 on v6

--- a/solution.py
+++ b/solution.py
@@ -35,12 +35,21 @@
     return lax.broadcasted_iota(jnp.int32, shape, 0)
 
 
-def half_kernel(blocks, screen, c_occ, ints, out, held, spread, coef, sems):
+def half_kernel(blocks_at, screen_at, c_occ_at, ints, out, blocks, screen, c_occ, held, spread, coef, sems):
     count = held.shape[0]
+    first = [
+        pltpu.make_async_copy(blocks_at, blocks, sems.at[count]),
+        pltpu.make_async_copy(screen_at, screen, sems.at[count + 1]),
+        pltpu.make_async_copy(c_occ_at, c_occ, sems.at[count + 2]),
+    ]
+    for copy in first:
+        copy.start()
     for b in range(count):
         pltpu.make_async_copy(ints.at[b], held.at[b], sems.at[b]).start()
     shape = (SHELL, 4096)
     spread[...] = (lanes(shape) // SHELL == rows(shape)).astype(F32).astype(BF16)
+    for copy in first:
+        copy.wait()
     own = []
     for b in range(count):
         first = blocks[0, b]
@@ -77,13 +86,16 @@
     return pl.pallas_call(
         half_kernel,
         out_shape=jax.ShapeDtypeStruct((8, 72, 128), F32),
-        in_specs=[SMEM, SMEM, VMEM, HBM],
+        in_specs=[HBM, HBM, HBM, HBM],
         out_specs=VMEM,
         scratch_shapes=[
+            pltpu.SMEM((2, ints.shape[0]), jnp.int32),
+            pltpu.SMEM(screen.shape, jnp.int32),
+            pltpu.VMEM((8, c_occ.shape[0]), BF16),
             pltpu.VMEM(ints.shape, BF16),
             pltpu.VMEM((SHELL, 4096), BF16),
             pltpu.VMEM((ints.shape[0], 8, 4096), F32),
-            pltpu.SemaphoreType.DMA((ints.shape[0],)),
+            pltpu.SemaphoreType.DMA((ints.shape[0] + 3,)),
         ],
         compiler_params=grant(54),
         name="half",
@@ -176,22 +188,20 @@
     )(recv, c_vir)
 
 
-def onward_kernel(below, above, low, high):
-    low[...] = above[0:32]
-    high[...] = below[32:64]
-
-
-def onward(below, above):
-    half = jax.ShapeDtypeStruct((32,) + below.shape[1:], BF16)
-    return pl.pallas_call(
-        onward_kernel,
-        out_shape=(half, half),
-        in_specs=[VMEM, VMEM],
-        out_specs=(VMEM, VMEM),
-        compiler_params=grant(4),
-        cost_estimate=pl.CostEstimate(flops=1 << 35, bytes_accessed=1 << 21, transcendentals=0),
+def onward_kernel(half, block, out):
+    out[...] = block[half * 32 : half * 32 + 32]
+
+
+def onward(half, block, cost):
+    return pl.pallas_call(
+        functools.partial(onward_kernel, half),
+        out_shape=jax.ShapeDtypeStruct((32,) + block.shape[1:], BF16),
+        in_specs=[VMEM],
+        out_specs=VMEM,
+        compiler_params=grant(2),
+        cost_estimate=pl.CostEstimate(flops=cost, bytes_accessed=1 << 20, transcendentals=0),
         name="onward",
-    )(below, above)
+    )(block)
 
 
 def gram_kernel(place, here, below, above, low, high, sides, two, keep, give, wide, thin, all_t, all_s):
@@ -336,8 +346,8 @@
     up = [(i, (i + 1) % 4) for i in range(4)]
     down = [(i, (i + 3) % 4) for i in range(4)]
     below, above = lax.ppermute(here, "x", up), lax.ppermute(here, "x", down)
-    low, high = onward(below, above)
-    low, high = lax.ppermute(low, "x", down), lax.ppermute(high, "x", up)
+    low = lax.ppermute(onward(0, above, 1 << 33), "x", down)
+    high = lax.ppermute(onward(1, below, 1 << 35), "x", up)
     sides = lax.all_to_all(thin, CHIPS, 0, 0, tiled=True)
 
     keep, give = gram(place, here, below, above, low, high, sides, two)

time: 144 us -> 150 us (1.042)
  blocking collectives: 78.8 us -> 82.3 us
  waiting for transfers between devices: 22.8 us -> 26.1 us
    ppermute x2, waiting for transfers between devices: 0.01 us -> 17 us  [body(): below, above = (lax.ppermute(here, 'x', up), lax.ppermute(here, 'x', down))]
    all_to_all x1, waiting for transfers between devices: 9.75 us -> 0.01 us  [body(): sides = lax.all_to_all(thin, CHIPS, 0, 0, tiled=True)]
    ppermute x2, waiting for transfers between devices: 10.4 us -> 6.51 us  [the longest x1 6.51 us: body(): high = lax.ppermute(onward(1, below, 1 << 35), 'x', up)]
    all_to_all x1, blocking collectives: 22.9 us -> 26.3 us  [body(): energy = lax.all_to_all(energy, CHIPS, 0, 0, tiled=True)]
    all_to_all x1, starting transfers between devices: 11.5 us -> 9.38 us  [body(): sides = lax.all_to_all(thin, CHIPS, 0, 0, tiled=True)]
  transfers between devices with their start and end apart: 6 -> 6, of which waited for: 4 -> 3; matrix products, arithmetic and copies ran while one was open for 0% -> 0% of each run, Pallas kernels for 1% -> 0%
where the time goes in v7:
time: 150 us
  blocking collectives  82.3 us (55%)
  starting transfers between devices  28.3 us (19%)
  waiting for transfers between devices  26.1 us (17%)
  Pallas kernels  12 us (8%)
    all_to_all x1, blocking collectives, body(): here = lax.all_to_all(wide, ('z', 'yl', 'yh'), 0, 0, tiled=True)  29.7 us
    all_to_all x1, blocking collectives, body(): energy = lax.all_to_all(energy, CHIPS, 0, 0, tiled=True)  26.3 us
    all_to_all x1, blocking collectives, body(): recv = lax.all_to_all(sent, GRP, 0, 0, tiled=True)  21.5 us
    ppermute x2, waiting for transfers between devices, body(): below, above = (lax.ppermute(here, 'x', up), lax.ppermute(here, 'x', down))  17 us
    all_to_all x1, starting transfers between devices, body(): sides = lax.all_to_all(thin, CHIPS, 0, 0, tiled=True)  9.38 us
    ppermute x1, waiting for transfers between devices, body(): high = lax.ppermute(onward(1, below, 1 << 35), 'x', up)  6.51 us
    ppermute x2, starting transfers between devices, body(): below, above = (lax.ppermute(here, 'x', up), lax.ppermute(here, 'x', down))  6.3 us
    ppermute x1, starting transfers between devices, body(): got = lax.ppermute(give, 'core', [(0, 1), (1, 0)])  6.15 us
  transfers between devices with their start and end apart: 6, of which 3 were waited for; matrix products, arithmetic and copies ran while one was open for 0% of the time, Pallas kernels for 0%

profile of v7, /device:TPU:1, one launch (start us, length us, event | category | flops | bytes accessed | tf_op | source)
XLA Modules:
  0.0 149.5 jit_solution(18177467882057363594)
XLA Ops:
  0.6 3.6 %half.1 = f32[8,72,128]{2,1,0:T(8,128)} custom-call(s32[2,4]{1,0:T(2,128)} %bitcast.25, s32[4]{0:T(128)} %screen_at.1, bf16[8,768]{1,0:T(8,128)(2,1)} %bitcast.24, bf16[4,32,4096]{2,1,0:T(8,128)(2,1)} %ints.1), custom_call_target="tpu_custom_call" | custom-call | tf_op jit(solution)/shard_map/half/pallas_call | solution.py:86
  4.2 21.5 %all_to_all.20.recv_at = f32[8,72,128]{2,1,0:T(8,128)S(1)} all-to-all(f32[8,72,128]{2,1,0:T(8,128)} %half.1), channel_id=1, replica_groups=mesh['z'=8,'x'=4,'yl'=2,'yh'=4,'core'=2] {'yh','core'}, dimensions={0} | all-to-all | bytes 589824 | tf_op jit(solution)/shard_map/all_to_all | solution.py:343
  25.7 3.4 %transform.1 = (bf16[32,2048]{1,0:T(8,128)(2,1)S(1)}, bf16[64,32,128]{2,1,0:T(8,128)(2,1)S(1)}, bf16[256,16,128]{2,1,0:T(8,128)(2,1)}) custom-call(f32[8,72,128]{2,1,0:T(8,128)S(1)} %all_to_all.20.recv_at, bf16[768,2048]{1,0:T(8,128)(2,1)} %c_vir.1), custom_call_target="tpu_custom_call" | custom-call | tf_op jit(solution)/shard_map/transform/pallas_call | solution.py:169
  29.1 29.7 %all_to_all.21 = bf16[64,32,128]{2,1,0:T(8,128)(2,1)S(1)} all-to-all(bf16[64,32,128]{2,1,0:T(8,128)(2,1)S(1)} %get-tuple-element.9), channel_id=1, replica_groups=mesh['z'=8,'x'=4,'yl'=2,'yh'=4,'core'=2] {'z','yl','yh'}, dimensions={0} | all-to-all | bytes 1048576 | tf_op jit(solution)/shard_map/all_to_all | solution.py:345
  58.8 4.4 %collective-permute-start.1 = (bf16[64,32,128]{2,1,0:T(8,128)(2,1)S(1)}, bf16[64,32,128]{2,1,0:T(8,128)(2,1)S(1)}, u32[]{:S(2)}, u32[]{:S(2)}) collective-permute-start(bf16[64,32,128]{2,1,0:T(8,128)(2,1)S(1)} %all_to_all.21), channel_id=1, source_target_pairs={{0,48},{16,0},{32,16},{48,32},{1,49},{17,1},{33,17},{49,33},{2,50}... | collective-permute-start | bytes 1572872 | tf_op jit(solution)/shard_map/ppermute | solution.py:348
  63.2 9.4 %all-to-all-start.2 = ((bf16[256,16,128]{2,1,0:T(8,128)(2,1)}), bf16[256,16,128]{2,1,0:T(8,128)(2,1)S(1)}, u32[]{:S(2)}, u32[]{:S(2)}) async-start(bf16[256,16,128]{2,1,0:T(8,128)(2,1)} %get-tuple-element.10), calls=%async_computation.2 | async-start | bytes 2097152 | tf_op jit(solution)/shard_map/all_to_all | solution.py:351
  72.6 1.9 %collective-permute-start = (bf16[64,32,128]{2,1,0:T(8,128)(2,1)S(1)}, bf16[64,32,128]{2,1,0:T(8,128)(2,1)S(1)}, u32[]{:S(2)}, u32[]{:S(2)}) collective-permute-start(bf16[64,32,128]{2,1,0:T(8,128)(2,1)S(1)} %all_to_all.21), channel_id=1, source_target_pairs={{0,16},{16,32},{32,48},{48,0},{1,17},{17,33},{33,49},{49,1},{2,18}... | collective-permute-start | bytes 1572872 | tf_op jit(solution)/shard_map/ppermute | solution.py:348
  74.5 0.0 collective-permute-done.1.block
  74.6 4.6 %collective-permute-start.2 = (bf16[32,32,128]{2,1,0:T(8,128)(2,1)S(1)}, bf16[32,32,128]{2,1,0:T(8,128)(2,1)S(1)}, u32[]{:S(2)}, u32[]{:S(2)}) collective-permute-start(bf16[32,32,128]{2,1,0:T(8,128)(2,1)S(1)} %onward.2), channel_id=1, source_target_pairs={{0,48},{16,0},{32,16},{48,32},{1,49},{17,1},{33,17},{49,33},{2,50}... | collective-permute-start | bytes 786440 | tf_op jit(solution)/shard_map/ppermute | solution.py:349
  79.1 17.0 %collective-permute-done.block = bf16[64,32,128]{2,1,0:T(8,128)(2,1)S(1)} collective-permute-done((bf16[64,32,128]{2,1,0:T(8,128)(2,1)S(1)}, bf16[64,32,128]{2,1,0:T(8,128)(2,1)S(1)}, u32[]{:S(2)}, u32[]{:S(2)}) %collective-permute-start) | collective-permute-done | bytes 524320 | tf_op jit(solution)/shard_map/ppermute | solution.py:348
  96.1 0.7 onward.3
  96.8 1.9 %collective-permute-start.3 = (bf16[32,32,128]{2,1,0:T(8,128)(2,1)}, bf16[32,32,128]{2,1,0:T(8,128)(2,1)S(1)}, u32[]{:S(2)}, u32[]{:S(2)}) collective-permute-start(bf16[32,32,128]{2,1,0:T(8,128)(2,1)} %onward.3), channel_id=1, source_target_pairs={{0,16},{16,32},{32,48},{48,0},{1,17},{17,33},{33,49},{49,1},{2,18}... | collective-permute-start | bytes 786440 | tf_op jit(solution)/shard_map/ppermute | solution.py:350
  98.8 0.1 stack.31.place
  98.9 0.0 collective-permute-done.2
  98.9 6.5 %collective-permute-done.3 = bf16[32,32,128]{2,1,0:T(8,128)(2,1)S(1)} collective-permute-done((bf16[32,32,128]{2,1,0:T(8,128)(2,1)}, bf16[32,32,128]{2,1,0:T(8,128)(2,1)S(1)}, u32[]{:S(2)}, u32[]{:S(2)}) %collective-permute-start.3) | collective-permute-done | bytes 262176 | tf_op jit(solution)/shard_map/ppermute | solution.py:350
  105.4 0.0 all-to-all-done.2
  105.4 0.0 copy-start
  105.4 0.0 copy-start.1
  105.4 2.5 %gram.1 = (f32[288,1024]{1,0:T(8,128)S(1)}, f32[320,1024]{1,0:T(8,128)S(1)}) custom-call(s32[7]{0:T(128)S(1)} %stack.31.place, bf16[16,8,16,128]{3,2,1,0:T(8,128)(2,1)S(1)} %bitcast.18, bf16[16,8,16,128]{3,2,1,0:T(8,128)(2,1)S(1)} %bitcast.20, bf16[16,8,16,128]{3,2,1,0:T(8,128)(2,1)S(1)} %bitcast.19, bf16[8,8,16,128]{3,2,1,0:T(8,128)(2,1)S(1)} %bitcast.21, ...), custom_call_target="tpu_custom_call" | custom-call | tf_op jit(solution)/shard_map/gram/pallas_call | solution.py:239
  107.8 6.1 %collective-permute-start.4 = (f32[320,1024]{1,0:T(8,128)S(1)}, f32[320,1024]{1,0:T(8,128)S(1)}, u32[]{:S(2)}, u32[]{:S(2)}) collective-permute-start(f32[320,1024]{1,0:T(8,128)S(1)} %get-tuple-element.13), channel_id=1, source_target_pairs={{0,1},{1,0},{2,3},{3,2},{4,5},{5,4},{6,7},{7,6},{8,9},{9,8},{10,11... | collective-permute-start | bytes 3932168 | tf_op jit(solution)/shard_map/ppermute | solution.py:354
  114.0 2.6 %collective-permute-done.4.got = f32[320,1024]{1,0:T(8,128)S(1)} collective-permute-done((f32[320,1024]{1,0:T(8,128)S(1)}, f32[320,1024]{1,0:T(8,128)S(1)}, u32[]{:S(2)}, u32[]{:S(2)}) %collective-permute-start.4) | collective-permute-done | bytes 1310752 | tf_op jit(solution)/shard_map/ppermute | solution.py:354
  116.6 0.0 copy-done
  116.6 0.0 copy-done.1
  116.6 1.5 energies.1
  118.1 26.3 %all_to_all.22.got = f32[256,1,128]{2,1,0:T(1,128)S(1)} all-to-all(f32[256,1,128]{2,1,0:T(1,128)S(1)} %get-tuple-element.15), channel_id=1, replica_groups=mesh['z'=8,'x'=4,'yl'=2,'yh'=4,'core'=2] {'z','x','yl','yh'}, dimensions={0} | all-to-all | bytes 262144 | tf_op jit(solution)/shard_map/all_to_all | solution.py:357
  144.5 0.3 last.1
  144.8 4.7 %psum.7 = f32[8,8]{1,0:T(8,128)} all-reduce(f32[8,8]{1,0:T(8,128)S(1)} %last.1), channel_id=1, replica_groups=mesh['z'=8,'x'=4,'yl'=2,'yh'=4,'core'=2] {'core'}, use_global_device_ids=true, to_apply=%region_0.0 | all-reduce | flops 64 | bytes 512 | tf_op jit(solution)/shard_map/psum | solution.py:358
  (1 shorter events, 0.0 us)
Async XLA Ops:
  58.8 15.7 %collective-permute-start.1 = (bf16[64,32,128]{2,1,0:T(8,128)(2,1)S(1)}, bf16[64,32,128]{2,1,0:T(8,128)(2,1)S(1)}, u32[]{:S(2)}, u32[]{:S(2)}) collective-permute-start(bf16[64,32,128]{2,1,0:T(8,128)(2,1)S(1)} %all_to_all.21), channel_id=1, source_target_pairs={{0,48},{16,0},{32,16},{48,32},{1,49},{17,1},{33,17},{49,33},{2,50}... | collective-permute-start | bytes 1572872 | tf_op jit(solution)/shard_map/ppermute | solution.py:348
  63.2 42.2 %all-to-all-start.2 = ((bf16[256,16,128]{2,1,0:T(8,128)(2,1)}), bf16[256,16,128]{2,1,0:T(8,128)(2,1)S(1)}, u32[]{:S(2)}, u32[]{:S(2)}) async-start(bf16[256,16,128]{2,1,0:T(8,128)(2,1)} %get-tuple-element.10), calls=%async_computation.2 | async-start | bytes 2097152 | tf_op jit(solution)/shard_map/all_to_all | solution.py:351
  72.6 23.5 %collective-permute-start = (bf16[64,32,128]{2,1,0:T(8,128)(2,1)S(1)}, bf16[64,32,128]{2,1,0:T(8,128)(2,1)S(1)}, u32[]{:S(2)}, u32[]{:S(2)}) collective-permute-start(bf16[64,32,128]{2,1,0:T(8,128)(2,1)S(1)} %all_to_all.21), channel_id=1, source_target_pairs={{0,16},{16,32},{32,48},{48,0},{1,17},{17,33},{33,49},{49,1},{2,18}... | collective-permute-start | bytes 1572872 | tf_op jit(solution)/shard_map/ppermute | solution.py:348
  74.6 24.3 %collective-permute-start.2 = (bf16[32,32,128]{2,1,0:T(8,128)(2,1)S(1)}, bf16[32,32,128]{2,1,0:T(8,128)(2,1)S(1)}, u32[]{:S(2)}, u32[]{:S(2)}) collective-permute-start(bf16[32,32,128]{2,1,0:T(8,128)(2,1)S(1)} %onward.2), channel_id=1, source_target_pairs={{0,48},{16,0},{32,16},{48,32},{1,49},{17,1},{33,17},{49,33},{2,50}... | collective-permute-start | bytes 786440 | tf_op jit(solution)/shard_map/ppermute | solution.py:349
  96.8 8.5 %collective-permute-start.3 = (bf16[32,32,128]{2,1,0:T(8,128)(2,1)}, bf16[32,32,128]{2,1,0:T(8,128)(2,1)S(1)}, u32[]{:S(2)}, u32[]{:S(2)}) collective-permute-start(bf16[32,32,128]{2,1,0:T(8,128)(2,1)} %onward.3), channel_id=1, source_target_pairs={{0,16},{16,32},{32,48},{48,0},{1,17},{17,33},{33,49},{49,1},{2,18}... | collective-permute-start | bytes 786440 | tf_op jit(solution)/shard_map/ppermute | solution.py:350
  105.4 11.3 %copy-start = (f32[2048]{0:T(1024)S(1)}, f32[2048]{0:T(1024)}, u32[]{:S(2)}) copy-start(f32[2048]{0:T(1024)} %param.13) | copy-start | bytes 24580
  105.4 11.3 %copy-start.1 = (f32[8]{0:T(128)S(1)}, f32[8]{0:T(128)}, u32[]{:S(2)}) copy-start(f32[8]{0:T(128)} %eps_occ.1) | copy-start | bytes 100
  107.8 8.8 %collective-permute-start.4 = (f32[320,1024]{1,0:T(8,128)S(1)}, f32[320,1024]{1,0:T(8,128)S(1)}, u32[]{:S(2)}, u32[]{:S(2)}) collective-permute-start(f32[320,1024]{1,0:T(8,128)S(1)} %get-tuple-element.13), channel_id=1, source_target_pairs={{0,1},{1,0},{2,3},{3,2},{4,5},{5,4},{6,7},{7,6},{8,9},{9,8},{10,11... | collective-permute-start | bytes 3932168 | tf_op jit(solution)/shard_map/ppermute | solution.py:354

commit v8 on v6

--- a/solution.py
+++ b/solution.py
@@ -11,9 +11,11 @@
 SHELLS = 12
 TILES = 16
 CHUNKS = 3
-AXES = ("z", "x", "yl", "yh", "core")
-CHIPS = ("z", "x", "yl", "yh")
-PAIR = ("z", "x", "yl")
+AXES = ("zh", "zl", "x", "yl", "yh", "core")
+CHIPS = ("zh", "zl", "x", "yl", "yh")
+PAIR = ("zh", "zl", "x", "yl")
+NEAR = ("zl", "x", "yl", "core")
+FAR = ("zh", "yh")
 GRP = ("yh", "core")
 F32 = jnp.float32
 BF16 = jnp.bfloat16
@@ -35,12 +37,21 @@
     return lax.broadcasted_iota(jnp.int32, shape, 0)
 
 
-def half_kernel(blocks, screen, c_occ, ints, out, held, spread, coef, sems):
+def half_kernel(blocks_at, screen_at, c_occ_at, ints, out, blocks, screen, c_occ, held, spread, coef, sems):
     count = held.shape[0]
+    first = [
+        pltpu.make_async_copy(blocks_at, blocks, sems.at[count]),
+        pltpu.make_async_copy(screen_at, screen, sems.at[count + 1]),
+        pltpu.make_async_copy(c_occ_at, c_occ, sems.at[count + 2]),
+    ]
+    for copy in first:
+        copy.start()
     for b in range(count):
         pltpu.make_async_copy(ints.at[b], held.at[b], sems.at[b]).start()
     shape = (SHELL, 4096)
     spread[...] = (lanes(shape) // SHELL == rows(shape)).astype(F32).astype(BF16)
+    for copy in first:
+        copy.wait()
     own = []
     for b in range(count):
         first = blocks[0, b]
@@ -77,13 +88,16 @@
     return pl.pallas_call(
         half_kernel,
         out_shape=jax.ShapeDtypeStruct((8, 72, 128), F32),
-        in_specs=[SMEM, SMEM, VMEM, HBM],
+        in_specs=[HBM, HBM, HBM, HBM],
         out_specs=VMEM,
         scratch_shapes=[
+            pltpu.SMEM((2, ints.shape[0]), jnp.int32),
+            pltpu.SMEM(screen.shape, jnp.int32),
+            pltpu.VMEM((8, c_occ.shape[0]), BF16),
             pltpu.VMEM(ints.shape, BF16),
             pltpu.VMEM((SHELL, 4096), BF16),
             pltpu.VMEM((ints.shape[0], 8, 4096), F32),
-            pltpu.SemaphoreType.DMA((ints.shape[0],)),
+            pltpu.SemaphoreType.DMA((ints.shape[0] + 3,)),
         ],
         compiler_params=grant(54),
         name="half",
@@ -290,7 +304,7 @@
 def energies(scale, place, eps_occ, keep, got, eps_vir, two):
     return pl.pallas_call(
         functools.partial(energy_kernel, scale),
-        out_shape=(jax.ShapeDtypeStruct((256, 1, 128), F32), jax.ShapeDtypeStruct(two.shape, BF16)),
+        out_shape=(jax.ShapeDtypeStruct((32, 1, 128), F32), jax.ShapeDtypeStruct(two.shape, BF16)),
         in_specs=[SMEM, SMEM, VMEM, VMEM, VMEM, VMEM],
         out_specs=(VMEM, VMEM),
         scratch_shapes=[pltpu.VMEM((64, 128), F32)],
@@ -300,10 +314,14 @@
 
 
 def position():
-    z, x, yl, yh, core = (lax.axis_index(axis) for axis in AXES)
-    tile, kind = z * 2 + yl, x * 4 + yh
+    zh, zl, x, yl, yh, core = (lax.axis_index(axis) for axis in AXES)
+    tile, kind = zh * 4 + zl * 2 + yl, x * 4 + yh
     step, side = lax.shift_right_logical(kind, 1) + 1, kind & 1
     return jnp.stack([tile, (tile + step) & (TILES - 1), step, side, core, lax.shift_right_logical(kind, 1), x])
+
+
+def again_kernel(got, out):
+    out[...] = jnp.broadcast_to(jnp.sum(got[...], axis=0)[None], out.shape)
 
 
 def last_kernel(got, out):
@@ -332,7 +350,7 @@
     sent = half_transform(c_occ, ints, blocks, screen)
     recv = lax.all_to_all(sent, GRP, 0, 0, tiled=True)
     two, wide, thin = transform(recv, c_vir)
-    here = lax.all_to_all(wide, ("z", "yl", "yh"), 0, 0, tiled=True)
+    here = lax.all_to_all(wide, ("zh", "zl", "yl", "yh"), 0, 0, tiled=True)
     up = [(i, (i + 1) % 4) for i in range(4)]
     down = [(i, (i + 3) % 4) for i in range(4)]
     below, above = lax.ppermute(here, "x", up), lax.ppermute(here, "x", down)
@@ -344,13 +362,14 @@
     got = lax.ppermute(give, "core", [(0, 1), (1, 0)])
     scale = 1.0 / (float(vir) * float(vir) * 2048.0)
     energy, bmat = energies(scale, place, eps_occ, keep, got, eps_vir, two)
-    energy = lax.all_to_all(energy, CHIPS, 0, 0, tiled=True)
-    energy = lax.psum(small(last_kernel, (occ, occ), "last")(energy), "core")
+    energy = lax.all_to_all(energy, NEAR, 0, 0, tiled=True)
+    energy = lax.all_to_all(small(again_kernel, (16, 1, 128), "again")(energy), FAR, 0, 0, tiled=True)
+    energy = small(last_kernel, (occ, occ), "last")(energy)
     return bmat.reshape(1, 32, vir), energy
 
 
 def solution(mesh):
-    fine = Mesh(mesh.devices.reshape(8, 4, 2, 4, 2), AXES)
+    fine = Mesh(mesh.devices.reshape(4, 2, 4, 2, 4, 2), AXES)
     return jax.shard_map(
         body,
         mesh=fine,

time: 144 us -> 144 us (level)
    psum x1 -> x0, blocking collectives: 4.72 us -> none  [body(): energy = lax.psum(small(last_kernel, (occ, occ), 'last')(energy), 'core')]
    all_to_all x2 -> x3, blocking collectives: 52.6 us -> 57.1 us  [the longest x1 29.7 us: body(): here = lax.all_to_all(wide, ('zh', 'zl', 'yl', 'yh'), 0, 0, tiled=True)]
where the time goes in v8:
time: 144 us; the launch traced here: 143 us
  blocking collectives  78.6 us (55%)
  starting transfers between devices  28.6 us (20%)
  waiting for transfers between devices  22.8 us (16%)
  Pallas kernels  12.4 us (9%)
    all_to_all x1, blocking collectives, body(): here = lax.all_to_all(wide, ('zh', 'zl', 'yl', 'yh'), 0, 0, tiled=True)  29.7 us
    all_to_all x1, blocking collectives, body(): recv = lax.all_to_all(sent, GRP, 0, 0, tiled=True)  21.5 us
    all_to_all x1, blocking collectives, body(): lax.all_to_all(small(again_kernel, (16, 1, 128), 'again')(energy), FAR, 0...  14.6 us
    all_to_all x1, blocking collectives, body(): energy = lax.all_to_all(energy, NEAR, 0, 0, tiled=True)  12.8 us
    all_to_all x1, starting transfers between devices, body(): sides = lax.all_to_all(thin, CHIPS, 0, 0, tiled=True)  11.5 us
    ppermute x2, waiting for transfers between devices, body(): low, high = (lax.ppermute(low, 'x', down), lax.ppermute(high, 'x', up))  10.4 us
    all_to_all x1, waiting for transfers between devices, body(): sides = lax.all_to_all(thin, CHIPS, 0, 0, tiled=True)  9.74 us
    ppermute x2, starting transfers between devices, body(): below, above = (lax.ppermute(here, 'x', up), lax.ppermute(here, 'x', down))  6.3 us
  transfers between devices with their start and end apart: 6, of which 4 were waited for; matrix products, arithmetic and copies ran while one was open for 0% of the time, Pallas kernels for 1%

profile of v8, /device:TPU:1, one launch (start us, length us, event | category | flops | bytes accessed | tf_op | source)
XLA Modules:
  0.0 143.3 jit_solution(13337884458712601601)
XLA Ops:
  0.6 3.6 %half.1 = f32[8,72,128]{2,1,0:T(8,128)} custom-call(s32[2,4]{1,0:T(2,128)} %bitcast.25, s32[4]{0:T(128)} %screen_at.1, bf16[8,768]{1,0:T(8,128)(2,1)} %bitcast.24, bf16[4,32,4096]{2,1,0:T(8,128)(2,1)} %ints.1), custom_call_target="tpu_custom_call" | custom-call | tf_op jit(solution)/shard_map/half/pallas_call | solution.py:88
  4.2 21.5 %all_to_all.25.recv_at = f32[8,72,128]{2,1,0:T(8,128)S(1)} all-to-all(f32[8,72,128]{2,1,0:T(8,128)} %half.1), channel_id=1, replica_groups=mesh['zh'=4,'zl'=2,'x'=4,'yl'=2,'yh'=4,'core'=2] {'yh','core'}, dimensions={0} | all-to-all | bytes 589824 | tf_op jit(solution)/shard_map/all_to_all | solution.py:351
  25.7 3.4 %transform.1 = (bf16[32,2048]{1,0:T(8,128)(2,1)S(1)}, bf16[64,32,128]{2,1,0:T(8,128)(2,1)S(1)}, bf16[256,16,128]{2,1,0:T(8,128)(2,1)}) custom-call(f32[8,72,128]{2,1,0:T(8,128)S(1)} %all_to_all.25.recv_at, bf16[768,2048]{1,0:T(8,128)(2,1)} %c_vir.1), custom_call_target="tpu_custom_call" | custom-call | tf_op jit(solution)/shard_map/transform/pallas_call | solution.py:171
  29.1 29.7 %all_to_all.26 = bf16[64,32,128]{2,1,0:T(8,128)(2,1)S(1)} all-to-all(bf16[64,32,128]{2,1,0:T(8,128)(2,1)S(1)} %get-tuple-element.11), channel_id=1, replica_groups=mesh['zh'=4,'zl'=2,'x'=4,'yl'=2,'yh'=4,'core'=2] {'zh','zl','yl','yh'}, dimensions={0} | all-to-all | bytes 1048576 | tf_op jit(solution)/shard_map/all_to_all | solution.py:353
  58.8 4.4 %collective-permute-start.1 = (bf16[64,32,128]{2,1,0:T(8,128)(2,1)S(1)}, bf16[64,32,128]{2,1,0:T(8,128)(2,1)S(1)}, u32[]{:S(2)}, u32[]{:S(2)}) collective-permute-start(bf16[64,32,128]{2,1,0:T(8,128)(2,1)S(1)} %all_to_all.26), channel_id=1, source_target_pairs={{0,48},{16,0},{32,16},{48,32},{1,49},{17,1},{33,17},{49,33},{2,50}... | collective-permute-start | bytes 1572872 | tf_op jit(solution)/shard_map/ppermute | solution.py:356
  63.2 1.9 %collective-permute-start = (bf16[64,32,128]{2,1,0:T(8,128)(2,1)S(1)}, bf16[64,32,128]{2,1,0:T(8,128)(2,1)S(1)}, u32[]{:S(2)}, u32[]{:S(2)}) collective-permute-start(bf16[64,32,128]{2,1,0:T(8,128)(2,1)S(1)} %all_to_all.26), channel_id=1, source_target_pairs={{0,16},{16,32},{32,48},{48,0},{1,17},{17,33},{33,49},{49,1},{2,18}... | collective-permute-start | bytes 1572872 | tf_op jit(solution)/shard_map/ppermute | solution.py:356
  65.1 11.5 %all-to-all-start.2 = ((bf16[256,16,128]{2,1,0:T(8,128)(2,1)}), bf16[256,16,128]{2,1,0:T(8,128)(2,1)S(1)}, u32[]{:S(2)}, u32[]{:S(2)}) async-start(bf16[256,16,128]{2,1,0:T(8,128)(2,1)} %get-tuple-element.14), calls=%async_computation.2 | async-start | bytes 2097152 | tf_op jit(solution)/shard_map/all_to_all | solution.py:359
  76.6 0.0 collective-permute-done.1.above
  76.7 0.0 collective-permute-done.below
  76.7 0.8 onward.1
  77.4 2.8 %collective-permute-start.2 = (bf16[32,32,128]{2,1,0:T(8,128)(2,1)}, bf16[32,32,128]{2,1,0:T(8,128)(2,1)S(1)}, u32[]{:S(2)}, u32[]{:S(2)}) collective-permute-start(bf16[32,32,128]{2,1,0:T(8,128)(2,1)} %get-tuple-element.12), channel_id=1, source_target_pairs={{0,48},{16,0},{32,16},{48,32},{1,49},{17,1},{33,17},{49,33},{2,50}... | collective-permute-start | bytes 786440 | tf_op jit(solution)/shard_map/ppermute | solution.py:358
  80.3 2.4 %collective-permute-start.3 = (bf16[32,32,128]{2,1,0:T(8,128)(2,1)S(1)}, bf16[32,32,128]{2,1,0:T(8,128)(2,1)S(1)}, u32[]{:S(2)}, u32[]{:S(2)}) collective-permute-start(bf16[32,32,128]{2,1,0:T(8,128)(2,1)S(1)} %get-tuple-element.13), channel_id=1, source_target_pairs={{0,16},{16,32},{32,48},{48,0},{1,17},{17,33},{33,49},{49,1},{2,18}... | collective-permute-start | bytes 786440 | tf_op jit(solution)/shard_map/ppermute | solution.py:358
  82.7 0.1 stack.31.place
  82.8 5.2 %collective-permute-done.2 = bf16[32,32,128]{2,1,0:T(8,128)(2,1)S(1)} collective-permute-done((bf16[32,32,128]{2,1,0:T(8,128)(2,1)}, bf16[32,32,128]{2,1,0:T(8,128)(2,1)S(1)}, u32[]{:S(2)}, u32[]{:S(2)}) %collective-permute-start.2) | collective-permute-done | bytes 262176 | tf_op jit(solution)/shard_map/ppermute | solution.py:358
  88.0 5.2 %collective-permute-done.3 = bf16[32,32,128]{2,1,0:T(8,128)(2,1)S(1)} collective-permute-done((bf16[32,32,128]{2,1,0:T(8,128)(2,1)S(1)}, bf16[32,32,128]{2,1,0:T(8,128)(2,1)S(1)}, u32[]{:S(2)}, u32[]{:S(2)}) %collective-permute-start.3) | collective-permute-done | bytes 262176 | tf_op jit(solution)/shard_map/ppermute | solution.py:358
  93.2 9.7 %all-to-all-done.2 = bf16[256,16,128]{2,1,0:T(8,128)(2,1)S(1)} async-done(((bf16[256,16,128]{2,1,0:T(8,128)(2,1)}), bf16[256,16,128]{2,1,0:T(8,128)(2,1)S(1)}, u32[]{:S(2)}, u32[]{:S(2)}) %all-to-all-start.2) | async-done | bytes 1048608 | tf_op jit(solution)/shard_map/all_to_all | solution.py:359
  103.0 0.0 copy-start
  103.0 0.0 copy-start.1
  103.0 2.5 %gram.1 = (f32[288,1024]{1,0:T(8,128)S(1)}, f32[320,1024]{1,0:T(8,128)S(1)}) custom-call(s32[7]{0:T(128)S(1)} %stack.31.place, bf16[16,8,16,128]{3,2,1,0:T(8,128)(2,1)S(1)} %bitcast.18, bf16[16,8,16,128]{3,2,1,0:T(8,128)(2,1)S(1)} %bitcast.20, bf16[16,8,16,128]{3,2,1,0:T(8,128)(2,1)S(1)} %bitcast.19, bf16[8,8,16,128]{3,2,1,0:T(8,128)(2,1)S(1)} %bitcast.21, ...), custom_call_target="tpu_custom_call" | custom-call | tf_op jit(solution)/shard_map/gram/pallas_call | solution.py:243
  105.4 5.6 %collective-permute-start.4 = (f32[320,1024]{1,0:T(8,128)S(1)}, f32[320,1024]{1,0:T(8,128)S(1)}, u32[]{:S(2)}, u32[]{:S(2)}) collective-permute-start(f32[320,1024]{1,0:T(8,128)S(1)} %get-tuple-element.17), channel_id=1, source_target_pairs={{0,1},{1,0},{2,3},{3,2},{4,5},{5,4},{6,7},{7,6},{8,9},{9,8},{10,11... | collective-permute-start | bytes 3932168 | tf_op jit(solution)/shard_map/ppermute | solution.py:362
  111.0 2.6 %collective-permute-done.4.got = f32[320,1024]{1,0:T(8,128)S(1)} collective-permute-done((f32[320,1024]{1,0:T(8,128)S(1)}, f32[320,1024]{1,0:T(8,128)S(1)}, u32[]{:S(2)}, u32[]{:S(2)}) %collective-permute-start.4) | collective-permute-done | bytes 1310752 | tf_op jit(solution)/shard_map/ppermute | solution.py:362
  113.7 0.0 copy-done
  113.7 0.0 copy-done.1
  113.7 1.5 %energies.1 = (f32[32,1,128]{2,1,0:T(1,128)S(1)}, bf16[32,2048]{1,0:T(8,128)(2,1)}) custom-call(s32[7]{0:T(128)S(1)} %stack.31.place, f32[8]{0:T(128)S(1)} %copy-done.1, f32[288,1024]{1,0:T(8,128)S(1)} %get-tuple-element.16.keep, f32[320,1024]{1,0:T(8,128)S(1)} %collective-permute-done.4.got, f32[16,128]{1,0:T(8,128)S(1)} %bitcast.23, ...), custom_call_target="tpu_custom_call" | custom-call | tf_op jit(solution)/shard_map/energies/pallas_call | solution.py:305
  115.1 12.8 %all_to_all.27.got = f32[32,1,128]{2,1,0:T(1,128)S(1)} all-to-all(f32[32,1,128]{2,1,0:T(1,128)S(1)} %get-tuple-element.19), channel_id=1, replica_groups=mesh['zh'=4,'zl'=2,'x'=4,'yl'=2,'yh'=4,'core'=2] {'zl','x','yl','core'}, dimensions={0} | all-to-all | bytes 32768 | tf_op jit(solution)/shard_map/all_to_all | solution.py:365
  128.0 14.6 %all_to_all.28.got = f32[16,1,128]{2,1,0:T(1,128)S(1)} all-to-all(f32[16,1,128]{2,1,0:T(1,128)S(1)} %again.1), channel_id=1, replica_groups=mesh['zh'=4,'zl'=2,'x'=4,'yl'=2,'yh'=4,'core'=2] {'zh','yh'}, dimensions={0} | all-to-all | bytes 16384 | tf_op jit(solution)/shard_map/all_to_all | solution.py:366
  142.6 0.7 last.1
  (1 shorter events, 0.0 us)
Async XLA Ops:
  58.8 17.8 %collective-permute-start.1 = (bf16[64,32,128]{2,1,0:T(8,128)(2,1)S(1)}, bf16[64,32,128]{2,1,0:T(8,128)(2,1)S(1)}, u32[]{:S(2)}, u32[]{:S(2)}) collective-permute-start(bf16[64,32,128]{2,1,0:T(8,128)(2,1)S(1)} %all_to_all.26), channel_id=1, source_target_pairs={{0,48},{16,0},{32,16},{48,32},{1,49},{17,1},{33,17},{49,33},{2,50}... | collective-permute-start | bytes 1572872 | tf_op jit(solution)/shard_map/ppermute | solution.py:356
  63.2 13.4 %collective-permute-start = (bf16[64,32,128]{2,1,0:T(8,128)(2,1)S(1)}, bf16[64,32,128]{2,1,0:T(8,128)(2,1)S(1)}, u32[]{:S(2)}, u32[]{:S(2)}) collective-permute-start(bf16[64,32,128]{2,1,0:T(8,128)(2,1)S(1)} %all_to_all.26), channel_id=1, source_target_pairs={{0,16},{16,32},{32,48},{48,0},{1,17},{17,33},{33,49},{49,1},{2,18}... | collective-permute-start | bytes 1572872 | tf_op jit(solution)/shard_map/ppermute | solution.py:356
  65.1 37.8 %all-to-all-start.2 = ((bf16[256,16,128]{2,1,0:T(8,128)(2,1)}), bf16[256,16,128]{2,1,0:T(8,128)(2,1)S(1)}, u32[]{:S(2)}, u32[]{:S(2)}) async-start(bf16[256,16,128]{2,1,0:T(8,128)(2,1)} %get-tuple-element.14), calls=%async_computation.2 | async-start | bytes 2097152 | tf_op jit(solution)/shard_map/all_to_all | solution.py:359
  77.4 10.6 %collective-permute-start.2 = (bf16[32,32,128]{2,1,0:T(8,128)(2,1)}, bf16[32,32,128]{2,1,0:T(8,128)(2,1)S(1)}, u32[]{:S(2)}, u32[]{:S(2)}) collective-permute-start(bf16[32,32,128]{2,1,0:T(8,128)(2,1)} %get-tuple-element.12), channel_id=1, source_target_pairs={{0,48},{16,0},{32,16},{48,32},{1,49},{17,1},{33,17},{49,33},{2,50}... | collective-permute-start | bytes 786440 | tf_op jit(solution)/shard_map/ppermute | solution.py:358
  80.3 13.0 %collective-permute-start.3 = (bf16[32,32,128]{2,1,0:T(8,128)(2,1)S(1)}, bf16[32,32,128]{2,1,0:T(8,128)(2,1)S(1)}, u32[]{:S(2)}, u32[]{:S(2)}) collective-permute-start(bf16[32,32,128]{2,1,0:T(8,128)(2,1)S(1)} %get-tuple-element.13), channel_id=1, source_target_pairs={{0,16},{16,32},{32,48},{48,0},{1,17},{17,33},{33,49},{49,1},{2,18}... | collective-permute-start | bytes 786440 | tf_op jit(solution)/shard_map/ppermute | solution.py:358
  103.0 10.7 %copy-start = (f32[2048]{0:T(1024)S(1)}, f32[2048]{0:T(1024)}, u32[]{:S(2)}) copy-start(f32[2048]{0:T(1024)} %param.13) | copy-start | bytes 24580
  103.0 10.7 %copy-start.1 = (f32[8]{0:T(128)S(1)}, f32[8]{0:T(128)}, u32[]{:S(2)}) copy-start(f32[8]{0:T(128)} %eps_occ.1) | copy-start | bytes 100
  105.4 8.2 %collective-permute-start.4 = (f32[320,1024]{1,0:T(8,128)S(1)}, f32[320,1024]{1,0:T(8,128)S(1)}, u32[]{:S(2)}, u32[]{:S(2)}) collective-permute-start(f32[320,1024]{1,0:T(8,128)S(1)} %get-tuple-element.17), channel_id=1, source_target_pairs={{0,1},{1,0},{2,3},{3,2},{4,5},{5,4},{6,7},{7,6},{8,9},{9,8},{10,11... | collective-permute-start | bytes 3932168 | tf_op jit(solution)/shard_map/ppermute | solution.py:362

commit v9 on v8

--- a/solution.py
+++ b/solution.py
@@ -10,7 +10,6 @@
 SHELL = 64
 SHELLS = 12
 TILES = 16
-CHUNKS = 3
 AXES = ("zh", "zl", "x", "yl", "yh", "core")
 CHIPS = ("zh", "zl", "x", "yl", "yh")
 PAIR = ("zh", "zl", "x", "yl")
@@ -104,6 +103,25 @@
     )(blocks.T, screen, c_occ.T, ints)
 
 
+def hold_kernel(c_vir, out, sem):
+    copy = pltpu.make_async_copy(c_vir, out, sem)
+    copy.start()
+    copy.wait()
+
+
+def hold(c_vir):
+    return pl.pallas_call(
+        hold_kernel,
+        out_shape=jax.ShapeDtypeStruct(c_vir.shape, BF16),
+        in_specs=[HBM],
+        out_specs=VMEM,
+        scratch_shapes=[pltpu.SemaphoreType.DMA],
+        compiler_params=grant(50),
+        cost_estimate=pl.CostEstimate(flops=1 << 33, bytes_accessed=1 << 22, transcendentals=0),
+        name="hold",
+    )(c_vir)
+
+
 def rounded(x):
     return x.astype(BF16).astype(F32)
 
@@ -117,15 +135,7 @@
         sides[tile * 2 + 1] = jnp.where(left, pltpu.roll(one, SHELL, 1), two).astype(BF16)
 
 
-def transform_kernel(recv_at, c_vir, bmat, wide, thin, recv, held, terms, sides, total, sems):
-    arrive = pltpu.make_async_copy(recv_at, recv, sems.at[CHUNKS])
-    arrive.start()
-    copies = []
-    for m in range(CHUNKS):
-        part = pl.ds(m * 256, 256)
-        copies.append(pltpu.make_async_copy(c_vir.at[part], held.at[part], sems.at[m]))
-        copies[m].start()
-    arrive.wait()
+def transform_kernel(recv, c_vir, bmat, wide, thin, terms, sides):
     left = lanes((16, 128)) < SHELL
     sums = [jnp.zeros((16, 128), F32) for _ in range(SHELLS)]
     for source in range(8):
@@ -146,18 +156,10 @@
                 part = rounded(value)
                 terms[term * 32 + i * 16 : term * 32 + i * 16 + 16, m * 128 : m * 128 + 128] = part.astype(BF16)
                 value = value - part
-    for m in range(CHUNKS):
-        copies[m].wait()
-        some = terms[:, m * 256 : m * 256 + 256]
-        for q in range(TILES // 2):
-            columns = slice(q * 256, q * 256 + 256)
-            got = jnp.dot(some, held[m * 256 : m * 256 + 256, columns], preferred_element_type=F32)
-            if m < CHUNKS - 1:
-                total[:, columns] = got if m == 0 else total[:, columns] + got
-                continue
-            got = total[:, columns] + got
-            full = (got[64:96] + got[32:64]) + got[0:32]
-            finish(q, full, left, bmat, sides)
+    for q in range(TILES // 2):
+        got = jnp.dot(terms[...], c_vir[:, q * 256 : q * 256 + 256], preferred_element_type=F32)
+        full = (got[64:96] + got[32:64]) + got[0:32]
+        finish(q, full, left, bmat, sides)
     for r in range(TILES):
         for yh in range(4):
             wide[r * 4 + yh] = bmat[:, r * 128 : r * 128 + 128]
@@ -175,17 +177,10 @@
             jax.ShapeDtypeStruct((64, 32, 128), BF16),
             jax.ShapeDtypeStruct((256, 16, 128), BF16),
         ),
-        in_specs=[HBM, HBM],
+        in_specs=[VMEM, VMEM],
         out_specs=(VMEM, VMEM, VMEM),
-        scratch_shapes=[
-            pltpu.VMEM(recv.shape, F32),
-            pltpu.VMEM(c_vir.shape, BF16),
-            pltpu.VMEM((96, c_vir.shape[0]), BF16),
-            pltpu.VMEM((32, 16, 128), BF16),
-            pltpu.VMEM((96, c_vir.shape[1]), F32),
-            pltpu.SemaphoreType.DMA((CHUNKS + 1,)),
-        ],
-        compiler_params=grant(52),
+        scratch_shapes=[pltpu.VMEM((96, c_vir.shape[0]), BF16), pltpu.VMEM((32, 16, 128), BF16)],
+        compiler_params=grant(16),
         name="transform",
     )(recv, c_vir)
 
@@ -349,7 +344,7 @@
     place = position()
     sent = half_transform(c_occ, ints, blocks, screen)
     recv = lax.all_to_all(sent, GRP, 0, 0, tiled=True)
-    two, wide, thin = transform(recv, c_vir)
+    two, wide, thin = transform(recv, hold(c_vir))
     here = lax.all_to_all(wide, ("zh", "zl", "yl", "yh"), 0, 0, tiled=True)
     up = [(i, (i + 1) % 4) for i in range(4)]
     down = [(i, (i + 3) % 4) for i in range(4)]

time: 144 us -> 141 us (0.979)
  blocking collectives: 78.6 us -> 55.8 us
  starting transfers between devices: 28.6 us -> 39.3 us
  waiting for transfers between devices: 22.8 us -> 32 us
    all_to_all x1 -> x0, blocking collectives: 21.5 us -> none  [body(): recv = lax.all_to_all(sent, GRP, 0, 0, tiled=True)]
    all_to_all x0 -> x1, starting transfers between devices: none -> 10.2 us  [body(): recv = lax.all_to_all(sent, GRP, 0, 0, tiled=True)]
    all_to_all x0 -> x1, waiting for transfers between devices: none -> 9.32 us  [body(): recv = lax.all_to_all(sent, GRP, 0, 0, tiled=True)]
    pallas_call x1, Pallas kernels: 3.4 us -> 1.31 us  [transform(): pl.pallas_call(transform_kernel, out_shape=(jax.ShapeDtypeStruct((32, c_v...]
    pallas_call x0 -> x1, Pallas kernels: none -> 1.9 us  [hold(): pl.pallas_call(hold_kernel, out_shape=jax.ShapeDtypeStruct(c_vir.shape, B...]
  transfers between devices with their start and end apart: 6 -> 7, of which waited for: 4 -> 5; matrix products, arithmetic and copies ran while one was open for 0% -> 0% of each run, Pallas kernels for 1% -> 2%
where the time goes in v9:
time: 141 us
  blocking collectives  55.8 us (40%)
  starting transfers between devices  39.3 us (28%)
  waiting for transfers between devices  32 us (23%)
  Pallas kernels  12.2 us (9%)
    all_to_all x1, blocking collectives, body(): here = lax.all_to_all(wide, ('zh', 'zl', 'yl', 'yh'), 0, 0, tiled=True)  28.4 us
    all_to_all x1, blocking collectives, body(): lax.all_to_all(small(again_kernel, (16, 1, 128), 'again')(energy), FAR, 0...  14.6 us
    all_to_all x1, blocking collectives, body(): energy = lax.all_to_all(energy, NEAR, 0, 0, tiled=True)  12.8 us
    all_to_all x1, starting transfers between devices, body(): sides = lax.all_to_all(thin, CHIPS, 0, 0, tiled=True)  11.8 us
    ppermute x2, waiting for transfers between devices, body(): low, high = (lax.ppermute(low, 'x', down), lax.ppermute(high, 'x', up))  10.9 us
    all_to_all x1, starting transfers between devices, body(): recv = lax.all_to_all(sent, GRP, 0, 0, tiled=True)  10.2 us
    all_to_all x1, waiting for transfers between devices, body(): recv = lax.all_to_all(sent, GRP, 0, 0, tiled=True)  9.32 us
    all_to_all x1, waiting for transfers between devices, body(): sides = lax.all_to_all(thin, CHIPS, 0, 0, tiled=True)  9.1 us
  transfers between devices with their start and end apart: 7, of which 5 were waited for; matrix products, arithmetic and copies ran while one was open for 0% of the time, Pallas kernels for 2%

profile of v9, /device:TPU:1, one launch (start us, length us, event | category | flops | bytes accessed | tf_op | source)
XLA Modules:
  0.0 140.8 jit_solution(11016076587687974112)
XLA Ops:
  0.6 3.6 %half.1 = f32[8,72,128]{2,1,0:T(8,128)} custom-call(s32[2,4]{1,0:T(2,128)} %bitcast.25, s32[4]{0:T(128)} %screen_at.1, bf16[8,768]{1,0:T(8,128)(2,1)} %bitcast.24, bf16[4,32,4096]{2,1,0:T(8,128)(2,1)} %ints.1), custom_call_target="tpu_custom_call" | custom-call | tf_op jit(solution)/shard_map/half/pallas_call | solution.py:87
  4.2 10.2 %all-to-all-start = ((f32[8,72,128]{2,1,0:T(8,128)}), f32[8,72,128]{2,1,0:T(8,128)S(1)}, u32[]{:S(2)}, u32[]{:S(2)}) async-start(f32[8,72,128]{2,1,0:T(8,128)} %half.1), calls=%async_computation | async-start | bytes 589824 | tf_op jit(solution)/shard_map/all_to_all | solution.py:346
  14.4 1.9 %hold.1.c_vir = bf16[768,2048]{1,0:T(8,128)(2,1)S(1)} custom-call(bf16[768,2048]{1,0:T(8,128)(2,1)} %c_vir.1), custom_call_target="tpu_custom_call" | custom-call | flops 8589934592 | bytes 4194304 | tf_op jit(solution)/shard_map/hold/pallas_call | solution.py:113
  16.3 9.3 %all-to-all-done.recv = f32[8,72,128]{2,1,0:T(8,128)S(1)} async-done(((f32[8,72,128]{2,1,0:T(8,128)}), f32[8,72,128]{2,1,0:T(8,128)S(1)}, u32[]{:S(2)}, u32[]{:S(2)}) %all-to-all-start) | async-done | bytes 294944 | tf_op jit(solution)/shard_map/all_to_all | solution.py:346
  25.6 1.3 transform.1
  27.0 0.0 copy-start.1
  27.0 0.6 copy-done.1
  27.6 0.0 copy-start
  27.6 28.4 %all_to_all.25 = bf16[64,32,128]{2,1,0:T(8,128)(2,1)S(1)} all-to-all(bf16[64,32,128]{2,1,0:T(8,128)(2,1)S(1)} %get-tuple-element.11), channel_id=1, replica_groups=mesh['zh'=4,'zl'=2,'x'=4,'yl'=2,'yh'=4,'core'=2] {'zh','zl','yl','yh'}, dimensions={0} | all-to-all | bytes 1048576 | tf_op jit(solution)/shard_map/all_to_all | solution.py:348
  56.0 4.4 %collective-permute-start.1 = (bf16[64,32,128]{2,1,0:T(8,128)(2,1)S(1)}, bf16[64,32,128]{2,1,0:T(8,128)(2,1)S(1)}, u32[]{:S(2)}, u32[]{:S(2)}) collective-permute-start(bf16[64,32,128]{2,1,0:T(8,128)(2,1)S(1)} %all_to_all.25), channel_id=1, source_target_pairs={{0,48},{16,0},{32,16},{48,32},{1,49},{17,1},{33,17},{49,33},{2,50}... | collective-permute-start | bytes 1572872 | tf_op jit(solution)/shard_map/ppermute | solution.py:351
  60.4 1.9 %collective-permute-start = (bf16[64,32,128]{2,1,0:T(8,128)(2,1)S(1)}, bf16[64,32,128]{2,1,0:T(8,128)(2,1)S(1)}, u32[]{:S(2)}, u32[]{:S(2)}) collective-permute-start(bf16[64,32,128]{2,1,0:T(8,128)(2,1)S(1)} %all_to_all.25), channel_id=1, source_target_pairs={{0,16},{16,32},{32,48},{48,0},{1,17},{17,33},{33,49},{49,1},{2,18}... | collective-permute-start | bytes 1572872 | tf_op jit(solution)/shard_map/ppermute | solution.py:351
  62.3 0.0 copy-done
  62.3 11.8 %all-to-all-start.2 = ((bf16[256,16,128]{2,1,0:T(8,128)(2,1)}), bf16[256,16,128]{2,1,0:T(8,128)(2,1)S(1)}, u32[]{:S(2)}, u32[]{:S(2)}) async-start(bf16[256,16,128]{2,1,0:T(8,128)(2,1)} %copy-done), calls=%async_computation.2 | async-start | bytes 2097152 | tf_op jit(solution)/shard_map/all_to_all | solution.py:354
  74.2 0.0 copy-start.2
  74.2 0.0 collective-permute-done.1.above
  74.2 0.0 collective-permute-done.below
  74.2 0.8 onward.1
  74.9 2.8 %collective-permute-start.2 = (bf16[32,32,128]{2,1,0:T(8,128)(2,1)}, bf16[32,32,128]{2,1,0:T(8,128)(2,1)S(1)}, u32[]{:S(2)}, u32[]{:S(2)}) collective-permute-start(bf16[32,32,128]{2,1,0:T(8,128)(2,1)} %get-tuple-element.12), channel_id=1, source_target_pairs={{0,48},{16,0},{32,16},{48,32},{1,49},{17,1},{33,17},{49,33},{2,50}... | collective-permute-start | bytes 786440 | tf_op jit(solution)/shard_map/ppermute | solution.py:353
  77.8 2.4 %collective-permute-start.3 = (bf16[32,32,128]{2,1,0:T(8,128)(2,1)S(1)}, bf16[32,32,128]{2,1,0:T(8,128)(2,1)S(1)}, u32[]{:S(2)}, u32[]{:S(2)}) collective-permute-start(bf16[32,32,128]{2,1,0:T(8,128)(2,1)S(1)} %get-tuple-element.13), channel_id=1, source_target_pairs={{0,16},{16,32},{32,48},{48,0},{1,17},{17,33},{33,49},{49,1},{2,18}... | collective-permute-start | bytes 786440 | tf_op jit(solution)/shard_map/ppermute | solution.py:353
  80.2 0.1 stack.31.place
  80.3 5.7 %collective-permute-done.2 = bf16[32,32,128]{2,1,0:T(8,128)(2,1)S(1)} collective-permute-done((bf16[32,32,128]{2,1,0:T(8,128)(2,1)}, bf16[32,32,128]{2,1,0:T(8,128)(2,1)S(1)}, u32[]{:S(2)}, u32[]{:S(2)}) %collective-permute-start.2) | collective-permute-done | bytes 262176 | tf_op jit(solution)/shard_map/ppermute | solution.py:353
  86.0 5.2 %collective-permute-done.3 = bf16[32,32,128]{2,1,0:T(8,128)(2,1)S(1)} collective-permute-done((bf16[32,32,128]{2,1,0:T(8,128)(2,1)S(1)}, bf16[32,32,128]{2,1,0:T(8,128)(2,1)S(1)}, u32[]{:S(2)}, u32[]{:S(2)}) %collective-permute-start.3) | collective-permute-done | bytes 262176 | tf_op jit(solution)/shard_map/ppermute | solution.py:353
  91.2 9.1 %all-to-all-done.2 = bf16[256,16,128]{2,1,0:T(8,128)(2,1)S(1)} async-done(((bf16[256,16,128]{2,1,0:T(8,128)(2,1)}), bf16[256,16,128]{2,1,0:T(8,128)(2,1)S(1)}, u32[]{:S(2)}, u32[]{:S(2)}) %all-to-all-start.2) | async-done | bytes 1048608 | tf_op jit(solution)/shard_map/all_to_all | solution.py:354
  100.3 0.0 copy-done.2
  100.3 0.0 copy-start.3
  100.3 0.0 copy-start.4
  100.3 2.5 %gram.1 = (f32[288,1024]{1,0:T(8,128)S(1)}, f32[320,1024]{1,0:T(8,128)S(1)}) custom-call(s32[7]{0:T(128)S(1)} %stack.31.place, bf16[16,8,16,128]{3,2,1,0:T(8,128)(2,1)S(1)} %bitcast.18, bf16[16,8,16,128]{3,2,1,0:T(8,128)(2,1)S(1)} %bitcast.20, bf16[16,8,16,128]{3,2,1,0:T(8,128)(2,1)S(1)} %bitcast.19, bf16[8,8,16,128]{3,2,1,0:T(8,128)(2,1)S(1)} %bitcast.21, ...), custom_call_target="tpu_custom_call" | custom-call | tf_op jit(solution)/shard_map/gram/pallas_call | solution.py:238
  102.8 5.7 %collective-permute-start.4 = (f32[320,1024]{1,0:T(8,128)S(1)}, f32[320,1024]{1,0:T(8,128)S(1)}, u32[]{:S(2)}, u32[]{:S(2)}) collective-permute-start(f32[320,1024]{1,0:T(8,128)S(1)} %get-tuple-element.17), channel_id=1, source_target_pairs={{0,1},{1,0},{2,3},{3,2},{4,5},{5,4},{6,7},{7,6},{8,9},{9,8},{10,11... | collective-permute-start | bytes 3932168 | tf_op jit(solution)/shard_map/ppermute | solution.py:357
  108.5 2.6 %collective-permute-done.4.got = f32[320,1024]{1,0:T(8,128)S(1)} collective-permute-done((f32[320,1024]{1,0:T(8,128)S(1)}, f32[320,1024]{1,0:T(8,128)S(1)}, u32[]{:S(2)}, u32[]{:S(2)}) %collective-permute-start.4) | collective-permute-done | bytes 1310752 | tf_op jit(solution)/shard_map/ppermute | solution.py:357
  111.2 0.0 copy-done.3
  111.2 0.0 copy-done.4
  111.2 1.5 %energies.1 = (f32[32,1,128]{2,1,0:T(1,128)S(1)}, bf16[32,2048]{1,0:T(8,128)(2,1)}) custom-call(s32[7]{0:T(128)S(1)} %stack.31.place, f32[8]{0:T(128)S(1)} %copy-done.4, f32[288,1024]{1,0:T(8,128)S(1)} %get-tuple-element.16.keep, f32[320,1024]{1,0:T(8,128)S(1)} %collective-permute-done.4.got, f32[16,128]{1,0:T(8,128)S(1)} %bitcast.23, ...), custom_call_target="tpu_custom_call" | custom-call | tf_op jit(solution)/shard_map/energies/pallas_call | solution.py:300
  112.7 12.8 %all_to_all.26.got = f32[32,1,128]{2,1,0:T(1,128)S(1)} all-to-all(f32[32,1,128]{2,1,0:T(1,128)S(1)} %get-tuple-element.19), channel_id=1, replica_groups=mesh['zh'=4,'zl'=2,'x'=4,'yl'=2,'yh'=4,'core'=2] {'zl','x','yl','core'}, dimensions={0} | all-to-all | bytes 32768 | tf_op jit(solution)/shard_map/all_to_all | solution.py:360
  125.5 14.6 %all_to_all.27.got = f32[16,1,128]{2,1,0:T(1,128)S(1)} all-to-all(f32[16,1,128]{2,1,0:T(1,128)S(1)} %again.1), channel_id=1, replica_groups=mesh['zh'=4,'zl'=2,'x'=4,'yl'=2,'yh'=4,'core'=2] {'zh','yh'}, dimensions={0} | all-to-all | bytes 16384 | tf_op jit(solution)/shard_map/all_to_all | solution.py:361
  140.1 0.7 last.1
  (1 shorter events, 0.0 us)
Async XLA Ops:
  4.2 21.4 %all-to-all-start = ((f32[8,72,128]{2,1,0:T(8,128)}), f32[8,72,128]{2,1,0:T(8,128)S(1)}, u32[]{:S(2)}, u32[]{:S(2)}) async-start(f32[8,72,128]{2,1,0:T(8,128)} %half.1), calls=%async_computation | async-start | bytes 589824 | tf_op jit(solution)/shard_map/all_to_all | solution.py:346
  27.0 0.7 copy-start.1
  27.6 34.7 %copy-start = (bf16[256,16,128]{2,1,0:T(8,128)(2,1)}, bf16[256,16,128]{2,1,0:T(8,128)(2,1)S(1)}, u32[]{:S(2)}) copy-start(bf16[256,16,128]{2,1,0:T(8,128)(2,1)S(1)} %get-tuple-element.14) | copy-start | bytes 3145732
  56.0 18.2 %collective-permute-start.1 = (bf16[64,32,128]{2,1,0:T(8,128)(2,1)S(1)}, bf16[64,32,128]{2,1,0:T(8,128)(2,1)S(1)}, u32[]{:S(2)}, u32[]{:S(2)}) collective-permute-start(bf16[64,32,128]{2,1,0:T(8,128)(2,1)S(1)} %all_to_all.25), channel_id=1, source_target_pairs={{0,48},{16,0},{32,16},{48,32},{1,49},{17,1},{33,17},{49,33},{2,50}... | collective-permute-start | bytes 1572872 | tf_op jit(solution)/shard_map/ppermute | solution.py:351
  60.4 13.8 %collective-permute-start = (bf16[64,32,128]{2,1,0:T(8,128)(2,1)S(1)}, bf16[64,32,128]{2,1,0:T(8,128)(2,1)S(1)}, u32[]{:S(2)}, u32[]{:S(2)}) collective-permute-start(bf16[64,32,128]{2,1,0:T(8,128)(2,1)S(1)} %all_to_all.25), channel_id=1, source_target_pairs={{0,16},{16,32},{32,48},{48,0},{1,17},{17,33},{33,49},{49,1},{2,18}... | collective-permute-start | bytes 1572872 | tf_op jit(solution)/shard_map/ppermute | solution.py:351
  62.3 38.0 %all-to-all-start.2 = ((bf16[256,16,128]{2,1,0:T(8,128)(2,1)}), bf16[256,16,128]{2,1,0:T(8,128)(2,1)S(1)}, u32[]{:S(2)}, u32[]{:S(2)}) async-start(bf16[256,16,128]{2,1,0:T(8,128)(2,1)} %copy-done), calls=%async_computation.2 | async-start | bytes 2097152 | tf_op jit(solution)/shard_map/all_to_all | solution.py:354
  74.2 26.2 %copy-start.2 = (bf16[32,2048]{1,0:T(8,128)(2,1)S(1)}, bf16[32,2048]{1,0:T(8,128)(2,1)}, u32[]{:S(2)}) copy-start(bf16[32,2048]{1,0:T(8,128)(2,1)} %copy-done.1) | copy-start | bytes 393220
  74.9 11.1 %collective-permute-start.2 = (bf16[32,32,128]{2,1,0:T(8,128)(2,1)}, bf16[32,32,128]{2,1,0:T(8,128)(2,1)S(1)}, u32[]{:S(2)}, u32[]{:S(2)}) collective-permute-start(bf16[32,32,128]{2,1,0:T(8,128)(2,1)} %get-tuple-element.12), channel_id=1, source_target_pairs={{0,48},{16,0},{32,16},{48,32},{1,49},{17,1},{33,17},{49,33},{2,50}... | collective-permute-start | bytes 786440 | tf_op jit(solution)/shard_map/ppermute | solution.py:353
  77.8 13.4 %collective-permute-start.3 = (bf16[32,32,128]{2,1,0:T(8,128)(2,1)S(1)}, bf16[32,32,128]{2,1,0:T(8,128)(2,1)S(1)}, u32[]{:S(2)}, u32[]{:S(2)}) collective-permute-start(bf16[32,32,128]{2,1,0:T(8,128)(2,1)S(1)} %get-tuple-element.13), channel_id=1, source_target_pairs={{0,16},{16,32},{32,48},{48,0},{1,17},{17,33},{33,49},{49,1},{2,18}... | collective-permute-start | bytes 786440 | tf_op jit(solution)/shard_map/ppermute | solution.py:353
  100.3 10.8 %copy-start.3 = (f32[2048]{0:T(1024)S(1)}, f32[2048]{0:T(1024)}, u32[]{:S(2)}) copy-start(f32[2048]{0:T(1024)} %param.13) | copy-start | bytes 24580
  100.3 10.8 %copy-start.4 = (f32[8]{0:T(128)S(1)}, f32[8]{0:T(128)}, u32[]{:S(2)}) copy-start(f32[8]{0:T(128)} %eps_occ.1) | copy-start | bytes 100
  102.8 8.4 %collective-permute-start.4 = (f32[320,1024]{1,0:T(8,128)S(1)}, f32[320,1024]{1,0:T(8,128)S(1)}, u32[]{:S(2)}, u32[]{:S(2)}) collective-permute-start(f32[320,1024]{1,0:T(8,128)S(1)} %get-tuple-element.17), channel_id=1, source_target_pairs={{0,1},{1,0},{2,3},{3,2},{4,5},{5,4},{6,7},{7,6},{8,9},{9,8},{10,11... | collective-permute-start | bytes 3932168 | tf_op jit(solution)/shard_map/ppermute | solution.py:357

commit v10 on v9

--- a/solution.py
+++ b/solution.py
@@ -203,8 +203,82 @@
     )(below, above)
 
 
-def gram_kernel(place, here, below, above, low, high, sides, two, keep, give, wide, thin, all_t, all_s):
-    core, side, own, x = place[4], place[3], place[5], place[6]
+def panel_kernel(place, here, below, above, low, high, two, keep, give, wide, all_s):
+    core, side, own = place[4], place[3], place[5]
+    first = 0
+    for tiles in (here, below, above, low, high):
+        count = tiles.shape[0] * 16
+        for i in range(8):
+            wide[first : first + count, i * 128 : i * 128 + 128] = tiles[:, i].reshape(count, 128)
+        first += count
+    mine = wide[:, pl.ds(pl.multiple_of(own * 128, 128), 128)]
+    others = wide[:, pl.ds(pl.multiple_of(side * 512, 512), 512)]
+    all_s[...] = lax.dot_general(mine, others, TRANSPOSED, preferred_element_type=F32)
+    for which, target in ((core, keep), (1 - core, give)):
+        at = pl.multiple_of(which * 256, 256)
+        for q in range(4):
+            target[0:32, q * 256 : q * 256 + 256] = all_s[q * 32 : q * 32 + 32, pl.ds(at, 256)]
+    at = pl.multiple_of((1 - core) * 16, 16)
+    for q in range(2):
+        give[32 + q * 16 : 48 + q * 16, :] = two[pl.ds(at, 16), q * 1024 : q * 1024 + 1024].astype(F32)
+
+
+def panel(place, blocks, two):
+    tiles = (block.reshape(-1, 8, 16, 128) for block in blocks)
+    return pl.pallas_call(
+        panel_kernel,
+        out_shape=(
+            jax.ShapeDtypeStruct((32, 1024), F32),
+            jax.ShapeDtypeStruct((64, 1024), F32),
+        ),
+        in_specs=[SMEM] + [VMEM] * 6,
+        out_specs=(VMEM, VMEM),
+        scratch_shapes=[pltpu.VMEM((1024, 1024), BF16), pltpu.VMEM((128, 512), F32)],
+        compiler_params=grant(8),
+        cost_estimate=pl.CostEstimate(flops=1 << 29, bytes_accessed=1 << 22, transcendentals=0),
+        name="panel",
+    )(place, *tiles, two)
+
+
+def settle_kernel(place, eps_occ, keep, got, eps_vir, mine, out, bmat):
+    tile, side, core, own = (place[n] for n in (0, 3, 4, 5))
+    row_a = eps_vir[pl.ds(tile, 1), :]
+    square = (128, 128)
+    col_a = jnp.sum(jnp.where(lanes(square) == rows(square), row_a, 0.0), axis=1, keepdims=True)
+    for m in range(2):
+        j = side * 4 + core * 2 + m
+        block = jnp.concatenate(
+            [
+                keep[0:32, q * 256 + m * 128 : q * 256 + m * 128 + 128]
+                + got[0:32, q * 256 + m * 128 : q * 256 + m * 128 + 128]
+                for q in range(4)
+            ],
+            axis=0,
+        )
+        denominators = (eps_occ[own] + eps_occ[j] - row_a) - col_a
+        terms = block * (2.0 * block - block.T) / denominators
+        out[m : m + 1, :] = jnp.sum(terms, axis=0, keepdims=True)
+    here = pl.ds(pl.multiple_of(core * 16, 16), 16)
+    bmat[here, :] = mine[here, :]
+    there = pl.ds(pl.multiple_of((1 - core) * 16, 16), 16)
+    for q in range(2):
+        bmat[there, q * 1024 : q * 1024 + 1024] = got[32 + q * 16 : 48 + q * 16, :].astype(BF16)
+
+
+def settle(place, eps_occ, keep, got, eps_vir, two):
+    return pl.pallas_call(
+        settle_kernel,
+        out_shape=(jax.ShapeDtypeStruct((8, 128), F32), jax.ShapeDtypeStruct(two.shape, BF16)),
+        in_specs=[SMEM, SMEM, VMEM, VMEM, VMEM, VMEM],
+        out_specs=(VMEM, VMEM),
+        compiler_params=grant(4),
+        cost_estimate=pl.CostEstimate(flops=1 << 28, bytes_accessed=1 << 20, transcendentals=0),
+        name="settle",
+    )(place, eps_occ, keep, got, eps_vir.reshape(-1, 128), two)
+
+
+def gram_kernel(place, here, below, above, low, high, sides, _, keep, give, wide, thin, all_t):
+    core, x = place[4], place[6]
     first = 0
     for away, tiles in ((0, here), (3, below), (1, above), (2, low), (2, high)):
         count = tiles.shape[0] * 16
@@ -218,40 +292,31 @@
     for p in range(4):
         part = lax.dot_general(thin[:, p * 128 : p * 128 + 128], wide[...], TRANSPOSED, preferred_element_type=F32)
         all_t[p * 128 : p * 128 + 128, :] = part
-    mine = wide[:, pl.ds(pl.multiple_of(own * 128, 128), 128)]
-    others = wide[:, pl.ds(pl.multiple_of(side * 512, 512), 512)]
-    all_s[...] = lax.dot_general(mine, others, TRANSPOSED, preferred_element_type=F32)
     for which, target in ((core, keep), (1 - core, give)):
         for j in range(8):
             at = pl.multiple_of(j * 64 + which * 32, 32)
             target[j * 32 : j * 32 + 32, :] = all_t[pl.ds(at, 32), :]
-        for q in range(4):
-            at = pl.multiple_of(which * 256, 256)
-            target[256:288, q * 256 : q * 256 + 256] = all_s[q * 32 : q * 32 + 32, pl.ds(at, 256)]
-    at = pl.multiple_of((1 - core) * 16, 16)
-    for q in range(2):
-        give[288 + q * 16 : 304 + q * 16, :] = two[pl.ds(at, 16), q * 1024 : q * 1024 + 1024].astype(F32)
-
-
-def gram(place, here, below, above, low, high, sides, two):
-    tiles = (block.reshape(-1, 8, 16, 128) for block in (here, below, above, low, high))
+
+
+def gram(place, blocks, sides, after):
+    tiles = (block.reshape(-1, 8, 16, 128) for block in blocks)
+    shape = jax.ShapeDtypeStruct((256, 1024), F32)
     return pl.pallas_call(
         gram_kernel,
-        out_shape=(jax.ShapeDtypeStruct((288, 1024), F32), jax.ShapeDtypeStruct((320, 1024), F32)),
-        in_specs=[SMEM] + [VMEM] * 7,
+        out_shape=(shape, shape),
+        in_specs=[SMEM] + [VMEM] * 6 + [HBM],
         out_specs=(VMEM, VMEM),
         scratch_shapes=[
             pltpu.VMEM((1024, 1024), BF16),
             pltpu.VMEM((1024, 512), BF16),
             pltpu.VMEM((512, 1024), F32),
-            pltpu.VMEM((128, 512), F32),
         ],
         compiler_params=grant(16),
         name="gram",
-    )(place, *tiles, sides.reshape(8, 4, 2, 4, 16, 128), two)
-
-
-def energy_kernel(scale, place, eps_occ, keep, got, eps_vir, mine, out, bmat, parts):
+    )(place, *tiles, sides.reshape(8, 4, 2, 4, 16, 128), after)
+
+
+def energy_kernel(scale, place, eps_occ, keep, got, eps_vir, selfs, out, parts):
     tile, other, step, side, core, own = (place[n] for n in range(6))
     row_a = eps_vir[pl.ds(tile, 1), :]
     row_b = eps_vir[pl.ds(other, 1), :]
@@ -269,43 +334,24 @@
             part = jnp.sum(terms, axis=0, keepdims=True) * weight
             parts[i * 8 + j : i * 8 + j + 1, :] = part
             parts[j * 8 + i : j * 8 + i + 1, :] = part
-    square = (128, 128)
-    eye = lanes(square) == rows(square)
-    col_a = jnp.sum(jnp.where(eye, row_a, 0.0), axis=1, keepdims=True)
     for m in range(2):
-        j = side * 4 + core * 2 + m
-        block = jnp.concatenate(
-            [
-                keep[256:288, q * 256 + m * 128 : q * 256 + m * 128 + 128]
-                + got[256:288, q * 256 + m * 128 : q * 256 + m * 128 + 128]
-                for q in range(4)
-            ],
-            axis=0,
-        )
-        denominators = (eps_occ[own] + eps_occ[j] - row_a) - col_a
-        terms = block * (2.0 * block - block.T) / denominators
-        at = pl.ds(own * 8 + j, 1)
-        parts[at, :] = parts[at, :] + jnp.sum(terms, axis=0, keepdims=True)
+        at = pl.ds(own * 8 + side * 4 + core * 2 + m, 1)
+        parts[at, :] = parts[at, :] + selfs[m : m + 1, :]
     column = jnp.sum(parts[...], axis=1, keepdims=True) * scale
     row = jnp.sum(jnp.where(lanes((64, 128)) == rows((64, 128)), column, 0.0), axis=0, keepdims=True)
     out[...] = jnp.broadcast_to(row[None], out.shape)
-    here = pl.ds(pl.multiple_of(core * 16, 16), 16)
-    bmat[here, :] = mine[here, :]
-    there = pl.ds(pl.multiple_of((1 - core) * 16, 16), 16)
-    for q in range(2):
-        bmat[there, q * 1024 : q * 1024 + 1024] = got[288 + q * 16 : 304 + q * 16, :].astype(BF16)
-
-
-def energies(scale, place, eps_occ, keep, got, eps_vir, two):
+
+
+def energies(scale, place, eps_occ, keep, got, eps_vir, selfs):
     return pl.pallas_call(
         functools.partial(energy_kernel, scale),
-        out_shape=(jax.ShapeDtypeStruct((32, 1, 128), F32), jax.ShapeDtypeStruct(two.shape, BF16)),
+        out_shape=jax.ShapeDtypeStruct((32, 1, 128), F32),
         in_specs=[SMEM, SMEM, VMEM, VMEM, VMEM, VMEM],
-        out_specs=(VMEM, VMEM),
+        out_specs=VMEM,
         scratch_shapes=[pltpu.VMEM((64, 128), F32)],
-        compiler_params=grant(8),
+        compiler_params=grant(6),
         name="energies",
-    )(place, eps_occ, keep, got, eps_vir.reshape(-1, 128), two)
+    )(place, eps_occ, keep, got, eps_vir.reshape(-1, 128), selfs)
 
 
 def position():
@@ -353,10 +399,14 @@
     low, high = lax.ppermute(low, "x", down), lax.ppermute(high, "x", up)
     sides = lax.all_to_all(thin, CHIPS, 0, 0, tiled=True)
 
-    keep, give = gram(place, here, below, above, low, high, sides, two)
-    got = lax.ppermute(give, "core", [(0, 1), (1, 0)])
+    swap = [(0, 1), (1, 0)]
+    blocks = (here, below, above, low, high)
+    keep, give = panel(place, blocks, two)
+    selfs, bmat = settle(place, eps_occ, keep, lax.ppermute(give, "core", swap), eps_vir, two)
+    keep, give = gram(place, blocks, sides, selfs)
+    got = lax.ppermute(give, "core", swap)
     scale = 1.0 / (float(vir) * float(vir) * 2048.0)
-    energy, bmat = energies(scale, place, eps_occ, keep, got, eps_vir, two)
+    energy = energies(scale, place, eps_occ, keep, got, eps_vir, selfs)
     energy = lax.all_to_all(energy, NEAR, 0, 0, tiled=True)
     energy = lax.all_to_all(small(again_kernel, (16, 1, 128), "again")(energy), FAR, 0, 0, tiled=True)
     energy = small(last_kernel, (occ, occ), "last")(energy)

time: 141 us -> 142 us (level)
  waiting for transfers between devices: 32 us -> 23.1 us
  starting transfers between devices: 39.3 us -> 44 us
  blocking collectives: 55.8 us -> 58.3 us
  Pallas kernels: 12.2 us -> 14.4 us
    all_to_all x1, waiting for transfers between devices: 9.1 us -> 0.01 us  [body(): sides = lax.all_to_all(thin, CHIPS, 0, 0, tiled=True)]
    ppermute x1 -> x2, starting transfers between devices: 5.73 us -> 11.3 us  [the longest x1 5.77 us: body(): got = lax.ppermute(give, 'core', swap)]
    all_to_all x1, blocking collectives: 14.6 us -> 17.1 us  [body(): lax.all_to_all(small(again_kernel, (16, 1, 128), 'again')(energy), FAR, 0...]
    pallas_call x2 -> x4, Pallas kernels: 3.98 us -> 6.04 us  [the longest x1 2.4 us: gram(): pl.pallas_call(gram_kernel, out_shape=(shape, shape), in_specs=[SMEM] + [...]
    ppermute x1 -> x2, waiting for transfers between devices: 2.64 us -> 3.4 us  [the longest x1 2.26 us: body(): got = lax.ppermute(give, 'core', swap)]
  transfers between devices with their start and end apart: 7 -> 8, of which waited for: 5 -> 5; matrix products, arithmetic and copies ran while one was open for 0% -> 0% of each run, Pallas kernels for 2% -> 4%
where the time goes in v10:
time: 142 us; the launch traced here: 141 us
  blocking collectives  58.3 us (41%)
  starting transfers between devices  44 us (31%)
  waiting for transfers between devices  23.1 us (16%)
  Pallas kernels  14.4 us (10%)
    all_to_all x1, blocking collectives, body(): here = lax.all_to_all(wide, ('zh', 'zl', 'yl', 'yh'), 0, 0, tiled=True)  28.4 us
    all_to_all x1, blocking collectives, body(): lax.all_to_all(small(again_kernel, (16, 1, 128), 'again')(energy), FAR, 0...  17.1 us
    all_to_all x1, blocking collectives, body(): energy = lax.all_to_all(energy, NEAR, 0, 0, tiled=True)  12.8 us
    all_to_all x1, starting transfers between devices, body(): sides = lax.all_to_all(thin, CHIPS, 0, 0, tiled=True)  10.7 us
    ppermute x2, waiting for transfers between devices, body(): low, high = (lax.ppermute(low, 'x', down), lax.ppermute(high, 'x', up))  10.4 us
    all_to_all x1, starting transfers between devices, body(): recv = lax.all_to_all(sent, GRP, 0, 0, tiled=True)  10.2 us
    all_to_all x1, waiting for transfers between devices, body(): recv = lax.all_to_all(sent, GRP, 0, 0, tiled=True)  9.32 us
    ppermute x2, starting transfers between devices, body(): below, above = (lax.ppermute(here, 'x', up), lax.ppermute(here, 'x', down))  6.48 us
  transfers between devices with their start and end apart: 8, of which 5 were waited for; matrix products, arithmetic and copies ran while one was open for 0% of the time, Pallas kernels for 4%

profile of v10, /device:TPU:1, one launch (start us, length us, event | category | flops | bytes accessed | tf_op | source)
XLA Modules:
  0.0 141.4 jit_solution(6583822519297089397)
XLA Ops:
  0.6 3.6 %half.1 = f32[8,72,128]{2,1,0:T(8,128)} custom-call(s32[2,4]{1,0:T(2,128)} %bitcast.31, s32[4]{0:T(128)} %screen_at.1, bf16[8,768]{1,0:T(8,128)(2,1)} %bitcast.30, bf16[4,32,4096]{2,1,0:T(8,128)(2,1)} %ints.1), custom_call_target="tpu_custom_call" | custom-call | tf_op jit(solution)/shard_map/half/pallas_call | solution.py:87
  4.2 10.2 %all-to-all-start = ((f32[8,72,128]{2,1,0:T(8,128)}), f32[8,72,128]{2,1,0:T(8,128)S(1)}, u32[]{:S(2)}, u32[]{:S(2)}) async-start(f32[8,72,128]{2,1,0:T(8,128)} %half.1), calls=%async_computation | async-start | bytes 589824 | tf_op jit(solution)/shard_map/all_to_all | solution.py:392
  14.4 1.9 %hold.1.c_vir = bf16[768,2048]{1,0:T(8,128)(2,1)S(1)} custom-call(bf16[768,2048]{1,0:T(8,128)(2,1)} %c_vir.1), custom_call_target="tpu_custom_call" | custom-call | flops 8589934592 | bytes 4194304 | tf_op jit(solution)/shard_map/hold/pallas_call | solution.py:113
  16.3 9.3 %all-to-all-done.recv = f32[8,72,128]{2,1,0:T(8,128)S(1)} async-done(((f32[8,72,128]{2,1,0:T(8,128)}), f32[8,72,128]{2,1,0:T(8,128)S(1)}, u32[]{:S(2)}, u32[]{:S(2)}) %all-to-all-start) | async-done | bytes 294944 | tf_op jit(solution)/shard_map/all_to_all | solution.py:392
  25.6 1.3 transform.1
  27.0 0.0 copy-start.1
  27.0 0.6 copy-done.1
  27.6 0.0 copy-start
  27.6 28.4 %all_to_all.25 = bf16[64,32,128]{2,1,0:T(8,128)(2,1)S(1)} all-to-all(bf16[64,32,128]{2,1,0:T(8,128)(2,1)S(1)} %get-tuple-element.13), channel_id=1, replica_groups=mesh['zh'=4,'zl'=2,'x'=4,'yl'=2,'yh'=4,'core'=2] {'zh','zl','yl','yh'}, dimensions={0} | all-to-all | bytes 1048576 | tf_op jit(solution)/shard_map/all_to_all | solution.py:394
  56.0 3.1 %collective-permute-start = (bf16[64,32,128]{2,1,0:T(8,128)(2,1)S(1)}, bf16[64,32,128]{2,1,0:T(8,128)(2,1)S(1)}, u32[]{:S(2)}, u32[]{:S(2)}) collective-permute-start(bf16[64,32,128]{2,1,0:T(8,128)(2,1)S(1)} %all_to_all.25), channel_id=1, source_target_pairs={{0,16},{16,32},{32,48},{48,0},{1,17},{17,33},{33,49},{49,1},{2,18}... | collective-permute-start | bytes 1572872 | tf_op jit(solution)/shard_map/ppermute | solution.py:397
  59.1 3.4 %collective-permute-start.1 = (bf16[64,32,128]{2,1,0:T(8,128)(2,1)S(1)}, bf16[64,32,128]{2,1,0:T(8,128)(2,1)S(1)}, u32[]{:S(2)}, u32[]{:S(2)}) collective-permute-start(bf16[64,32,128]{2,1,0:T(8,128)(2,1)S(1)} %all_to_all.25), channel_id=1, source_target_pairs={{0,48},{16,0},{32,16},{48,32},{1,49},{17,1},{33,17},{49,33},{2,50}... | collective-permute-start | bytes 1572872 | tf_op jit(solution)/shard_map/ppermute | solution.py:397
  62.5 0.0 copy-done
  62.5 10.7 %all-to-all-start.2 = ((bf16[256,16,128]{2,1,0:T(8,128)(2,1)}), bf16[256,16,128]{2,1,0:T(8,128)(2,1)S(1)}, u32[]{:S(2)}, u32[]{:S(2)}) async-start(bf16[256,16,128]{2,1,0:T(8,128)(2,1)} %copy-done), calls=%async_computation.2 | async-start | bytes 2097152 | tf_op jit(solution)/shard_map/all_to_all | solution.py:400
  73.2 0.0 copy-start.2
  73.2 0.0 copy-start.3
  73.2 0.0 copy-start.4
  73.2 0.0 collective-permute-done.below
  73.3 0.0 collective-permute-done.1.above
  73.3 0.9 onward.1
  74.1 2.8 %collective-permute-start.2 = (bf16[32,32,128]{2,1,0:T(8,128)(2,1)}, bf16[32,32,128]{2,1,0:T(8,128)(2,1)S(1)}, u32[]{:S(2)}, u32[]{:S(2)}) collective-permute-start(bf16[32,32,128]{2,1,0:T(8,128)(2,1)} %get-tuple-element.14), channel_id=1, source_target_pairs={{0,48},{16,0},{32,16},{48,32},{1,49},{17,1},{33,17},{49,33},{2,50}... | collective-permute-start | bytes 786440 | tf_op jit(solution)/shard_map/ppermute | solution.py:399
  77.0 2.4 %collective-permute-start.3 = (bf16[32,32,128]{2,1,0:T(8,128)(2,1)}, bf16[32,32,128]{2,1,0:T(8,128)(2,1)S(1)}, u32[]{:S(2)}, u32[]{:S(2)}) collective-permute-start(bf16[32,32,128]{2,1,0:T(8,128)(2,1)} %get-tuple-element.15), channel_id=1, source_target_pairs={{0,16},{16,32},{32,48},{48,0},{1,17},{17,33},{33,49},{49,1},{2,18}... | collective-permute-start | bytes 786440 | tf_op jit(solution)/shard_map/ppermute | solution.py:399
  79.4 0.1 stack.31.place
  79.5 6.9 %collective-permute-done.2 = bf16[32,32,128]{2,1,0:T(8,128)(2,1)S(1)} collective-permute-done((bf16[32,32,128]{2,1,0:T(8,128)(2,1)}, bf16[32,32,128]{2,1,0:T(8,128)(2,1)S(1)}, u32[]{:S(2)}, u32[]{:S(2)}) %collective-permute-start.2) | collective-permute-done | bytes 262176 | tf_op jit(solution)/shard_map/ppermute | solution.py:399
  86.4 3.5 %collective-permute-done.3 = bf16[32,32,128]{2,1,0:T(8,128)(2,1)S(1)} collective-permute-done((bf16[32,32,128]{2,1,0:T(8,128)(2,1)}, bf16[32,32,128]{2,1,0:T(8,128)(2,1)S(1)}, u32[]{:S(2)}, u32[]{:S(2)}) %collective-permute-start.3) | collective-permute-done | bytes 262176 | tf_op jit(solution)/shard_map/ppermute | solution.py:399
  89.9 0.0 copy-done.2
  89.9 1.5 %panel.1 = (f32[32,1024]{1,0:T(8,128)S(1)}, f32[64,1024]{1,0:T(8,128)S(1)}) custom-call(s32[7]{0:T(128)S(1)} %stack.31.place, bf16[16,8,16,128]{3,2,1,0:T(8,128)(2,1)S(1)} %bitcast.17, bf16[16,8,16,128]{3,2,1,0:T(8,128)(2,1)S(1)} %bitcast.20, bf16[16,8,16,128]{3,2,1,0:T(8,128)(2,1)S(1)} %bitcast.22, bf16[8,8,16,128]{3,2,1,0:T(8,128)(2,1)S(1)} %bitcast.24, ...), custom_call_target="tpu_custom_call" | custom-call | flops 536870912 | bytes 4194304 | tf_op jit(solution)/shard_map/panel/pallas_call | solution.py:228
  91.4 5.6 %collective-permute-start.4 = (f32[64,1024]{1,0:T(8,128)S(1)}, f32[64,1024]{1,0:T(8,128)S(1)}, u32[]{:S(2)}, u32[]{:S(2)}) collective-permute-start(f32[64,1024]{1,0:T(8,128)S(1)} %get-tuple-element.18), channel_id=1, source_target_pairs={{0,1},{1,0},{2,3},{3,2},{4,5},{5,4},{6,7},{7,6},{8,9},{9,8},{10,11... | collective-permute-start | bytes 786440 | tf_op jit(solution)/shard_map/ppermute | solution.py:405
  97.0 1.1 collective-permute-done.4.got
  98.1 0.0 copy-done.3
  98.1 0.0 copy-done.4
  98.1 1.2 settle.1
  99.3 0.0 all-to-all-done.2
  99.3 2.4 %gram.1 = (f32[256,1024]{1,0:T(8,128)S(1)}, f32[256,1024]{1,0:T(8,128)S(1)}) custom-call(s32[7]{0:T(128)S(1)} %stack.31.place, bf16[16,8,16,128]{3,2,1,0:T(8,128)(2,1)S(1)} %bitcast.18, bf16[16,8,16,128]{3,2,1,0:T(8,128)(2,1)S(1)} %bitcast.21, bf16[16,8,16,128]{3,2,1,0:T(8,128)(2,1)S(1)} %bitcast.23, bf16[8,8,16,128]{3,2,1,0:T(8,128)(2,1)S(1)} %bitcast.25, ...), custom_call_target="tpu_custom_call" | custom-call | tf_op jit(solution)/shard_map/gram/pallas_call | solution.py:304
  101.7 5.8 %collective-permute-start.5 = (f32[256,1024]{1,0:T(8,128)S(1)}, f32[256,1024]{1,0:T(8,128)S(1)}, u32[]{:S(2)}, u32[]{:S(2)}) collective-permute-start(f32[256,1024]{1,0:T(8,128)S(1)} %get-tuple-element.23), channel_id=1, source_target_pairs={{0,1},{1,0},{2,3},{3,2},{4,5},{5,4},{6,7},{7,6},{8,9},{9,8},{10,11... | collective-permute-start | bytes 3145736 | tf_op jit(solution)/shard_map/ppermute | solution.py:407
  107.5 2.3 %collective-permute-done.5.got = f32[256,1024]{1,0:T(8,128)S(1)} collective-permute-done((f32[256,1024]{1,0:T(8,128)S(1)}, f32[256,1024]{1,0:T(8,128)S(1)}, u32[]{:S(2)}, u32[]{:S(2)}) %collective-permute-start.5) | collective-permute-done | bytes 1048608 | tf_op jit(solution)/shard_map/ppermute | solution.py:407
  109.8 0.9 energies.1
  110.7 12.8 %all_to_all.26.got = f32[32,1,128]{2,1,0:T(1,128)S(1)} all-to-all(f32[32,1,128]{2,1,0:T(1,128)S(1)} %energies.1), channel_id=1, replica_groups=mesh['zh'=4,'zl'=2,'x'=4,'yl'=2,'yh'=4,'core'=2] {'zl','x','yl','core'}, dimensions={0} | all-to-all | bytes 32768 | tf_op jit(solution)/shard_map/all_to_all | solution.py:410
  123.6 17.1 %all_to_all.27.got = f32[16,1,128]{2,1,0:T(1,128)S(1)} all-to-all(f32[16,1,128]{2,1,0:T(1,128)S(1)} %again.1), channel_id=1, replica_groups=mesh['zh'=4,'zl'=2,'x'=4,'yl'=2,'yh'=4,'core'=2] {'zh','yh'}, dimensions={0} | all-to-all | bytes 16384 | tf_op jit(solution)/shard_map/all_to_all | solution.py:411
  140.7 0.7 last.1
  (1 shorter events, 0.0 us)
Async XLA Ops:
  4.2 21.4 %all-to-all-start = ((f32[8,72,128]{2,1,0:T(8,128)}), f32[8,72,128]{2,1,0:T(8,128)S(1)}, u32[]{:S(2)}, u32[]{:S(2)}) async-start(f32[8,72,128]{2,1,0:T(8,128)} %half.1), calls=%async_computation | async-start | bytes 589824 | tf_op jit(solution)/shard_map/all_to_all | solution.py:392
  27.0 0.7 copy-start.1
  27.6 34.9 %copy-start = (bf16[256,16,128]{2,1,0:T(8,128)(2,1)}, bf16[256,16,128]{2,1,0:T(8,128)(2,1)S(1)}, u32[]{:S(2)}) copy-start(bf16[256,16,128]{2,1,0:T(8,128)(2,1)S(1)} %get-tuple-element.20) | copy-start | bytes 3145732
  56.0 17.2 %collective-permute-start = (bf16[64,32,128]{2,1,0:T(8,128)(2,1)S(1)}, bf16[64,32,128]{2,1,0:T(8,128)(2,1)S(1)}, u32[]{:S(2)}, u32[]{:S(2)}) collective-permute-start(bf16[64,32,128]{2,1,0:T(8,128)(2,1)S(1)} %all_to_all.25), channel_id=1, source_target_pairs={{0,16},{16,32},{32,48},{48,0},{1,17},{17,33},{33,49},{49,1},{2,18}... | collective-permute-start | bytes 1572872 | tf_op jit(solution)/shard_map/ppermute | solution.py:397
  59.1 14.1 %collective-permute-start.1 = (bf16[64,32,128]{2,1,0:T(8,128)(2,1)S(1)}, bf16[64,32,128]{2,1,0:T(8,128)(2,1)S(1)}, u32[]{:S(2)}, u32[]{:S(2)}) collective-permute-start(bf16[64,32,128]{2,1,0:T(8,128)(2,1)S(1)} %all_to_all.25), channel_id=1, source_target_pairs={{0,48},{16,0},{32,16},{48,32},{1,49},{17,1},{33,17},{49,33},{2,50}... | collective-permute-start | bytes 1572872 | tf_op jit(solution)/shard_map/ppermute | solution.py:397
  62.5 36.8 %all-to-all-start.2 = ((bf16[256,16,128]{2,1,0:T(8,128)(2,1)}), bf16[256,16,128]{2,1,0:T(8,128)(2,1)S(1)}, u32[]{:S(2)}, u32[]{:S(2)}) async-start(bf16[256,16,128]{2,1,0:T(8,128)(2,1)} %copy-done), calls=%async_computation.2 | async-start | bytes 2097152 | tf_op jit(solution)/shard_map/all_to_all | solution.py:400
  73.2 16.7 %copy-start.2 = (bf16[32,2048]{1,0:T(8,128)(2,1)S(1)}, bf16[32,2048]{1,0:T(8,128)(2,1)}, u32[]{:S(2)}) copy-start(bf16[32,2048]{1,0:T(8,128)(2,1)} %copy-done.1) | copy-start | bytes 393220
  73.2 24.9 %copy-start.3 = (f32[2048]{0:T(1024)S(1)}, f32[2048]{0:T(1024)}, u32[]{:S(2)}) copy-start(f32[2048]{0:T(1024)} %param.13) | copy-start | bytes 24580
  73.2 24.9 %copy-start.4 = (f32[8]{0:T(128)S(1)}, f32[8]{0:T(128)}, u32[]{:S(2)}) copy-start(f32[8]{0:T(128)} %eps_occ.3) | copy-start | bytes 100
  74.1 12.3 %collective-permute-start.2 = (bf16[32,32,128]{2,1,0:T(8,128)(2,1)}, bf16[32,32,128]{2,1,0:T(8,128)(2,1)S(1)}, u32[]{:S(2)}, u32[]{:S(2)}) collective-permute-start(bf16[32,32,128]{2,1,0:T(8,128)(2,1)} %get-tuple-element.14), channel_id=1, source_target_pairs={{0,48},{16,0},{32,16},{48,32},{1,49},{17,1},{33,17},{49,33},{2,50}... | collective-permute-start | bytes 786440 | tf_op jit(solution)/shard_map/ppermute | solution.py:399
  77.0 12.9 %collective-permute-start.3 = (bf16[32,32,128]{2,1,0:T(8,128)(2,1)}, bf16[32,32,128]{2,1,0:T(8,128)(2,1)S(1)}, u32[]{:S(2)}, u32[]{:S(2)}) collective-permute-start(bf16[32,32,128]{2,1,0:T(8,128)(2,1)} %get-tuple-element.15), channel_id=1, source_target_pairs={{0,16},{16,32},{32,48},{48,0},{1,17},{17,33},{33,49},{49,1},{2,18}... | collective-permute-start | bytes 786440 | tf_op jit(solution)/shard_map/ppermute | solution.py:399
  91.4 6.7 %collective-permute-start.4 = (f32[64,1024]{1,0:T(8,128)S(1)}, f32[64,1024]{1,0:T(8,128)S(1)}, u32[]{:S(2)}, u32[]{:S(2)}) collective-permute-start(f32[64,1024]{1,0:T(8,128)S(1)} %get-tuple-element.18), channel_id=1, source_target_pairs={{0,1},{1,0},{2,3},{3,2},{4,5},{5,4},{6,7},{7,6},{8,9},{9,8},{10,11... | collective-permute-start | bytes 786440 | tf_op jit(solution)/shard_map/ppermute | solution.py:405
  101.7 8.0 %collective-permute-start.5 = (f32[256,1024]{1,0:T(8,128)S(1)}, f32[256,1024]{1,0:T(8,128)S(1)}, u32[]{:S(2)}, u32[]{:S(2)}) collective-permute-start(f32[256,1024]{1,0:T(8,128)S(1)} %get-tuple-element.23), channel_id=1, source_target_pairs={{0,1},{1,0},{2,3},{3,2},{4,5},{5,4},{6,7},{7,6},{8,9},{9,8},{10,11... | collective-permute-start | bytes 3145736 | tf_op jit(solution)/shard_map/ppermute | solution.py:407

commit v11 on v10

--- a/solution.py
+++ b/solution.py
@@ -402,8 +402,9 @@
     swap = [(0, 1), (1, 0)]
     blocks = (here, below, above, low, high)
     keep, give = panel(place, blocks, two)
-    selfs, bmat = settle(place, eps_occ, keep, lax.ppermute(give, "core", swap), eps_vir, two)
-    keep, give = gram(place, blocks, sides, selfs)
+    other = lax.ppermute(give, "core", swap)
+    selfs, bmat = settle(place, eps_occ, keep, other, eps_vir, two)
+    keep, give = gram(place, blocks, sides, other)
     got = lax.ppermute(give, "core", swap)
     scale = 1.0 / (float(vir) * float(vir) * 2048.0)
     energy = energies(scale, place, eps_occ, keep, got, eps_vir, selfs)

time: 142 us -> 141 us (level)
  waiting for transfers between devices: 23.1 us -> 21.4 us
  transfers between devices with their start and end apart: 8 -> 8, of which waited for: 5 -> 6; matrix products, arithmetic and copies ran while one was open for 0% -> 0% of each run, Pallas kernels for 4% -> 4%
where the time goes in v11:
time: 141 us
  blocking collectives  57.6 us (41%)
  starting transfers between devices  45.1 us (32%)
  waiting for transfers between devices  21.4 us (15%)
  Pallas kernels  14.3 us (10%)
  local copies, waits for them, and re-layouts  1.41 us (1%)
    all_to_all x1, blocking collectives, body(): here = lax.all_to_all(wide, ('zh', 'zl', 'yl', 'yh'), 0, 0, tiled=True)  28.4 us
    all_to_all x1, blocking collectives, body(): lax.all_to_all(small(again_kernel, (16, 1, 128), 'again')(energy), FAR, 0...  16.4 us
    all_to_all x1, blocking collectives, body(): energy = lax.all_to_all(energy, NEAR, 0, 0, tiled=True)  12.8 us
    all_to_all x1, starting transfers between devices, body(): sides = lax.all_to_all(thin, CHIPS, 0, 0, tiled=True)  10.7 us
    all_to_all x1, starting transfers between devices, body(): recv = lax.all_to_all(sent, GRP, 0, 0, tiled=True)  10.2 us
    ppermute x2, waiting for transfers between devices, body(): low, high = (lax.ppermute(low, 'x', down), lax.ppermute(high, 'x', up))  9.77 us
    all_to_all x1, waiting for transfers between devices, body(): recv = lax.all_to_all(sent, GRP, 0, 0, tiled=True)  9.32 us
    ppermute x2, starting transfers between devices, body(): below, above = (lax.ppermute(here, 'x', up), lax.ppermute(here, 'x', down))  6.48 us
  transfers between devices with their start and end apart: 8, of which 6 were waited for; matrix products, arithmetic and copies ran while one was open for 0% of the time, Pallas kernels for 4%

profile of v11, /device:TPU:1, one launch (start us, length us, event | category | flops | bytes accessed | tf_op | source)
XLA Modules:
  0.0 140.7 jit_solution(188780546121553619)
XLA Ops:
  0.6 3.6 %half.1 = f32[8,72,128]{2,1,0:T(8,128)} custom-call(s32[2,4]{1,0:T(2,128)} %bitcast.31, s32[4]{0:T(128)} %screen_at.1, bf16[8,768]{1,0:T(8,128)(2,1)} %bitcast.30, bf16[4,32,4096]{2,1,0:T(8,128)(2,1)} %ints.1), custom_call_target="tpu_custom_call" | custom-call | tf_op jit(solution)/shard_map/half/pallas_call | solution.py:87
  4.2 10.2 %all-to-all-start = ((f32[8,72,128]{2,1,0:T(8,128)}), f32[8,72,128]{2,1,0:T(8,128)S(1)}, u32[]{:S(2)}, u32[]{:S(2)}) async-start(f32[8,72,128]{2,1,0:T(8,128)} %half.1), calls=%async_computation | async-start | bytes 589824 | tf_op jit(solution)/shard_map/all_to_all | solution.py:392
  14.4 1.9 %hold.1.c_vir = bf16[768,2048]{1,0:T(8,128)(2,1)S(1)} custom-call(bf16[768,2048]{1,0:T(8,128)(2,1)} %c_vir.1), custom_call_target="tpu_custom_call" | custom-call | flops 8589934592 | bytes 4194304 | tf_op jit(solution)/shard_map/hold/pallas_call | solution.py:113
  16.3 9.3 %all-to-all-done.recv = f32[8,72,128]{2,1,0:T(8,128)S(1)} async-done(((f32[8,72,128]{2,1,0:T(8,128)}), f32[8,72,128]{2,1,0:T(8,128)S(1)}, u32[]{:S(2)}, u32[]{:S(2)}) %all-to-all-start) | async-done | bytes 294944 | tf_op jit(solution)/shard_map/all_to_all | solution.py:392
  25.6 1.3 transform.1
  27.0 0.0 copy-start.1
  27.0 0.6 copy-done.1
  27.6 0.0 copy-start
  27.6 28.4 %all_to_all.25 = bf16[64,32,128]{2,1,0:T(8,128)(2,1)S(1)} all-to-all(bf16[64,32,128]{2,1,0:T(8,128)(2,1)S(1)} %get-tuple-element.13), channel_id=1, replica_groups=mesh['zh'=4,'zl'=2,'x'=4,'yl'=2,'yh'=4,'core'=2] {'zh','zl','yl','yh'}, dimensions={0} | all-to-all | bytes 1048576 | tf_op jit(solution)/shard_map/all_to_all | solution.py:394
  56.0 3.1 %collective-permute-start = (bf16[64,32,128]{2,1,0:T(8,128)(2,1)S(1)}, bf16[64,32,128]{2,1,0:T(8,128)(2,1)S(1)}, u32[]{:S(2)}, u32[]{:S(2)}) collective-permute-start(bf16[64,32,128]{2,1,0:T(8,128)(2,1)S(1)} %all_to_all.25), channel_id=1, source_target_pairs={{0,16},{16,32},{32,48},{48,0},{1,17},{17,33},{33,49},{49,1},{2,18}... | collective-permute-start | bytes 1572872 | tf_op jit(solution)/shard_map/ppermute | solution.py:397
  59.1 3.4 %collective-permute-start.1 = (bf16[64,32,128]{2,1,0:T(8,128)(2,1)S(1)}, bf16[64,32,128]{2,1,0:T(8,128)(2,1)S(1)}, u32[]{:S(2)}, u32[]{:S(2)}) collective-permute-start(bf16[64,32,128]{2,1,0:T(8,128)(2,1)S(1)} %all_to_all.25), channel_id=1, source_target_pairs={{0,48},{16,0},{32,16},{48,32},{1,49},{17,1},{33,17},{49,33},{2,50}... | collective-permute-start | bytes 1572872 | tf_op jit(solution)/shard_map/ppermute | solution.py:397
  62.5 0.0 copy-done
  62.5 10.7 %all-to-all-start.2 = ((bf16[256,16,128]{2,1,0:T(8,128)(2,1)}), bf16[256,16,128]{2,1,0:T(8,128)(2,1)S(1)}, u32[]{:S(2)}, u32[]{:S(2)}) async-start(bf16[256,16,128]{2,1,0:T(8,128)(2,1)} %copy-done), calls=%async_computation.2 | async-start | bytes 2097152 | tf_op jit(solution)/shard_map/all_to_all | solution.py:400
  73.2 0.0 copy-start.2
  73.2 0.0 collective-permute-done.below
  73.2 0.0 collective-permute-done.1.above
  73.2 0.7 onward.1
  74.0 0.0 copy-start.3
  74.0 0.0 copy-start.4
  74.0 3.0 %collective-permute-start.2 = (bf16[32,32,128]{2,1,0:T(8,128)(2,1)}, bf16[32,32,128]{2,1,0:T(8,128)(2,1)S(1)}, u32[]{:S(2)}, u32[]{:S(2)}) collective-permute-start(bf16[32,32,128]{2,1,0:T(8,128)(2,1)} %get-tuple-element.14), channel_id=1, source_target_pairs={{0,48},{16,0},{32,16},{48,32},{1,49},{17,1},{33,17},{49,33},{2,50}... | collective-permute-start | bytes 786440 | tf_op jit(solution)/shard_map/ppermute | solution.py:399
  77.0 2.4 %collective-permute-start.3 = (bf16[32,32,128]{2,1,0:T(8,128)(2,1)S(1)}, bf16[32,32,128]{2,1,0:T(8,128)(2,1)S(1)}, u32[]{:S(2)}, u32[]{:S(2)}) collective-permute-start(bf16[32,32,128]{2,1,0:T(8,128)(2,1)S(1)} %get-tuple-element.15), channel_id=1, source_target_pairs={{0,16},{16,32},{32,48},{48,0},{1,17},{17,33},{33,49},{49,1},{2,18}... | collective-permute-start | bytes 786440 | tf_op jit(solution)/shard_map/ppermute | solution.py:399
  79.4 0.1 stack.31.place
  79.5 6.9 %collective-permute-done.2 = bf16[32,32,128]{2,1,0:T(8,128)(2,1)S(1)} collective-permute-done((bf16[32,32,128]{2,1,0:T(8,128)(2,1)}, bf16[32,32,128]{2,1,0:T(8,128)(2,1)S(1)}, u32[]{:S(2)}, u32[]{:S(2)}) %collective-permute-start.2) | collective-permute-done | bytes 262176 | tf_op jit(solution)/shard_map/ppermute | solution.py:399
  86.4 2.9 %collective-permute-done.3 = bf16[32,32,128]{2,1,0:T(8,128)(2,1)S(1)} collective-permute-done((bf16[32,32,128]{2,1,0:T(8,128)(2,1)S(1)}, bf16[32,32,128]{2,1,0:T(8,128)(2,1)S(1)}, u32[]{:S(2)}, u32[]{:S(2)}) %collective-permute-start.3) | collective-permute-done | bytes 262176 | tf_op jit(solution)/shard_map/ppermute | solution.py:399
  89.3 0.0 copy-done.2
  89.3 1.5 %panel.1 = (f32[32,1024]{1,0:T(8,128)S(1)}, f32[64,1024]{1,0:T(8,128)S(1)}) custom-call(s32[7]{0:T(128)S(1)} %stack.31.place, bf16[16,8,16,128]{3,2,1,0:T(8,128)(2,1)S(1)} %bitcast.17, bf16[16,8,16,128]{3,2,1,0:T(8,128)(2,1)S(1)} %bitcast.20, bf16[16,8,16,128]{3,2,1,0:T(8,128)(2,1)S(1)} %bitcast.22, bf16[8,8,16,128]{3,2,1,0:T(8,128)(2,1)S(1)} %bitcast.24, ...), custom_call_target="tpu_custom_call" | custom-call | flops 536870912 | bytes 4194304 | tf_op jit(solution)/shard_map/panel/pallas_call | solution.py:228
  90.7 0.0 copy-start.5
  90.8 0.6 copy-done.5
  91.4 6.0 %collective-permute-start.4 = (f32[64,1024]{1,0:T(8,128)S(1)}, f32[64,1024]{1,0:T(8,128)S(1)}, u32[]{:S(2)}, u32[]{:S(2)}) collective-permute-start(f32[64,1024]{1,0:T(8,128)S(1)} %get-tuple-element.18), channel_id=1, source_target_pairs={{0,1},{1,0},{2,3},{3,2},{4,5},{5,4},{6,7},{7,6},{8,9},{9,8},{10,11... | collective-permute-start | bytes 786440 | tf_op jit(solution)/shard_map/ppermute | solution.py:405
  97.4 1.1 collective-permute-done.4.got._
  98.6 0.2 all-to-all-done.2
  98.7 0.0 copy-start.6
  98.7 2.4 %gram.1 = (f32[256,1024]{1,0:T(8,128)S(1)}, f32[256,1024]{1,0:T(8,128)S(1)}) custom-call(s32[7]{0:T(128)S(1)} %stack.31.place, bf16[16,8,16,128]{3,2,1,0:T(8,128)(2,1)S(1)} %bitcast.18, bf16[16,8,16,128]{3,2,1,0:T(8,128)(2,1)S(1)} %bitcast.21, bf16[16,8,16,128]{3,2,1,0:T(8,128)(2,1)S(1)} %bitcast.23, bf16[8,8,16,128]{3,2,1,0:T(8,128)(2,1)S(1)} %bitcast.25, ...), custom_call_target="tpu_custom_call" | custom-call | tf_op jit(solution)/shard_map/gram/pallas_call | solution.py:304
  101.2 6.4 %collective-permute-start.5 = (f32[256,1024]{1,0:T(8,128)S(1)}, f32[256,1024]{1,0:T(8,128)S(1)}, u32[]{:S(2)}, u32[]{:S(2)}) collective-permute-start(f32[256,1024]{1,0:T(8,128)S(1)} %get-tuple-element.22), channel_id=1, source_target_pairs={{0,1},{1,0},{2,3},{3,2},{4,5},{5,4},{6,7},{7,6},{8,9},{9,8},{10,11... | collective-permute-start | bytes 3145736 | tf_op jit(solution)/shard_map/ppermute | solution.py:408
  107.5 0.0 copy-done.3
  107.5 0.0 copy-done.4
  107.5 0.0 copy-done.6
  107.6 1.2 settle.1
  108.8 1.0 collective-permute-done.5.got
  109.8 0.9 energies.1
  110.7 12.8 %all_to_all.26.got = f32[32,1,128]{2,1,0:T(1,128)S(1)} all-to-all(f32[32,1,128]{2,1,0:T(1,128)S(1)} %energies.1), channel_id=1, replica_groups=mesh['zh'=4,'zl'=2,'x'=4,'yl'=2,'yh'=4,'core'=2] {'zl','x','yl','core'}, dimensions={0} | all-to-all | bytes 32768 | tf_op jit(solution)/shard_map/all_to_all | solution.py:411
  123.6 16.4 %all_to_all.27.got = f32[16,1,128]{2,1,0:T(1,128)S(1)} all-to-all(f32[16,1,128]{2,1,0:T(1,128)S(1)} %again.1), channel_id=1, replica_groups=mesh['zh'=4,'zl'=2,'x'=4,'yl'=2,'yh'=4,'core'=2] {'zh','yh'}, dimensions={0} | all-to-all | bytes 16384 | tf_op jit(solution)/shard_map/all_to_all | solution.py:412
  140.0 0.7 last.1
  (1 shorter events, 0.0 us)
Async XLA Ops:
  4.2 21.4 %all-to-all-start = ((f32[8,72,128]{2,1,0:T(8,128)}), f32[8,72,128]{2,1,0:T(8,128)S(1)}, u32[]{:S(2)}, u32[]{:S(2)}) async-start(f32[8,72,128]{2,1,0:T(8,128)} %half.1), calls=%async_computation | async-start | bytes 589824 | tf_op jit(solution)/shard_map/all_to_all | solution.py:392
  27.0 0.7 copy-start.1
  27.6 34.9 %copy-start = (bf16[256,16,128]{2,1,0:T(8,128)(2,1)}, bf16[256,16,128]{2,1,0:T(8,128)(2,1)S(1)}, u32[]{:S(2)}) copy-start(bf16[256,16,128]{2,1,0:T(8,128)(2,1)S(1)} %get-tuple-element.20) | copy-start | bytes 3145732
  56.0 17.2 %collective-permute-start = (bf16[64,32,128]{2,1,0:T(8,128)(2,1)S(1)}, bf16[64,32,128]{2,1,0:T(8,128)(2,1)S(1)}, u32[]{:S(2)}, u32[]{:S(2)}) collective-permute-start(bf16[64,32,128]{2,1,0:T(8,128)(2,1)S(1)} %all_to_all.25), channel_id=1, source_target_pairs={{0,16},{16,32},{32,48},{48,0},{1,17},{17,33},{33,49},{49,1},{2,18}... | collective-permute-start | bytes 1572872 | tf_op jit(solution)/shard_map/ppermute | solution.py:397
  59.1 14.1 %collective-permute-start.1 = (bf16[64,32,128]{2,1,0:T(8,128)(2,1)S(1)}, bf16[64,32,128]{2,1,0:T(8,128)(2,1)S(1)}, u32[]{:S(2)}, u32[]{:S(2)}) collective-permute-start(bf16[64,32,128]{2,1,0:T(8,128)(2,1)S(1)} %all_to_all.25), channel_id=1, source_target_pairs={{0,48},{16,0},{32,16},{48,32},{1,49},{17,1},{33,17},{49,33},{2,50}... | collective-permute-start | bytes 1572872 | tf_op jit(solution)/shard_map/ppermute | solution.py:397
  62.5 36.2 %all-to-all-start.2 = ((bf16[256,16,128]{2,1,0:T(8,128)(2,1)}), bf16[256,16,128]{2,1,0:T(8,128)(2,1)S(1)}, u32[]{:S(2)}, u32[]{:S(2)}) async-start(bf16[256,16,128]{2,1,0:T(8,128)(2,1)} %copy-done), calls=%async_computation.2 | async-start | bytes 2097152 | tf_op jit(solution)/shard_map/all_to_all | solution.py:400
  73.2 16.1 %copy-start.2 = (bf16[32,2048]{1,0:T(8,128)(2,1)S(1)}, bf16[32,2048]{1,0:T(8,128)(2,1)}, u32[]{:S(2)}) copy-start(bf16[32,2048]{1,0:T(8,128)(2,1)} %copy-done.1) | copy-start | bytes 393220
  74.0 33.5 %copy-start.3 = (f32[2048]{0:T(1024)S(1)}, f32[2048]{0:T(1024)}, u32[]{:S(2)}) copy-start(f32[2048]{0:T(1024)} %param.13) | copy-start | bytes 24580
  74.0 33.6 %copy-start.4 = (f32[8]{0:T(128)S(1)}, f32[8]{0:T(128)}, u32[]{:S(2)}) copy-start(f32[8]{0:T(128)} %eps_occ.3) | copy-start | bytes 100
  74.0 12.4 %collective-permute-start.2 = (bf16[32,32,128]{2,1,0:T(8,128)(2,1)}, bf16[32,32,128]{2,1,0:T(8,128)(2,1)S(1)}, u32[]{:S(2)}, u32[]{:S(2)}) collective-permute-start(bf16[32,32,128]{2,1,0:T(8,128)(2,1)} %get-tuple-element.14), channel_id=1, source_target_pairs={{0,48},{16,0},{32,16},{48,32},{1,49},{17,1},{33,17},{49,33},{2,50}... | collective-permute-start | bytes 786440 | tf_op jit(solution)/shard_map/ppermute | solution.py:399
  77.0 12.3 %collective-permute-start.3 = (bf16[32,32,128]{2,1,0:T(8,128)(2,1)S(1)}, bf16[32,32,128]{2,1,0:T(8,128)(2,1)S(1)}, u32[]{:S(2)}, u32[]{:S(2)}) collective-permute-start(bf16[32,32,128]{2,1,0:T(8,128)(2,1)S(1)} %get-tuple-element.15), channel_id=1, source_target_pairs={{0,16},{16,32},{32,48},{48,0},{1,17},{17,33},{33,49},{49,1},{2,18}... | collective-permute-start | bytes 786440 | tf_op jit(solution)/shard_map/ppermute | solution.py:399
  90.7 0.7 copy-start.5
  91.4 7.2 %collective-permute-start.4 = (f32[64,1024]{1,0:T(8,128)S(1)}, f32[64,1024]{1,0:T(8,128)S(1)}, u32[]{:S(2)}, u32[]{:S(2)}) collective-permute-start(f32[64,1024]{1,0:T(8,128)S(1)} %get-tuple-element.18), channel_id=1, source_target_pairs={{0,1},{1,0},{2,3},{3,2},{4,5},{5,4},{6,7},{7,6},{8,9},{9,8},{10,11... | collective-permute-start | bytes 786440 | tf_op jit(solution)/shard_map/ppermute | solution.py:405
  98.7 8.8 %copy-start.6 = (f32[32,1024]{1,0:T(8,128)S(1)}, f32[32,1024]{1,0:T(8,128)}, u32[]{:S(2)}) copy-start(f32[32,1024]{1,0:T(8,128)} %copy-done.5) | copy-start | bytes 393220
  101.2 8.6 %collective-permute-start.5 = (f32[256,1024]{1,0:T(8,128)S(1)}, f32[256,1024]{1,0:T(8,128)S(1)}, u32[]{:S(2)}, u32[]{:S(2)}) collective-permute-start(f32[256,1024]{1,0:T(8,128)S(1)} %get-tuple-element.22), channel_id=1, source_target_pairs={{0,1},{1,0},{2,3},{3,2},{4,5},{5,4},{6,7},{7,6},{8,9},{9,8},{10,11... | collective-permute-start | bytes 3145736 | tf_op jit(solution)/shard_map/ppermute | solution.py:408

commit v12 on v10

--- a/solution.py
+++ b/solution.py
@@ -13,8 +13,6 @@
 AXES = ("zh", "zl", "x", "yl", "yh", "core")
 CHIPS = ("zh", "zl", "x", "yl", "yh")
 PAIR = ("zh", "zl", "x", "yl")
-NEAR = ("zl", "x", "yl", "core")
-FAR = ("zh", "yh")
 GRP = ("yh", "core")
 F32 = jnp.float32
 BF16 = jnp.bfloat16
@@ -345,7 +343,7 @@
 def energies(scale, place, eps_occ, keep, got, eps_vir, selfs):
     return pl.pallas_call(
         functools.partial(energy_kernel, scale),
-        out_shape=jax.ShapeDtypeStruct((32, 1, 128), F32),
+        out_shape=jax.ShapeDtypeStruct((256, 1, 128), F32),
         in_specs=[SMEM, SMEM, VMEM, VMEM, VMEM, VMEM],
         out_specs=VMEM,
         scratch_shapes=[pltpu.VMEM((64, 128), F32)],
@@ -359,10 +357,6 @@
     tile, kind = zh * 4 + zl * 2 + yl, x * 4 + yh
     step, side = lax.shift_right_logical(kind, 1) + 1, kind & 1
     return jnp.stack([tile, (tile + step) & (TILES - 1), step, side, core, lax.shift_right_logical(kind, 1), x])
-
-
-def again_kernel(got, out):
-    out[...] = jnp.broadcast_to(jnp.sum(got[...], axis=0)[None], out.shape)
 
 
 def last_kernel(got, out):
@@ -407,9 +401,8 @@
     got = lax.ppermute(give, "core", swap)
     scale = 1.0 / (float(vir) * float(vir) * 2048.0)
     energy = energies(scale, place, eps_occ, keep, got, eps_vir, selfs)
-    energy = lax.all_to_all(energy, NEAR, 0, 0, tiled=True)
-    energy = lax.all_to_all(small(again_kernel, (16, 1, 128), "again")(energy), FAR, 0, 0, tiled=True)
-    energy = small(last_kernel, (occ, occ), "last")(energy)
+    energy = lax.all_to_all(energy, CHIPS, 0, 0, tiled=True)
+    energy = lax.psum(small(last_kernel, (occ, occ), "last")(energy), "core")
     return bmat.reshape(1, 32, vir), energy
 
 

time: 142 us -> 142 us (level)
    psum x0 -> x1, blocking collectives: none -> 4.72 us  [body(): energy = lax.psum(small(last_kernel, (occ, occ), 'last')(energy), 'core')]
    all_to_all x2 -> x1, blocking collectives: 29.9 us -> 25.2 us  [body(): energy = lax.all_to_all(energy, CHIPS, 0, 0, tiled=True)]
where the time goes in v12:
time: 142 us; the launch traced here: 141 us
  blocking collectives  58.3 us (41%)
  starting transfers between devices  44 us (31%)
  waiting for transfers between devices  23.2 us (16%)
  Pallas kernels  14.1 us (10%)
    all_to_all x1, blocking collectives, body(): here = lax.all_to_all(wide, ('zh', 'zl', 'yl', 'yh'), 0, 0, tiled=True)  28.4 us
    all_to_all x1, blocking collectives, body(): energy = lax.all_to_all(energy, CHIPS, 0, 0, tiled=True)  25.2 us
    all_to_all x1, starting transfers between devices, body(): sides = lax.all_to_all(thin, CHIPS, 0, 0, tiled=True)  10.7 us
    ppermute x2, waiting for transfers between devices, body(): low, high = (lax.ppermute(low, 'x', down), lax.ppermute(high, 'x', up))  10.4 us
    all_to_all x1, starting transfers between devices, body(): recv = lax.all_to_all(sent, GRP, 0, 0, tiled=True)  10.2 us
    all_to_all x1, waiting for transfers between devices, body(): recv = lax.all_to_all(sent, GRP, 0, 0, tiled=True)  9.32 us
    ppermute x2, starting transfers between devices, body(): below, above = (lax.ppermute(here, 'x', up), lax.ppermute(here, 'x', down))  6.48 us
    ppermute x1, starting transfers between devices, body(): got = lax.ppermute(give, 'core', swap)  5.77 us
  transfers between devices with their start and end apart: 8, of which 5 were waited for; matrix products, arithmetic and copies ran while one was open for 0% of the time, Pallas kernels for 4%

profile of v12, /device:TPU:1, one launch (start us, length us, event | category | flops | bytes accessed | tf_op | source)
XLA Modules:
  0.0 141.0 jit_solution(17703246071797193774)
XLA Ops:
  0.6 3.6 %half.1 = f32[8,72,128]{2,1,0:T(8,128)} custom-call(s32[2,4]{1,0:T(2,128)} %bitcast.31, s32[4]{0:T(128)} %screen_at.1, bf16[8,768]{1,0:T(8,128)(2,1)} %bitcast.30, bf16[4,32,4096]{2,1,0:T(8,128)(2,1)} %ints.1), custom_call_target="tpu_custom_call" | custom-call | tf_op jit(solution)/shard_map/half/pallas_call | solution.py:85
  4.2 10.2 %all-to-all-start = ((f32[8,72,128]{2,1,0:T(8,128)}), f32[8,72,128]{2,1,0:T(8,128)S(1)}, u32[]{:S(2)}, u32[]{:S(2)}) async-start(f32[8,72,128]{2,1,0:T(8,128)} %half.1), calls=%async_computation | async-start | bytes 589824 | tf_op jit(solution)/shard_map/all_to_all | solution.py:386
  14.4 1.9 %hold.1.c_vir = bf16[768,2048]{1,0:T(8,128)(2,1)S(1)} custom-call(bf16[768,2048]{1,0:T(8,128)(2,1)} %c_vir.1), custom_call_target="tpu_custom_call" | custom-call | flops 8589934592 | bytes 4194304 | tf_op jit(solution)/shard_map/hold/pallas_call | solution.py:111
  16.3 9.3 %all-to-all-done.recv = f32[8,72,128]{2,1,0:T(8,128)S(1)} async-done(((f32[8,72,128]{2,1,0:T(8,128)}), f32[8,72,128]{2,1,0:T(8,128)S(1)}, u32[]{:S(2)}, u32[]{:S(2)}) %all-to-all-start) | async-done | bytes 294944 | tf_op jit(solution)/shard_map/all_to_all | solution.py:386
  25.6 1.3 transform.1
  27.0 0.0 copy-start.1
  27.0 0.6 copy-done.1
  27.6 0.0 copy-start
  27.6 28.4 %all_to_all.20 = bf16[64,32,128]{2,1,0:T(8,128)(2,1)S(1)} all-to-all(bf16[64,32,128]{2,1,0:T(8,128)(2,1)S(1)} %get-tuple-element.13), channel_id=1, replica_groups=mesh['zh'=4,'zl'=2,'x'=4,'yl'=2,'yh'=4,'core'=2] {'zh','zl','yl','yh'}, dimensions={0} | all-to-all | bytes 1048576 | tf_op jit(solution)/shard_map/all_to_all | solution.py:388
  56.0 3.1 %collective-permute-start = (bf16[64,32,128]{2,1,0:T(8,128)(2,1)S(1)}, bf16[64,32,128]{2,1,0:T(8,128)(2,1)S(1)}, u32[]{:S(2)}, u32[]{:S(2)}) collective-permute-start(bf16[64,32,128]{2,1,0:T(8,128)(2,1)S(1)} %all_to_all.20), channel_id=1, source_target_pairs={{0,16},{16,32},{32,48},{48,0},{1,17},{17,33},{33,49},{49,1},{2,18}... | collective-permute-start | bytes 1572872 | tf_op jit(solution)/shard_map/ppermute | solution.py:391
  59.1 3.4 %collective-permute-start.1 = (bf16[64,32,128]{2,1,0:T(8,128)(2,1)S(1)}, bf16[64,32,128]{2,1,0:T(8,128)(2,1)S(1)}, u32[]{:S(2)}, u32[]{:S(2)}) collective-permute-start(bf16[64,32,128]{2,1,0:T(8,128)(2,1)S(1)} %all_to_all.20), channel_id=1, source_target_pairs={{0,48},{16,0},{32,16},{48,32},{1,49},{17,1},{33,17},{49,33},{2,50}... | collective-permute-start | bytes 1572872 | tf_op jit(solution)/shard_map/ppermute | solution.py:391
  62.5 0.0 copy-done
  62.5 10.7 %all-to-all-start.2 = ((bf16[256,16,128]{2,1,0:T(8,128)(2,1)}), bf16[256,16,128]{2,1,0:T(8,128)(2,1)S(1)}, u32[]{:S(2)}, u32[]{:S(2)}) async-start(bf16[256,16,128]{2,1,0:T(8,128)(2,1)} %copy-done), calls=%async_computation.2 | async-start | bytes 2097152 | tf_op jit(solution)/shard_map/all_to_all | solution.py:394
  73.2 0.0 copy-start.2
  73.2 0.0 copy-start.3
  73.2 0.0 copy-start.4
  73.2 0.0 collective-permute-done.below
  73.3 0.0 collective-permute-done.1.above
  73.3 0.9 onward.1
  74.1 2.8 %collective-permute-start.2 = (bf16[32,32,128]{2,1,0:T(8,128)(2,1)}, bf16[32,32,128]{2,1,0:T(8,128)(2,1)S(1)}, u32[]{:S(2)}, u32[]{:S(2)}) collective-permute-start(bf16[32,32,128]{2,1,0:T(8,128)(2,1)} %get-tuple-element.14), channel_id=1, source_target_pairs={{0,48},{16,0},{32,16},{48,32},{1,49},{17,1},{33,17},{49,33},{2,50}... | collective-permute-start | bytes 786440 | tf_op jit(solution)/shard_map/ppermute | solution.py:393
  77.0 2.4 %collective-permute-start.3 = (bf16[32,32,128]{2,1,0:T(8,128)(2,1)}, bf16[32,32,128]{2,1,0:T(8,128)(2,1)S(1)}, u32[]{:S(2)}, u32[]{:S(2)}) collective-permute-start(bf16[32,32,128]{2,1,0:T(8,128)(2,1)} %get-tuple-element.15), channel_id=1, source_target_pairs={{0,16},{16,32},{32,48},{48,0},{1,17},{17,33},{33,49},{49,1},{2,18}... | collective-permute-start | bytes 786440 | tf_op jit(solution)/shard_map/ppermute | solution.py:393
  79.4 0.1 stack.31.place
  79.5 6.9 %collective-permute-done.2 = bf16[32,32,128]{2,1,0:T(8,128)(2,1)S(1)} collective-permute-done((bf16[32,32,128]{2,1,0:T(8,128)(2,1)}, bf16[32,32,128]{2,1,0:T(8,128)(2,1)S(1)}, u32[]{:S(2)}, u32[]{:S(2)}) %collective-permute-start.2) | collective-permute-done | bytes 262176 | tf_op jit(solution)/shard_map/ppermute | solution.py:393
  86.4 3.5 %collective-permute-done.3 = bf16[32,32,128]{2,1,0:T(8,128)(2,1)S(1)} collective-permute-done((bf16[32,32,128]{2,1,0:T(8,128)(2,1)}, bf16[32,32,128]{2,1,0:T(8,128)(2,1)S(1)}, u32[]{:S(2)}, u32[]{:S(2)}) %collective-permute-start.3) | collective-permute-done | bytes 262176 | tf_op jit(solution)/shard_map/ppermute | solution.py:393
  89.9 0.0 copy-done.2
  89.9 1.5 %panel.1 = (f32[32,1024]{1,0:T(8,128)S(1)}, f32[64,1024]{1,0:T(8,128)S(1)}) custom-call(s32[7]{0:T(128)S(1)} %stack.31.place, bf16[16,8,16,128]{3,2,1,0:T(8,128)(2,1)S(1)} %bitcast.17, bf16[16,8,16,128]{3,2,1,0:T(8,128)(2,1)S(1)} %bitcast.20, bf16[16,8,16,128]{3,2,1,0:T(8,128)(2,1)S(1)} %bitcast.22, bf16[8,8,16,128]{3,2,1,0:T(8,128)(2,1)S(1)} %bitcast.24, ...), custom_call_target="tpu_custom_call" | custom-call | flops 536870912 | bytes 4194304 | tf_op jit(solution)/shard_map/panel/pallas_call | solution.py:226
  91.4 5.5 %collective-permute-start.4 = (f32[64,1024]{1,0:T(8,128)S(1)}, f32[64,1024]{1,0:T(8,128)S(1)}, u32[]{:S(2)}, u32[]{:S(2)}) collective-permute-start(f32[64,1024]{1,0:T(8,128)S(1)} %get-tuple-element.18), channel_id=1, source_target_pairs={{0,1},{1,0},{2,3},{3,2},{4,5},{5,4},{6,7},{7,6},{8,9},{9,8},{10,11... | collective-permute-start | bytes 786440 | tf_op jit(solution)/shard_map/ppermute | solution.py:399
  97.0 1.1 collective-permute-done.4.got
  98.1 0.0 copy-done.3
  98.1 0.0 copy-done.4
  98.1 1.2 settle.1
  99.3 0.0 all-to-all-done.2
  99.3 2.4 %gram.1 = (f32[256,1024]{1,0:T(8,128)S(1)}, f32[256,1024]{1,0:T(8,128)S(1)}) custom-call(s32[7]{0:T(128)S(1)} %stack.31.place, bf16[16,8,16,128]{3,2,1,0:T(8,128)(2,1)S(1)} %bitcast.18, bf16[16,8,16,128]{3,2,1,0:T(8,128)(2,1)S(1)} %bitcast.21, bf16[16,8,16,128]{3,2,1,0:T(8,128)(2,1)S(1)} %bitcast.23, bf16[8,8,16,128]{3,2,1,0:T(8,128)(2,1)S(1)} %bitcast.25, ...), custom_call_target="tpu_custom_call" | custom-call | tf_op jit(solution)/shard_map/gram/pallas_call | solution.py:302
  101.7 5.8 %collective-permute-start.5 = (f32[256,1024]{1,0:T(8,128)S(1)}, f32[256,1024]{1,0:T(8,128)S(1)}, u32[]{:S(2)}, u32[]{:S(2)}) collective-permute-start(f32[256,1024]{1,0:T(8,128)S(1)} %get-tuple-element.23), channel_id=1, source_target_pairs={{0,1},{1,0},{2,3},{3,2},{4,5},{5,4},{6,7},{7,6},{8,9},{9,8},{10,11... | collective-permute-start | bytes 3145736 | tf_op jit(solution)/shard_map/ppermute | solution.py:401
  107.5 2.3 %collective-permute-done.5.got = f32[256,1024]{1,0:T(8,128)S(1)} collective-permute-done((f32[256,1024]{1,0:T(8,128)S(1)}, f32[256,1024]{1,0:T(8,128)S(1)}, u32[]{:S(2)}, u32[]{:S(2)}) %collective-permute-start.5) | collective-permute-done | bytes 1048608 | tf_op jit(solution)/shard_map/ppermute | solution.py:401
  109.8 1.0 energies.1
  110.8 25.2 %all_to_all.21.got = f32[256,1,128]{2,1,0:T(1,128)S(1)} all-to-all(f32[256,1,128]{2,1,0:T(1,128)S(1)} %energies.1), channel_id=1, replica_groups=mesh['zh'=4,'zl'=2,'x'=4,'yl'=2,'yh'=4,'core'=2] {'zh','zl','x','yl','yh'}, dimensions={0} | all-to-all | bytes 262144 | tf_op jit(solution)/shard_map/all_to_all | solution.py:404
  136.0 0.3 last.1
  136.3 4.7 %psum.7 = f32[8,8]{1,0:T(8,128)} all-reduce(f32[8,8]{1,0:T(8,128)S(1)} %last.1), channel_id=1, replica_groups=mesh['zh'=4,'zl'=2,'x'=4,'yl'=2,'yh'=4,'core'=2] {'core'}, use_global_device_ids=true, to_apply=%region_0.0 | all-reduce | flops 64 | bytes 512 | tf_op jit(solution)/shard_map/psum | solution.py:405
Async XLA Ops:
  4.2 21.4 %all-to-all-start = ((f32[8,72,128]{2,1,0:T(8,128)}), f32[8,72,128]{2,1,0:T(8,128)S(1)}, u32[]{:S(2)}, u32[]{:S(2)}) async-start(f32[8,72,128]{2,1,0:T(8,128)} %half.1), calls=%async_computation | async-start | bytes 589824 | tf_op jit(solution)/shard_map/all_to_all | solution.py:386
  27.0 0.7 copy-start.1
  27.6 34.9 %copy-start = (bf16[256,16,128]{2,1,0:T(8,128)(2,1)}, bf16[256,16,128]{2,1,0:T(8,128)(2,1)S(1)}, u32[]{:S(2)}) copy-start(bf16[256,16,128]{2,1,0:T(8,128)(2,1)S(1)} %get-tuple-element.20) | copy-start | bytes 3145732
  56.0 17.2 %collective-permute-start = (bf16[64,32,128]{2,1,0:T(8,128)(2,1)S(1)}, bf16[64,32,128]{2,1,0:T(8,128)(2,1)S(1)}, u32[]{:S(2)}, u32[]{:S(2)}) collective-permute-start(bf16[64,32,128]{2,1,0:T(8,128)(2,1)S(1)} %all_to_all.20), channel_id=1, source_target_pairs={{0,16},{16,32},{32,48},{48,0},{1,17},{17,33},{33,49},{49,1},{2,18}... | collective-permute-start | bytes 1572872 | tf_op jit(solution)/shard_map/ppermute | solution.py:391
  59.1 14.1 %collective-permute-start.1 = (bf16[64,32,128]{2,1,0:T(8,128)(2,1)S(1)}, bf16[64,32,128]{2,1,0:T(8,128)(2,1)S(1)}, u32[]{:S(2)}, u32[]{:S(2)}) collective-permute-start(bf16[64,32,128]{2,1,0:T(8,128)(2,1)S(1)} %all_to_all.20), channel_id=1, source_target_pairs={{0,48},{16,0},{32,16},{48,32},{1,49},{17,1},{33,17},{49,33},{2,50}... | collective-permute-start | bytes 1572872 | tf_op jit(solution)/shard_map/ppermute | solution.py:391
  62.5 36.8 %all-to-all-start.2 = ((bf16[256,16,128]{2,1,0:T(8,128)(2,1)}), bf16[256,16,128]{2,1,0:T(8,128)(2,1)S(1)}, u32[]{:S(2)}, u32[]{:S(2)}) async-start(bf16[256,16,128]{2,1,0:T(8,128)(2,1)} %copy-done), calls=%async_computation.2 | async-start | bytes 2097152 | tf_op jit(solution)/shard_map/all_to_all | solution.py:394
  73.2 16.7 %copy-start.2 = (bf16[32,2048]{1,0:T(8,128)(2,1)S(1)}, bf16[32,2048]{1,0:T(8,128)(2,1)}, u32[]{:S(2)}) copy-start(bf16[32,2048]{1,0:T(8,128)(2,1)} %copy-done.1) | copy-start | bytes 393220
  73.2 24.9 %copy-start.3 = (f32[2048]{0:T(1024)S(1)}, f32[2048]{0:T(1024)}, u32[]{:S(2)}) copy-start(f32[2048]{0:T(1024)} %param.13) | copy-start | bytes 24580
  73.2 24.9 %copy-start.4 = (f32[8]{0:T(128)S(1)}, f32[8]{0:T(128)}, u32[]{:S(2)}) copy-start(f32[8]{0:T(128)} %eps_occ.3) | copy-start | bytes 100
  74.1 12.3 %collective-permute-start.2 = (bf16[32,32,128]{2,1,0:T(8,128)(2,1)}, bf16[32,32,128]{2,1,0:T(8,128)(2,1)S(1)}, u32[]{:S(2)}, u32[]{:S(2)}) collective-permute-start(bf16[32,32,128]{2,1,0:T(8,128)(2,1)} %get-tuple-element.14), channel_id=1, source_target_pairs={{0,48},{16,0},{32,16},{48,32},{1,49},{17,1},{33,17},{49,33},{2,50}... | collective-permute-start | bytes 786440 | tf_op jit(solution)/shard_map/ppermute | solution.py:393
  77.0 12.9 %collective-permute-start.3 = (bf16[32,32,128]{2,1,0:T(8,128)(2,1)}, bf16[32,32,128]{2,1,0:T(8,128)(2,1)S(1)}, u32[]{:S(2)}, u32[]{:S(2)}) collective-permute-start(bf16[32,32,128]{2,1,0:T(8,128)(2,1)} %get-tuple-element.15), channel_id=1, source_target_pairs={{0,16},{16,32},{32,48},{48,0},{1,17},{17,33},{33,49},{49,1},{2,18}... | collective-permute-start | bytes 786440 | tf_op jit(solution)/shard_map/ppermute | solution.py:393
  91.4 6.7 %collective-permute-start.4 = (f32[64,1024]{1,0:T(8,128)S(1)}, f32[64,1024]{1,0:T(8,128)S(1)}, u32[]{:S(2)}, u32[]{:S(2)}) collective-permute-start(f32[64,1024]{1,0:T(8,128)S(1)} %get-tuple-element.18), channel_id=1, source_target_pairs={{0,1},{1,0},{2,3},{3,2},{4,5},{5,4},{6,7},{7,6},{8,9},{9,8},{10,11... | collective-permute-start | bytes 786440 | tf_op jit(solution)/shard_map/ppermute | solution.py:399
  101.7 8.0 %collective-permute-start.5 = (f32[256,1024]{1,0:T(8,128)S(1)}, f32[256,1024]{1,0:T(8,128)S(1)}, u32[]{:S(2)}, u32[]{:S(2)}) collective-permute-start(f32[256,1024]{1,0:T(8,128)S(1)} %get-tuple-element.23), channel_id=1, source_target_pairs={{0,1},{1,0},{2,3},{3,2},{4,5},{5,4},{6,7},{7,6},{8,9},{9,8},{10,11... | collective-permute-start | bytes 3145736 | tf_op jit(solution)/shard_map/ppermute | solution.py:401

commit v13 on v10

--- a/solution.py
+++ b/solution.py
@@ -135,7 +135,7 @@
         sides[tile * 2 + 1] = jnp.where(left, pltpu.roll(one, SHELL, 1), two).astype(BF16)
 
 
-def transform_kernel(recv, c_vir, bmat, wide, thin, terms, sides):
+def transform_kernel(recv, c_vir, wide, thin, bmat, terms, sides):
     left = lanes((16, 128)) < SHELL
     sums = [jnp.zeros((16, 128), F32) for _ in range(SHELLS)]
     for source in range(8):
@@ -173,13 +173,16 @@
     return pl.pallas_call(
         transform_kernel,
         out_shape=(
-            jax.ShapeDtypeStruct((32, c_vir.shape[1]), BF16),
             jax.ShapeDtypeStruct((64, 32, 128), BF16),
             jax.ShapeDtypeStruct((256, 16, 128), BF16),
         ),
         in_specs=[VMEM, VMEM],
-        out_specs=(VMEM, VMEM, VMEM),
-        scratch_shapes=[pltpu.VMEM((96, c_vir.shape[0]), BF16), pltpu.VMEM((32, 16, 128), BF16)],
+        out_specs=(VMEM, VMEM),
+        scratch_shapes=[
+            pltpu.VMEM((32, c_vir.shape[1]), BF16),
+            pltpu.VMEM((96, c_vir.shape[0]), BF16),
+            pltpu.VMEM((32, 16, 128), BF16),
+        ],
         compiler_params=grant(16),
         name="transform",
     )(recv, c_vir)
@@ -203,41 +206,60 @@
     )(below, above)
 
 
-def panel_kernel(place, here, below, above, low, high, two, keep, give, wide, all_s):
+def panel_kernel(place, here, below, above, low, high, thin, keep, give, mine, wide, all_s, held, sem):
     core, side, own = place[4], place[3], place[5]
+    copies = []
+    for piece in range(2 * TILES):
+        r = (piece // 2 - 1) % TILES
+        at = (r // 2 * 8 + r % 2) * 4 + piece % 2
+        copies.append(pltpu.make_async_copy(thin.at[at], held.at[piece], sem.at[piece]))
+        copies[piece].start()
     first = 0
     for tiles in (here, below, above, low, high):
         count = tiles.shape[0] * 16
         for i in range(8):
             wide[first : first + count, i * 128 : i * 128 + 128] = tiles[:, i].reshape(count, 128)
         first += count
-    mine = wide[:, pl.ds(pl.multiple_of(own * 128, 128), 128)]
+    first = wide[:, pl.ds(pl.multiple_of(own * 128, 128), 128)]
     others = wide[:, pl.ds(pl.multiple_of(side * 512, 512), 512)]
-    all_s[...] = lax.dot_general(mine, others, TRANSPOSED, preferred_element_type=F32)
+    all_s[...] = lax.dot_general(first, others, TRANSPOSED, preferred_element_type=F32)
     for which, target in ((core, keep), (1 - core, give)):
         at = pl.multiple_of(which * 256, 256)
         for q in range(4):
             target[0:32, q * 256 : q * 256 + 256] = all_s[q * 32 : q * 32 + 32, pl.ds(at, 256)]
-    at = pl.multiple_of((1 - core) * 16, 16)
-    for q in range(2):
-        give[32 + q * 16 : 48 + q * 16, :] = two[pl.ds(at, 16), q * 1024 : q * 1024 + 1024].astype(F32)
-
-
-def panel(place, blocks, two):
+    for copy in copies:
+        copy.wait()
+    left = lanes((16, 128)) < SHELL
+    for t in range(TILES):
+        one, two = held[t * 2].astype(F32), held[t * 2 + 1].astype(F32)
+        even = jnp.where(left, one, pltpu.roll(two, SHELL, 1))
+        odd = jnp.where(left, pltpu.roll(one, SHELL, 1), two)
+        mine[:, t * 128 : t * 128 + 128] = jnp.where(core == 0, even, odd).astype(BF16)
+        q, at = t // 8, t % 8 * 128
+        give[32 + q * 16 : 48 + q * 16, at : at + 128] = jnp.where(core == 0, odd, even)
+
+
+def panel(place, blocks, thin):
     tiles = (block.reshape(-1, 8, 16, 128) for block in blocks)
     return pl.pallas_call(
         panel_kernel,
         out_shape=(
             jax.ShapeDtypeStruct((32, 1024), F32),
             jax.ShapeDtypeStruct((64, 1024), F32),
+            jax.ShapeDtypeStruct((16, 128 * TILES), BF16),
         ),
-        in_specs=[SMEM] + [VMEM] * 6,
-        out_specs=(VMEM, VMEM),
-        scratch_shapes=[pltpu.VMEM((1024, 1024), BF16), pltpu.VMEM((128, 512), F32)],
+        in_specs=[SMEM] + [VMEM] * 5 + [HBM],
+        out_specs=(VMEM, VMEM, VMEM),
+        scratch_shapes=[
+            pltpu.VMEM((1024, 1024), BF16),
+            pltpu.VMEM((128, 512), F32),
+            pltpu.VMEM((2 * TILES, 16, 128), BF16),
+            pltpu.SemaphoreType.DMA((2 * TILES,)),
+        ],
         compiler_params=grant(8),
         cost_estimate=pl.CostEstimate(flops=1 << 29, bytes_accessed=1 << 22, transcendentals=0),
         name="panel",
-    )(place, *tiles, two)
+    )(place, *tiles, thin)
 
 
 def settle_kernel(place, eps_occ, keep, got, eps_vir, mine, out, bmat):
@@ -259,22 +281,22 @@
         terms = block * (2.0 * block - block.T) / denominators
         out[m : m + 1, :] = jnp.sum(terms, axis=0, keepdims=True)
     here = pl.ds(pl.multiple_of(core * 16, 16), 16)
-    bmat[here, :] = mine[here, :]
+    bmat[here, :] = mine[...]
     there = pl.ds(pl.multiple_of((1 - core) * 16, 16), 16)
     for q in range(2):
         bmat[there, q * 1024 : q * 1024 + 1024] = got[32 + q * 16 : 48 + q * 16, :].astype(BF16)
 
 
-def settle(place, eps_occ, keep, got, eps_vir, two):
+def settle(place, eps_occ, keep, got, eps_vir, mine):
     return pl.pallas_call(
         settle_kernel,
-        out_shape=(jax.ShapeDtypeStruct((8, 128), F32), jax.ShapeDtypeStruct(two.shape, BF16)),
+        out_shape=(jax.ShapeDtypeStruct((8, 128), F32), jax.ShapeDtypeStruct((32, mine.shape[1]), BF16)),
         in_specs=[SMEM, SMEM, VMEM, VMEM, VMEM, VMEM],
         out_specs=(VMEM, VMEM),
         compiler_params=grant(4),
         cost_estimate=pl.CostEstimate(flops=1 << 28, bytes_accessed=1 << 20, transcendentals=0),
         name="settle",
-    )(place, eps_occ, keep, got, eps_vir.reshape(-1, 128), two)
+    )(place, eps_occ, keep, got, eps_vir.reshape(-1, 128), mine)
 
 
 def gram_kernel(place, here, below, above, low, high, sides, _, keep, give, wide, thin, all_t):
@@ -390,7 +412,7 @@
     place = position()
     sent = half_transform(c_occ, ints, blocks, screen)
     recv = lax.all_to_all(sent, GRP, 0, 0, tiled=True)
-    two, wide, thin = transform(recv, hold(c_vir))
+    wide, thin = transform(recv, hold(c_vir))
     here = lax.all_to_all(wide, ("zh", "zl", "yl", "yh"), 0, 0, tiled=True)
     up = [(i, (i + 1) % 4) for i in range(4)]
     down = [(i, (i + 3) % 4) for i in range(4)]
@@ -401,8 +423,8 @@
 
     swap = [(0, 1), (1, 0)]
     blocks = (here, below, above, low, high)
-    keep, give = panel(place, blocks, two)
-    selfs, bmat = settle(place, eps_occ, keep, lax.ppermute(give, "core", swap), eps_vir, two)
+    keep, give, mine = panel(place, blocks, thin)
+    selfs, bmat = settle(place, eps_occ, keep, lax.ppermute(give, "core", swap), eps_vir, mine)
     keep, give = gram(place, blocks, sides, selfs)
     got = lax.ppermute(give, "core", swap)
     scale = 1.0 / (float(vir) * float(vir) * 2048.0)

time: 142 us -> 143 us (level)
  Pallas kernels: 14.4 us -> 16.3 us
where the time goes in v13:
time: 143 us
  blocking collectives  59.2 us (41%)
  starting transfers between devices  43.6 us (30%)
  waiting for transfers between devices  22.6 us (16%)
  Pallas kernels  16.3 us (11%)
    all_to_all x1, blocking collectives, body(): here = lax.all_to_all(wide, ('zh', 'zl', 'yl', 'yh'), 0, 0, tiled=True)  28.4 us
    all_to_all x1, blocking collectives, body(): lax.all_to_all(small(again_kernel, (16, 1, 128), 'again')(energy), FAR, 0...  18 us
    all_to_all x1, blocking collectives, body(): energy = lax.all_to_all(energy, NEAR, 0, 0, tiled=True)  12.8 us
    all_to_all x1, starting transfers between devices, body(): sides = lax.all_to_all(thin, CHIPS, 0, 0, tiled=True)  10.7 us
    all_to_all x1, starting transfers between devices, body(): recv = lax.all_to_all(sent, GRP, 0, 0, tiled=True)  10.2 us
    ppermute x2, waiting for transfers between devices, body(): low, high = (lax.ppermute(low, 'x', down), lax.ppermute(high, 'x', up))  9.84 us
    all_to_all x1, waiting for transfers between devices, body(): recv = lax.all_to_all(sent, GRP, 0, 0, tiled=True)  9.32 us
    ppermute x2, starting transfers between devices, body(): below, above = (lax.ppermute(here, 'x', up), lax.ppermute(here, 'x', down))  6.48 us
  transfers between devices with their start and end apart: 8, of which 5 were waited for; matrix products, arithmetic and copies ran while one was open for 0% of the time, Pallas kernels for 4%

profile of v13, /device:TPU:1, one launch (start us, length us, event | category | flops | bytes accessed | tf_op | source)
XLA Modules:
  0.0 142.6 jit_solution(17254383602005487642)
XLA Ops:
  0.6 3.6 %half.1 = f32[8,72,128]{2,1,0:T(8,128)} custom-call(s32[2,4]{1,0:T(2,128)} %bitcast.31, s32[4]{0:T(128)} %screen_at.1, bf16[8,768]{1,0:T(8,128)(2,1)} %bitcast.30, bf16[4,32,4096]{2,1,0:T(8,128)(2,1)} %ints.1), custom_call_target="tpu_custom_call" | custom-call | tf_op jit(solution)/shard_map/half/pallas_call | solution.py:87
  4.2 10.2 %all-to-all-start = ((f32[8,72,128]{2,1,0:T(8,128)}), f32[8,72,128]{2,1,0:T(8,128)S(1)}, u32[]{:S(2)}, u32[]{:S(2)}) async-start(f32[8,72,128]{2,1,0:T(8,128)} %half.1), calls=%async_computation | async-start | bytes 589824 | tf_op jit(solution)/shard_map/all_to_all | solution.py:414
  14.4 1.9 %hold.1.c_vir = bf16[768,2048]{1,0:T(8,128)(2,1)S(1)} custom-call(bf16[768,2048]{1,0:T(8,128)(2,1)} %c_vir.1), custom_call_target="tpu_custom_call" | custom-call | flops 8589934592 | bytes 4194304 | tf_op jit(solution)/shard_map/hold/pallas_call | solution.py:113
  16.3 9.3 %all-to-all-done.recv = f32[8,72,128]{2,1,0:T(8,128)S(1)} async-done(((f32[8,72,128]{2,1,0:T(8,128)}), f32[8,72,128]{2,1,0:T(8,128)S(1)}, u32[]{:S(2)}, u32[]{:S(2)}) %all-to-all-start) | async-done | bytes 294944 | tf_op jit(solution)/shard_map/all_to_all | solution.py:414
  25.6 2.3 %transform.1 = (bf16[64,32,128]{2,1,0:T(8,128)(2,1)S(1)}, bf16[256,16,128]{2,1,0:T(8,128)(2,1)}) custom-call(f32[8,72,128]{2,1,0:T(8,128)S(1)} %all-to-all-done.recv, bf16[768,2048]{1,0:T(8,128)(2,1)S(1)} %hold.1.c_vir), custom_call_target="tpu_custom_call" | custom-call | tf_op jit(solution)/shard_map/transform/pallas_call | solution.py:173
  27.9 28.4 %all_to_all.25 = bf16[64,32,128]{2,1,0:T(8,128)(2,1)S(1)} all-to-all(bf16[64,32,128]{2,1,0:T(8,128)(2,1)S(1)} %get-tuple-element.13), channel_id=1, replica_groups=mesh['zh'=4,'zl'=2,'x'=4,'yl'=2,'yh'=4,'core'=2] {'zh','zl','yl','yh'}, dimensions={0} | all-to-all | bytes 1048576 | tf_op jit(solution)/shard_map/all_to_all | solution.py:416
  56.3 3.1 %collective-permute-start = (bf16[64,32,128]{2,1,0:T(8,128)(2,1)S(1)}, bf16[64,32,128]{2,1,0:T(8,128)(2,1)S(1)}, u32[]{:S(2)}, u32[]{:S(2)}) collective-permute-start(bf16[64,32,128]{2,1,0:T(8,128)(2,1)S(1)} %all_to_all.25), channel_id=1, source_target_pairs={{0,16},{16,32},{32,48},{48,0},{1,17},{17,33},{33,49},{49,1},{2,18}... | collective-permute-start | bytes 1572872 | tf_op jit(solution)/shard_map/ppermute | solution.py:419
  59.5 3.4 %collective-permute-start.1 = (bf16[64,32,128]{2,1,0:T(8,128)(2,1)S(1)}, bf16[64,32,128]{2,1,0:T(8,128)(2,1)S(1)}, u32[]{:S(2)}, u32[]{:S(2)}) collective-permute-start(bf16[64,32,128]{2,1,0:T(8,128)(2,1)S(1)} %all_to_all.25), channel_id=1, source_target_pairs={{0,48},{16,0},{32,16},{48,32},{1,49},{17,1},{33,17},{49,33},{2,50}... | collective-permute-start | bytes 1572872 | tf_op jit(solution)/shard_map/ppermute | solution.py:419
  62.8 10.7 %all-to-all-start.2 = ((bf16[256,16,128]{2,1,0:T(8,128)(2,1)}), bf16[256,16,128]{2,1,0:T(8,128)(2,1)S(1)}, u32[]{:S(2)}, u32[]{:S(2)}) async-start(bf16[256,16,128]{2,1,0:T(8,128)(2,1)} %get-tuple-element.16.thin), calls=%async_computation.2 | async-start | bytes 2097152 | tf_op jit(solution)/shard_map/all_to_all | solution.py:422
  73.5 0.0 collective-permute-done.below
  73.5 0.0 collective-permute-done.1.above
  73.5 0.8 onward.1
  74.3 0.0 copy-start
  74.3 0.0 copy-start.1
  74.3 3.0 %collective-permute-start.2 = (bf16[32,32,128]{2,1,0:T(8,128)(2,1)}, bf16[32,32,128]{2,1,0:T(8,128)(2,1)S(1)}, u32[]{:S(2)}, u32[]{:S(2)}) collective-permute-start(bf16[32,32,128]{2,1,0:T(8,128)(2,1)} %get-tuple-element.14), channel_id=1, source_target_pairs={{0,48},{16,0},{32,16},{48,32},{1,49},{17,1},{33,17},{49,33},{2,50}... | collective-permute-start | bytes 786440 | tf_op jit(solution)/shard_map/ppermute | solution.py:421
  77.3 2.4 %collective-permute-start.3 = (bf16[32,32,128]{2,1,0:T(8,128)(2,1)S(1)}, bf16[32,32,128]{2,1,0:T(8,128)(2,1)S(1)}, u32[]{:S(2)}, u32[]{:S(2)}) collective-permute-start(bf16[32,32,128]{2,1,0:T(8,128)(2,1)S(1)} %get-tuple-element.15), channel_id=1, source_target_pairs={{0,16},{16,32},{32,48},{48,0},{1,17},{17,33},{33,49},{49,1},{2,18}... | collective-permute-start | bytes 786440 | tf_op jit(solution)/shard_map/ppermute | solution.py:421
  79.7 0.1 stack.31.place
  79.8 6.9 %collective-permute-done.2 = bf16[32,32,128]{2,1,0:T(8,128)(2,1)S(1)} collective-permute-done((bf16[32,32,128]{2,1,0:T(8,128)(2,1)}, bf16[32,32,128]{2,1,0:T(8,128)(2,1)S(1)}, u32[]{:S(2)}, u32[]{:S(2)}) %collective-permute-start.2) | collective-permute-done | bytes 262176 | tf_op jit(solution)/shard_map/ppermute | solution.py:421
  86.7 3.0 %collective-permute-done.3 = bf16[32,32,128]{2,1,0:T(8,128)(2,1)S(1)} collective-permute-done((bf16[32,32,128]{2,1,0:T(8,128)(2,1)S(1)}, bf16[32,32,128]{2,1,0:T(8,128)(2,1)S(1)}, u32[]{:S(2)}, u32[]{:S(2)}) %collective-permute-start.3) | collective-permute-done | bytes 262176 | tf_op jit(solution)/shard_map/ppermute | solution.py:421
  89.7 2.5 %panel.1 = (f32[32,1024]{1,0:T(8,128)S(1)}, f32[64,1024]{1,0:T(8,128)S(1)}, bf16[16,2048]{1,0:T(8,128)(2,1)S(1)}) custom-call(s32[7]{0:T(128)S(1)} %stack.31.place, bf16[16,8,16,128]{3,2,1,0:T(8,128)(2,1)S(1)} %bitcast.17, bf16[16,8,16,128]{3,2,1,0:T(8,128)(2,1)S(1)} %bitcast.20, bf16[16,8,16,128]{3,2,1,0:T(8,128)(2,1)S(1)} %bitcast.22, ...), custom_call_target="tpu_custom_call" | custom-call | flops 536870912 | bytes 4194304 | tf_op jit(solution)/shard_map/panel/pallas_call | solution.py:244
  92.1 6.0 %collective-permute-start.4 = (f32[64,1024]{1,0:T(8,128)S(1)}, f32[64,1024]{1,0:T(8,128)S(1)}, u32[]{:S(2)}, u32[]{:S(2)}) collective-permute-start(f32[64,1024]{1,0:T(8,128)S(1)} %get-tuple-element.18), channel_id=1, source_target_pairs={{0,1},{1,0},{2,3},{3,2},{4,5},{5,4},{6,7},{7,6},{8,9},{9,8},{10,11... | collective-permute-start | bytes 786440 | tf_op jit(solution)/shard_map/ppermute | solution.py:427
  98.1 1.1 collective-permute-done.4.got
  99.3 0.0 copy-done
  99.3 0.0 copy-done.1
  99.3 1.2 settle.1
  100.5 0.0 all-to-all-done.2
  100.5 2.4 %gram.1 = (f32[256,1024]{1,0:T(8,128)S(1)}, f32[256,1024]{1,0:T(8,128)S(1)}) custom-call(s32[7]{0:T(128)S(1)} %stack.31.place, bf16[16,8,16,128]{3,2,1,0:T(8,128)(2,1)S(1)} %bitcast.18, bf16[16,8,16,128]{3,2,1,0:T(8,128)(2,1)S(1)} %bitcast.21, bf16[16,8,16,128]{3,2,1,0:T(8,128)(2,1)S(1)} %bitcast.23, bf16[8,8,16,128]{3,2,1,0:T(8,128)(2,1)S(1)} %bitcast.25, ...), custom_call_target="tpu_custom_call" | custom-call | tf_op jit(solution)/shard_map/gram/pallas_call | solution.py:326
  102.9 4.9 %collective-permute-start.5 = (f32[256,1024]{1,0:T(8,128)S(1)}, f32[256,1024]{1,0:T(8,128)S(1)}, u32[]{:S(2)}, u32[]{:S(2)}) collective-permute-start(f32[256,1024]{1,0:T(8,128)S(1)} %get-tuple-element.23), channel_id=1, source_target_pairs={{0,1},{1,0},{2,3},{3,2},{4,5},{5,4},{6,7},{7,6},{8,9},{9,8},{10,11... | collective-permute-start | bytes 3145736 | tf_op jit(solution)/shard_map/ppermute | solution.py:429
  107.8 2.3 %collective-permute-done.5.got = f32[256,1024]{1,0:T(8,128)S(1)} collective-permute-done((f32[256,1024]{1,0:T(8,128)S(1)}, f32[256,1024]{1,0:T(8,128)S(1)}, u32[]{:S(2)}, u32[]{:S(2)}) %collective-permute-start.5) | collective-permute-done | bytes 1048608 | tf_op jit(solution)/shard_map/ppermute | solution.py:429
  110.1 0.9 energies.1
  111.0 12.8 %all_to_all.26.got = f32[32,1,128]{2,1,0:T(1,128)S(1)} all-to-all(f32[32,1,128]{2,1,0:T(1,128)S(1)} %energies.1), channel_id=1, replica_groups=mesh['zh'=4,'zl'=2,'x'=4,'yl'=2,'yh'=4,'core'=2] {'zl','x','yl','core'}, dimensions={0} | all-to-all | bytes 32768 | tf_op jit(solution)/shard_map/all_to_all | solution.py:432
  123.9 18.0 %all_to_all.27.got = f32[16,1,128]{2,1,0:T(1,128)S(1)} all-to-all(f32[16,1,128]{2,1,0:T(1,128)S(1)} %again.1), channel_id=1, replica_groups=mesh['zh'=4,'zl'=2,'x'=4,'yl'=2,'yh'=4,'core'=2] {'zh','yh'}, dimensions={0} | all-to-all | bytes 16384 | tf_op jit(solution)/shard_map/all_to_all | solution.py:433
  141.9 0.7 last.1
  (1 shorter events, 0.0 us)
Async XLA Ops:
  4.2 21.4 %all-to-all-start = ((f32[8,72,128]{2,1,0:T(8,128)}), f32[8,72,128]{2,1,0:T(8,128)S(1)}, u32[]{:S(2)}, u32[]{:S(2)}) async-start(f32[8,72,128]{2,1,0:T(8,128)} %half.1), calls=%async_computation | async-start | bytes 589824 | tf_op jit(solution)/shard_map/all_to_all | solution.py:414
  56.3 17.2 %collective-permute-start = (bf16[64,32,128]{2,1,0:T(8,128)(2,1)S(1)}, bf16[64,32,128]{2,1,0:T(8,128)(2,1)S(1)}, u32[]{:S(2)}, u32[]{:S(2)}) collective-permute-start(bf16[64,32,128]{2,1,0:T(8,128)(2,1)S(1)} %all_to_all.25), channel_id=1, source_target_pairs={{0,16},{16,32},{32,48},{48,0},{1,17},{17,33},{33,49},{49,1},{2,18}... | collective-permute-start | bytes 1572872 | tf_op jit(solution)/shard_map/ppermute | solution.py:419
  59.5 14.1 %collective-permute-start.1 = (bf16[64,32,128]{2,1,0:T(8,128)(2,1)S(1)}, bf16[64,32,128]{2,1,0:T(8,128)(2,1)S(1)}, u32[]{:S(2)}, u32[]{:S(2)}) collective-permute-start(bf16[64,32,128]{2,1,0:T(8,128)(2,1)S(1)} %all_to_all.25), channel_id=1, source_target_pairs={{0,48},{16,0},{32,16},{48,32},{1,49},{17,1},{33,17},{49,33},{2,50}... | collective-permute-start | bytes 1572872 | tf_op jit(solution)/shard_map/ppermute | solution.py:419
  62.8 37.7 %all-to-all-start.2 = ((bf16[256,16,128]{2,1,0:T(8,128)(2,1)}), bf16[256,16,128]{2,1,0:T(8,128)(2,1)S(1)}, u32[]{:S(2)}, u32[]{:S(2)}) async-start(bf16[256,16,128]{2,1,0:T(8,128)(2,1)} %get-tuple-element.16.thin), calls=%async_computation.2 | async-start | bytes 2097152 | tf_op jit(solution)/shard_map/all_to_all | solution.py:422
  74.3 25.0 %copy-start = (f32[2048]{0:T(1024)S(1)}, f32[2048]{0:T(1024)}, u32[]{:S(2)}) copy-start(f32[2048]{0:T(1024)} %param.13) | copy-start | bytes 24580
  74.3 25.0 %copy-start.1 = (f32[8]{0:T(128)S(1)}, f32[8]{0:T(128)}, u32[]{:S(2)}) copy-start(f32[8]{0:T(128)} %eps_occ.3) | copy-start | bytes 100
  74.3 12.4 %collective-permute-start.2 = (bf16[32,32,128]{2,1,0:T(8,128)(2,1)}, bf16[32,32,128]{2,1,0:T(8,128)(2,1)S(1)}, u32[]{:S(2)}, u32[]{:S(2)}) collective-permute-start(bf16[32,32,128]{2,1,0:T(8,128)(2,1)} %get-tuple-element.14), channel_id=1, source_target_pairs={{0,48},{16,0},{32,16},{48,32},{1,49},{17,1},{33,17},{49,33},{2,50}... | collective-permute-start | bytes 786440 | tf_op jit(solution)/shard_map/ppermute | solution.py:421
  77.3 12.4 %collective-permute-start.3 = (bf16[32,32,128]{2,1,0:T(8,128)(2,1)S(1)}, bf16[32,32,128]{2,1,0:T(8,128)(2,1)S(1)}, u32[]{:S(2)}, u32[]{:S(2)}) collective-permute-start(bf16[32,32,128]{2,1,0:T(8,128)(2,1)S(1)} %get-tuple-element.15), channel_id=1, source_target_pairs={{0,16},{16,32},{32,48},{48,0},{1,17},{17,33},{33,49},{49,1},{2,18}... | collective-permute-start | bytes 786440 | tf_op jit(solution)/shard_map/ppermute | solution.py:421
  92.1 7.1 %collective-permute-start.4 = (f32[64,1024]{1,0:T(8,128)S(1)}, f32[64,1024]{1,0:T(8,128)S(1)}, u32[]{:S(2)}, u32[]{:S(2)}) collective-permute-start(f32[64,1024]{1,0:T(8,128)S(1)} %get-tuple-element.18), channel_id=1, source_target_pairs={{0,1},{1,0},{2,3},{3,2},{4,5},{5,4},{6,7},{7,6},{8,9},{9,8},{10,11... | collective-permute-start | bytes 786440 | tf_op jit(solution)/shard_map/ppermute | solution.py:427
  102.9 7.2 %collective-permute-start.5 = (f32[256,1024]{1,0:T(8,128)S(1)}, f32[256,1024]{1,0:T(8,128)S(1)}, u32[]{:S(2)}, u32[]{:S(2)}) collective-permute-start(f32[256,1024]{1,0:T(8,128)S(1)} %get-tuple-element.23), channel_id=1, source_target_pairs={{0,1},{1,0},{2,3},{3,2},{4,5},{5,4},{6,7},{7,6},{8,9},{9,8},{10,11... | collective-permute-start | bytes 3145736 | tf_op jit(solution)/shard_map/ppermute | solution.py:429

commit v14 on v10

--- a/solution.py
+++ b/solution.py
@@ -208,11 +208,11 @@
     first = 0
     for tiles in (here, below, above, low, high):
         count = tiles.shape[0] * 16
-        for i in range(8):
-            wide[first : first + count, i * 128 : i * 128 + 128] = tiles[:, i].reshape(count, 128)
+        wide[first : first + count, 512:640] = tiles[:, own].reshape(count, 128)
+        for m in range(4):
+            wide[first : first + count, m * 128 : m * 128 + 128] = tiles[:, side * 4 + m].reshape(count, 128)
         first += count
-    mine = wide[:, pl.ds(pl.multiple_of(own * 128, 128), 128)]
-    others = wide[:, pl.ds(pl.multiple_of(side * 512, 512), 512)]
+    mine, others = wide[:, 512:640], wide[:, 0:512]
     all_s[...] = lax.dot_general(mine, others, TRANSPOSED, preferred_element_type=F32)
     for which, target in ((core, keep), (1 - core, give)):
         at = pl.multiple_of(which * 256, 256)
@@ -233,7 +233,7 @@
         ),
         in_specs=[SMEM] + [VMEM] * 6,
         out_specs=(VMEM, VMEM),
-        scratch_shapes=[pltpu.VMEM((1024, 1024), BF16), pltpu.VMEM((128, 512), F32)],
+        scratch_shapes=[pltpu.VMEM((1024, 640), BF16), pltpu.VMEM((128, 512), F32)],
         compiler_params=grant(8),
         cost_estimate=pl.CostEstimate(flops=1 << 29, bytes_accessed=1 << 22, transcendentals=0),
         name="panel",

time: 142 us -> 142 us (level)
  no operation moved by 1% of the time
where the time goes in v14:
time: 142 us; the launch traced here: 141 us
  blocking collectives  57.9 us (41%)
  starting transfers between devices  44.4 us (31%)
  waiting for transfers between devices  23.1 us (16%)
  Pallas kernels  14 us (10%)
    all_to_all x1, blocking collectives, body(): here = lax.all_to_all(wide, ('zh', 'zl', 'yl', 'yh'), 0, 0, tiled=True)  28.4 us
    all_to_all x1, blocking collectives, body(): lax.all_to_all(small(again_kernel, (16, 1, 128), 'again')(energy), FAR, 0...  16.7 us
    all_to_all x1, blocking collectives, body(): energy = lax.all_to_all(energy, NEAR, 0, 0, tiled=True)  12.8 us
    all_to_all x1, starting transfers between devices, body(): sides = lax.all_to_all(thin, CHIPS, 0, 0, tiled=True)  10.7 us
    ppermute x2, waiting for transfers between devices, body(): low, high = (lax.ppermute(low, 'x', down), lax.ppermute(high, 'x', up))  10.4 us
    all_to_all x1, starting transfers between devices, body(): recv = lax.all_to_all(sent, GRP, 0, 0, tiled=True)  10.2 us
    all_to_all x1, waiting for transfers between devices, body(): recv = lax.all_to_all(sent, GRP, 0, 0, tiled=True)  9.32 us
    ppermute x2, starting transfers between devices, body(): below, above = (lax.ppermute(here, 'x', up), lax.ppermute(here, 'x', down))  6.48 us
  transfers between devices with their start and end apart: 8, of which 5 were waited for; matrix products, arithmetic and copies ran while one was open for 0% of the time, Pallas kernels for 4%

profile of v14, /device:TPU:1, one launch (start us, length us, event | category | flops | bytes accessed | tf_op | source)
XLA Modules:
  0.0 141.0 jit_solution(3469641194750003578)
XLA Ops:
  0.6 3.6 %half.1 = f32[8,72,128]{2,1,0:T(8,128)} custom-call(s32[2,4]{1,0:T(2,128)} %bitcast.31, s32[4]{0:T(128)} %screen_at.1, bf16[8,768]{1,0:T(8,128)(2,1)} %bitcast.30, bf16[4,32,4096]{2,1,0:T(8,128)(2,1)} %ints.1), custom_call_target="tpu_custom_call" | custom-call | tf_op jit(solution)/shard_map/half/pallas_call | solution.py:87
  4.2 10.2 %all-to-all-start = ((f32[8,72,128]{2,1,0:T(8,128)}), f32[8,72,128]{2,1,0:T(8,128)S(1)}, u32[]{:S(2)}, u32[]{:S(2)}) async-start(f32[8,72,128]{2,1,0:T(8,128)} %half.1), calls=%async_computation | async-start | bytes 589824 | tf_op jit(solution)/shard_map/all_to_all | solution.py:392
  14.4 1.9 %hold.1.c_vir = bf16[768,2048]{1,0:T(8,128)(2,1)S(1)} custom-call(bf16[768,2048]{1,0:T(8,128)(2,1)} %c_vir.1), custom_call_target="tpu_custom_call" | custom-call | flops 8589934592 | bytes 4194304 | tf_op jit(solution)/shard_map/hold/pallas_call | solution.py:113
  16.3 9.3 %all-to-all-done.recv = f32[8,72,128]{2,1,0:T(8,128)S(1)} async-done(((f32[8,72,128]{2,1,0:T(8,128)}), f32[8,72,128]{2,1,0:T(8,128)S(1)}, u32[]{:S(2)}, u32[]{:S(2)}) %all-to-all-start) | async-done | bytes 294944 | tf_op jit(solution)/shard_map/all_to_all | solution.py:392
  25.6 1.3 transform.1
  27.0 0.0 copy-start.1
  27.0 0.6 copy-done.1
  27.6 0.0 copy-start
  27.6 28.4 %all_to_all.25 = bf16[64,32,128]{2,1,0:T(8,128)(2,1)S(1)} all-to-all(bf16[64,32,128]{2,1,0:T(8,128)(2,1)S(1)} %get-tuple-element.13), channel_id=1, replica_groups=mesh['zh'=4,'zl'=2,'x'=4,'yl'=2,'yh'=4,'core'=2] {'zh','zl','yl','yh'}, dimensions={0} | all-to-all | bytes 1048576 | tf_op jit(solution)/shard_map/all_to_all | solution.py:394
  56.0 3.1 %collective-permute-start = (bf16[64,32,128]{2,1,0:T(8,128)(2,1)S(1)}, bf16[64,32,128]{2,1,0:T(8,128)(2,1)S(1)}, u32[]{:S(2)}, u32[]{:S(2)}) collective-permute-start(bf16[64,32,128]{2,1,0:T(8,128)(2,1)S(1)} %all_to_all.25), channel_id=1, source_target_pairs={{0,16},{16,32},{32,48},{48,0},{1,17},{17,33},{33,49},{49,1},{2,18}... | collective-permute-start | bytes 1572872 | tf_op jit(solution)/shard_map/ppermute | solution.py:397
  59.1 3.4 %collective-permute-start.1 = (bf16[64,32,128]{2,1,0:T(8,128)(2,1)S(1)}, bf16[64,32,128]{2,1,0:T(8,128)(2,1)S(1)}, u32[]{:S(2)}, u32[]{:S(2)}) collective-permute-start(bf16[64,32,128]{2,1,0:T(8,128)(2,1)S(1)} %all_to_all.25), channel_id=1, source_target_pairs={{0,48},{16,0},{32,16},{48,32},{1,49},{17,1},{33,17},{49,33},{2,50}... | collective-permute-start | bytes 1572872 | tf_op jit(solution)/shard_map/ppermute | solution.py:397
  62.5 0.0 copy-done
  62.5 10.7 %all-to-all-start.2 = ((bf16[256,16,128]{2,1,0:T(8,128)(2,1)}), bf16[256,16,128]{2,1,0:T(8,128)(2,1)S(1)}, u32[]{:S(2)}, u32[]{:S(2)}) async-start(bf16[256,16,128]{2,1,0:T(8,128)(2,1)} %copy-done), calls=%async_computation.2 | async-start | bytes 2097152 | tf_op jit(solution)/shard_map/all_to_all | solution.py:400
  73.2 0.0 copy-start.2
  73.2 0.0 copy-start.3
  73.2 0.0 copy-start.4
  73.2 0.0 collective-permute-done.below
  73.3 0.0 collective-permute-done.1.above
  73.3 0.9 onward.1
  74.1 2.8 %collective-permute-start.2 = (bf16[32,32,128]{2,1,0:T(8,128)(2,1)}, bf16[32,32,128]{2,1,0:T(8,128)(2,1)S(1)}, u32[]{:S(2)}, u32[]{:S(2)}) collective-permute-start(bf16[32,32,128]{2,1,0:T(8,128)(2,1)} %get-tuple-element.14), channel_id=1, source_target_pairs={{0,48},{16,0},{32,16},{48,32},{1,49},{17,1},{33,17},{49,33},{2,50}... | collective-permute-start | bytes 786440 | tf_op jit(solution)/shard_map/ppermute | solution.py:399
  77.0 2.4 %collective-permute-start.3 = (bf16[32,32,128]{2,1,0:T(8,128)(2,1)}, bf16[32,32,128]{2,1,0:T(8,128)(2,1)S(1)}, u32[]{:S(2)}, u32[]{:S(2)}) collective-permute-start(bf16[32,32,128]{2,1,0:T(8,128)(2,1)} %get-tuple-element.15), channel_id=1, source_target_pairs={{0,16},{16,32},{32,48},{48,0},{1,17},{17,33},{33,49},{49,1},{2,18}... | collective-permute-start | bytes 786440 | tf_op jit(solution)/shard_map/ppermute | solution.py:399
  79.4 0.1 stack.31.place
  79.5 6.9 %collective-permute-done.2 = bf16[32,32,128]{2,1,0:T(8,128)(2,1)S(1)} collective-permute-done((bf16[32,32,128]{2,1,0:T(8,128)(2,1)}, bf16[32,32,128]{2,1,0:T(8,128)(2,1)S(1)}, u32[]{:S(2)}, u32[]{:S(2)}) %collective-permute-start.2) | collective-permute-done | bytes 262176 | tf_op jit(solution)/shard_map/ppermute | solution.py:399
  86.4 3.5 %collective-permute-done.3 = bf16[32,32,128]{2,1,0:T(8,128)(2,1)S(1)} collective-permute-done((bf16[32,32,128]{2,1,0:T(8,128)(2,1)}, bf16[32,32,128]{2,1,0:T(8,128)(2,1)S(1)}, u32[]{:S(2)}, u32[]{:S(2)}) %collective-permute-start.3) | collective-permute-done | bytes 262176 | tf_op jit(solution)/shard_map/ppermute | solution.py:399
  89.9 0.0 copy-done.2
  89.9 1.1 panel.1
  91.0 5.6 %collective-permute-start.4 = (f32[64,1024]{1,0:T(8,128)S(1)}, f32[64,1024]{1,0:T(8,128)S(1)}, u32[]{:S(2)}, u32[]{:S(2)}) collective-permute-start(f32[64,1024]{1,0:T(8,128)S(1)} %get-tuple-element.18), channel_id=1, source_target_pairs={{0,1},{1,0},{2,3},{3,2},{4,5},{5,4},{6,7},{7,6},{8,9},{9,8},{10,11... | collective-permute-start | bytes 786440 | tf_op jit(solution)/shard_map/ppermute | solution.py:405
  96.6 1.1 collective-permute-done.4.got
  97.7 0.0 copy-done.3
  97.7 0.0 copy-done.4
  97.7 1.2 settle.1
  99.0 0.0 all-to-all-done.2
  99.0 2.4 %gram.1 = (f32[256,1024]{1,0:T(8,128)S(1)}, f32[256,1024]{1,0:T(8,128)S(1)}) custom-call(s32[7]{0:T(128)S(1)} %stack.31.place, bf16[16,8,16,128]{3,2,1,0:T(8,128)(2,1)S(1)} %bitcast.18, bf16[16,8,16,128]{3,2,1,0:T(8,128)(2,1)S(1)} %bitcast.21, bf16[16,8,16,128]{3,2,1,0:T(8,128)(2,1)S(1)} %bitcast.23, bf16[8,8,16,128]{3,2,1,0:T(8,128)(2,1)S(1)} %bitcast.25, ...), custom_call_target="tpu_custom_call" | custom-call | tf_op jit(solution)/shard_map/gram/pallas_call | solution.py:304
  101.4 6.1 %collective-permute-start.5 = (f32[256,1024]{1,0:T(8,128)S(1)}, f32[256,1024]{1,0:T(8,128)S(1)}, u32[]{:S(2)}, u32[]{:S(2)}) collective-permute-start(f32[256,1024]{1,0:T(8,128)S(1)} %get-tuple-element.23), channel_id=1, source_target_pairs={{0,1},{1,0},{2,3},{3,2},{4,5},{5,4},{6,7},{7,6},{8,9},{9,8},{10,11... | collective-permute-start | bytes 3145736 | tf_op jit(solution)/shard_map/ppermute | solution.py:407
  107.5 2.3 %collective-permute-done.5.got = f32[256,1024]{1,0:T(8,128)S(1)} collective-permute-done((f32[256,1024]{1,0:T(8,128)S(1)}, f32[256,1024]{1,0:T(8,128)S(1)}, u32[]{:S(2)}, u32[]{:S(2)}) %collective-permute-start.5) | collective-permute-done | bytes 1048608 | tf_op jit(solution)/shard_map/ppermute | solution.py:407
  109.8 0.9 energies.1
  110.7 12.8 %all_to_all.26.got = f32[32,1,128]{2,1,0:T(1,128)S(1)} all-to-all(f32[32,1,128]{2,1,0:T(1,128)S(1)} %energies.1), channel_id=1, replica_groups=mesh['zh'=4,'zl'=2,'x'=4,'yl'=2,'yh'=4,'core'=2] {'zl','x','yl','core'}, dimensions={0} | all-to-all | bytes 32768 | tf_op jit(solution)/shard_map/all_to_all | solution.py:410
  123.6 16.7 %all_to_all.27.got = f32[16,1,128]{2,1,0:T(1,128)S(1)} all-to-all(f32[16,1,128]{2,1,0:T(1,128)S(1)} %again.1), channel_id=1, replica_groups=mesh['zh'=4,'zl'=2,'x'=4,'yl'=2,'yh'=4,'core'=2] {'zh','yh'}, dimensions={0} | all-to-all | bytes 16384 | tf_op jit(solution)/shard_map/all_to_all | solution.py:411
  140.3 0.7 last.1
  (1 shorter events, 0.0 us)
Async XLA Ops:
  4.2 21.4 %all-to-all-start = ((f32[8,72,128]{2,1,0:T(8,128)}), f32[8,72,128]{2,1,0:T(8,128)S(1)}, u32[]{:S(2)}, u32[]{:S(2)}) async-start(f32[8,72,128]{2,1,0:T(8,128)} %half.1), calls=%async_computation | async-start | bytes 589824 | tf_op jit(solution)/shard_map/all_to_all | solution.py:392
  27.0 0.7 copy-start.1
  27.6 34.9 %copy-start = (bf16[256,16,128]{2,1,0:T(8,128)(2,1)}, bf16[256,16,128]{2,1,0:T(8,128)(2,1)S(1)}, u32[]{:S(2)}) copy-start(bf16[256,16,128]{2,1,0:T(8,128)(2,1)S(1)} %get-tuple-element.20) | copy-start | bytes 3145732
  56.0 17.2 %collective-permute-start = (bf16[64,32,128]{2,1,0:T(8,128)(2,1)S(1)}, bf16[64,32,128]{2,1,0:T(8,128)(2,1)S(1)}, u32[]{:S(2)}, u32[]{:S(2)}) collective-permute-start(bf16[64,32,128]{2,1,0:T(8,128)(2,1)S(1)} %all_to_all.25), channel_id=1, source_target_pairs={{0,16},{16,32},{32,48},{48,0},{1,17},{17,33},{33,49},{49,1},{2,18}... | collective-permute-start | bytes 1572872 | tf_op jit(solution)/shard_map/ppermute | solution.py:397
  59.1 14.1 %collective-permute-start.1 = (bf16[64,32,128]{2,1,0:T(8,128)(2,1)S(1)}, bf16[64,32,128]{2,1,0:T(8,128)(2,1)S(1)}, u32[]{:S(2)}, u32[]{:S(2)}) collective-permute-start(bf16[64,32,128]{2,1,0:T(8,128)(2,1)S(1)} %all_to_all.25), channel_id=1, source_target_pairs={{0,48},{16,0},{32,16},{48,32},{1,49},{17,1},{33,17},{49,33},{2,50}... | collective-permute-start | bytes 1572872 | tf_op jit(solution)/shard_map/ppermute | solution.py:397
  62.5 36.4 %all-to-all-start.2 = ((bf16[256,16,128]{2,1,0:T(8,128)(2,1)}), bf16[256,16,128]{2,1,0:T(8,128)(2,1)S(1)}, u32[]{:S(2)}, u32[]{:S(2)}) async-start(bf16[256,16,128]{2,1,0:T(8,128)(2,1)} %copy-done), calls=%async_computation.2 | async-start | bytes 2097152 | tf_op jit(solution)/shard_map/all_to_all | solution.py:400
  73.2 16.7 %copy-start.2 = (bf16[32,2048]{1,0:T(8,128)(2,1)S(1)}, bf16[32,2048]{1,0:T(8,128)(2,1)}, u32[]{:S(2)}) copy-start(bf16[32,2048]{1,0:T(8,128)(2,1)} %copy-done.1) | copy-start | bytes 393220
  73.2 24.5 %copy-start.3 = (f32[2048]{0:T(1024)S(1)}, f32[2048]{0:T(1024)}, u32[]{:S(2)}) copy-start(f32[2048]{0:T(1024)} %param.13) | copy-start | bytes 24580
  73.2 24.5 %copy-start.4 = (f32[8]{0:T(128)S(1)}, f32[8]{0:T(128)}, u32[]{:S(2)}) copy-start(f32[8]{0:T(128)} %eps_occ.3) | copy-start | bytes 100
  74.1 12.3 %collective-permute-start.2 = (bf16[32,32,128]{2,1,0:T(8,128)(2,1)}, bf16[32,32,128]{2,1,0:T(8,128)(2,1)S(1)}, u32[]{:S(2)}, u32[]{:S(2)}) collective-permute-start(bf16[32,32,128]{2,1,0:T(8,128)(2,1)} %get-tuple-element.14), channel_id=1, source_target_pairs={{0,48},{16,0},{32,16},{48,32},{1,49},{17,1},{33,17},{49,33},{2,50}... | collective-permute-start | bytes 786440 | tf_op jit(solution)/shard_map/ppermute | solution.py:399
  77.0 12.9 %collective-permute-start.3 = (bf16[32,32,128]{2,1,0:T(8,128)(2,1)}, bf16[32,32,128]{2,1,0:T(8,128)(2,1)S(1)}, u32[]{:S(2)}, u32[]{:S(2)}) collective-permute-start(bf16[32,32,128]{2,1,0:T(8,128)(2,1)} %get-tuple-element.15), channel_id=1, source_target_pairs={{0,16},{16,32},{32,48},{48,0},{1,17},{17,33},{33,49},{49,1},{2,18}... | collective-permute-start | bytes 786440 | tf_op jit(solution)/shard_map/ppermute | solution.py:399
  91.0 6.7 %collective-permute-start.4 = (f32[64,1024]{1,0:T(8,128)S(1)}, f32[64,1024]{1,0:T(8,128)S(1)}, u32[]{:S(2)}, u32[]{:S(2)}) collective-permute-start(f32[64,1024]{1,0:T(8,128)S(1)} %get-tuple-element.18), channel_id=1, source_target_pairs={{0,1},{1,0},{2,3},{3,2},{4,5},{5,4},{6,7},{7,6},{8,9},{9,8},{10,11... | collective-permute-start | bytes 786440 | tf_op jit(solution)/shard_map/ppermute | solution.py:405
  101.4 8.4 %collective-permute-start.5 = (f32[256,1024]{1,0:T(8,128)S(1)}, f32[256,1024]{1,0:T(8,128)S(1)}, u32[]{:S(2)}, u32[]{:S(2)}) collective-permute-start(f32[256,1024]{1,0:T(8,128)S(1)} %get-tuple-element.23), channel_id=1, source_target_pairs={{0,1},{1,0},{2,3},{3,2},{4,5},{5,4},{6,7},{7,6},{8,9},{9,8},{10,11... | collective-permute-start | bytes 3145736 | tf_op jit(solution)/shard_map/ppermute | solution.py:407

commit v15 on v14

--- a/solution.py
+++ b/solution.py
@@ -402,8 +402,9 @@
     swap = [(0, 1), (1, 0)]
     blocks = (here, below, above, low, high)
     keep, give = panel(place, blocks, two)
-    selfs, bmat = settle(place, eps_occ, keep, lax.ppermute(give, "core", swap), eps_vir, two)
-    keep, give = gram(place, blocks, sides, selfs)
+    other = lax.ppermute(give, "core", swap)
+    selfs, bmat = settle(place, eps_occ, keep, other, eps_vir, two)
+    keep, give = gram(place, blocks, sides, other)
     got = lax.ppermute(give, "core", swap)
     scale = 1.0 / (float(vir) * float(vir) * 2048.0)
     energy = energies(scale, place, eps_occ, keep, got, eps_vir, selfs)

time: 142 us -> 141 us (level)
  transfers between devices with their start and end apart: 8 -> 8, of which waited for: 5 -> 6; matrix products, arithmetic and copies ran while one was open for 0% -> 0% of each run, Pallas kernels for 4% -> 4%
where the time goes in v15:
time: 141 us; the launch traced here: 140 us
  blocking collectives  57.2 us (41%)
  starting transfers between devices  45.1 us (32%)
  waiting for transfers between devices  21.8 us (15%)
  Pallas kernels  13.9 us (10%)
  local copies, waits for them, and re-layouts  1.41 us (1%)
    all_to_all x1, blocking collectives, body(): here = lax.all_to_all(wide, ('zh', 'zl', 'yl', 'yh'), 0, 0, tiled=True)  28.4 us
    all_to_all x1, blocking collectives, body(): lax.all_to_all(small(again_kernel, (16, 1, 128), 'again')(energy), FAR, 0...  16 us
    all_to_all x1, blocking collectives, body(): energy = lax.all_to_all(energy, NEAR, 0, 0, tiled=True)  12.8 us
    all_to_all x1, starting transfers between devices, body(): sides = lax.all_to_all(thin, CHIPS, 0, 0, tiled=True)  10.7 us
    all_to_all x1, starting transfers between devices, body(): recv = lax.all_to_all(sent, GRP, 0, 0, tiled=True)  10.2 us
    ppermute x2, waiting for transfers between devices, body(): low, high = (lax.ppermute(low, 'x', down), lax.ppermute(high, 'x', up))  9.77 us
    all_to_all x1, waiting for transfers between devices, body(): recv = lax.all_to_all(sent, GRP, 0, 0, tiled=True)  9.32 us
    ppermute x2, starting transfers between devices, body(): below, above = (lax.ppermute(here, 'x', up), lax.ppermute(here, 'x', down))  6.48 us
  transfers between devices with their start and end apart: 8, of which 6 were waited for; matrix products, arithmetic and copies ran while one was open for 0% of the time, Pallas kernels for 4%

profile of v15, /device:TPU:1, one launch (start us, length us, event | category | flops | bytes accessed | tf_op | source)
XLA Modules:
  0.0 140.3 jit_solution(14026455191826644444)
XLA Ops:
  0.6 3.6 %half.1 = f32[8,72,128]{2,1,0:T(8,128)} custom-call(s32[2,4]{1,0:T(2,128)} %bitcast.31, s32[4]{0:T(128)} %screen_at.1, bf16[8,768]{1,0:T(8,128)(2,1)} %bitcast.30, bf16[4,32,4096]{2,1,0:T(8,128)(2,1)} %ints.1), custom_call_target="tpu_custom_call" | custom-call | tf_op jit(solution)/shard_map/half/pallas_call | solution.py:87
  4.2 10.2 %all-to-all-start = ((f32[8,72,128]{2,1,0:T(8,128)}), f32[8,72,128]{2,1,0:T(8,128)S(1)}, u32[]{:S(2)}, u32[]{:S(2)}) async-start(f32[8,72,128]{2,1,0:T(8,128)} %half.1), calls=%async_computation | async-start | bytes 589824 | tf_op jit(solution)/shard_map/all_to_all | solution.py:392
  14.4 1.9 %hold.1.c_vir = bf16[768,2048]{1,0:T(8,128)(2,1)S(1)} custom-call(bf16[768,2048]{1,0:T(8,128)(2,1)} %c_vir.1), custom_call_target="tpu_custom_call" | custom-call | flops 8589934592 | bytes 4194304 | tf_op jit(solution)/shard_map/hold/pallas_call | solution.py:113
  16.3 9.3 %all-to-all-done.recv = f32[8,72,128]{2,1,0:T(8,128)S(1)} async-done(((f32[8,72,128]{2,1,0:T(8,128)}), f32[8,72,128]{2,1,0:T(8,128)S(1)}, u32[]{:S(2)}, u32[]{:S(2)}) %all-to-all-start) | async-done | bytes 294944 | tf_op jit(solution)/shard_map/all_to_all | solution.py:392
  25.6 1.3 transform.1
  27.0 0.0 copy-start.1
  27.0 0.6 copy-done.1
  27.6 0.0 copy-start
  27.6 28.4 %all_to_all.25 = bf16[64,32,128]{2,1,0:T(8,128)(2,1)S(1)} all-to-all(bf16[64,32,128]{2,1,0:T(8,128)(2,1)S(1)} %get-tuple-element.13), channel_id=1, replica_groups=mesh['zh'=4,'zl'=2,'x'=4,'yl'=2,'yh'=4,'core'=2] {'zh','zl','yl','yh'}, dimensions={0} | all-to-all | bytes 1048576 | tf_op jit(solution)/shard_map/all_to_all | solution.py:394
  56.0 3.1 %collective-permute-start = (bf16[64,32,128]{2,1,0:T(8,128)(2,1)S(1)}, bf16[64,32,128]{2,1,0:T(8,128)(2,1)S(1)}, u32[]{:S(2)}, u32[]{:S(2)}) collective-permute-start(bf16[64,32,128]{2,1,0:T(8,128)(2,1)S(1)} %all_to_all.25), channel_id=1, source_target_pairs={{0,16},{16,32},{32,48},{48,0},{1,17},{17,33},{33,49},{49,1},{2,18}... | collective-permute-start | bytes 1572872 | tf_op jit(solution)/shard_map/ppermute | solution.py:397
  59.1 3.4 %collective-permute-start.1 = (bf16[64,32,128]{2,1,0:T(8,128)(2,1)S(1)}, bf16[64,32,128]{2,1,0:T(8,128)(2,1)S(1)}, u32[]{:S(2)}, u32[]{:S(2)}) collective-permute-start(bf16[64,32,128]{2,1,0:T(8,128)(2,1)S(1)} %all_to_all.25), channel_id=1, source_target_pairs={{0,48},{16,0},{32,16},{48,32},{1,49},{17,1},{33,17},{49,33},{2,50}... | collective-permute-start | bytes 1572872 | tf_op jit(solution)/shard_map/ppermute | solution.py:397
  62.5 0.0 copy-done
  62.5 10.7 %all-to-all-start.2 = ((bf16[256,16,128]{2,1,0:T(8,128)(2,1)}), bf16[256,16,128]{2,1,0:T(8,128)(2,1)S(1)}, u32[]{:S(2)}, u32[]{:S(2)}) async-start(bf16[256,16,128]{2,1,0:T(8,128)(2,1)} %copy-done), calls=%async_computation.2 | async-start | bytes 2097152 | tf_op jit(solution)/shard_map/all_to_all | solution.py:400
  73.2 0.0 copy-start.2
  73.2 0.0 collective-permute-done.below
  73.2 0.0 collective-permute-done.1.above
  73.2 0.7 onward.1
  74.0 0.0 copy-start.3
  74.0 0.0 copy-start.4
  74.0 3.0 %collective-permute-start.2 = (bf16[32,32,128]{2,1,0:T(8,128)(2,1)}, bf16[32,32,128]{2,1,0:T(8,128)(2,1)S(1)}, u32[]{:S(2)}, u32[]{:S(2)}) collective-permute-start(bf16[32,32,128]{2,1,0:T(8,128)(2,1)} %get-tuple-element.14), channel_id=1, source_target_pairs={{0,48},{16,0},{32,16},{48,32},{1,49},{17,1},{33,17},{49,33},{2,50}... | collective-permute-start | bytes 786440 | tf_op jit(solution)/shard_map/ppermute | solution.py:399
  77.0 2.4 %collective-permute-start.3 = (bf16[32,32,128]{2,1,0:T(8,128)(2,1)S(1)}, bf16[32,32,128]{2,1,0:T(8,128)(2,1)S(1)}, u32[]{:S(2)}, u32[]{:S(2)}) collective-permute-start(bf16[32,32,128]{2,1,0:T(8,128)(2,1)S(1)} %get-tuple-element.15), channel_id=1, source_target_pairs={{0,16},{16,32},{32,48},{48,0},{1,17},{17,33},{33,49},{49,1},{2,18}... | collective-permute-start | bytes 786440 | tf_op jit(solution)/shard_map/ppermute | solution.py:399
  79.4 0.1 stack.31.place
  79.5 6.9 %collective-permute-done.2 = bf16[32,32,128]{2,1,0:T(8,128)(2,1)S(1)} collective-permute-done((bf16[32,32,128]{2,1,0:T(8,128)(2,1)}, bf16[32,32,128]{2,1,0:T(8,128)(2,1)S(1)}, u32[]{:S(2)}, u32[]{:S(2)}) %collective-permute-start.2) | collective-permute-done | bytes 262176 | tf_op jit(solution)/shard_map/ppermute | solution.py:399
  86.4 2.9 %collective-permute-done.3 = bf16[32,32,128]{2,1,0:T(8,128)(2,1)S(1)} collective-permute-done((bf16[32,32,128]{2,1,0:T(8,128)(2,1)S(1)}, bf16[32,32,128]{2,1,0:T(8,128)(2,1)S(1)}, u32[]{:S(2)}, u32[]{:S(2)}) %collective-permute-start.3) | collective-permute-done | bytes 262176 | tf_op jit(solution)/shard_map/ppermute | solution.py:399
  89.3 0.0 copy-done.2
  89.3 1.1 panel.1
  90.4 0.0 copy-start.5
  90.4 0.6 copy-done.5
  91.0 6.0 %collective-permute-start.4 = (f32[64,1024]{1,0:T(8,128)S(1)}, f32[64,1024]{1,0:T(8,128)S(1)}, u32[]{:S(2)}, u32[]{:S(2)}) collective-permute-start(f32[64,1024]{1,0:T(8,128)S(1)} %get-tuple-element.18), channel_id=1, source_target_pairs={{0,1},{1,0},{2,3},{3,2},{4,5},{5,4},{6,7},{7,6},{8,9},{9,8},{10,11... | collective-permute-start | bytes 786440 | tf_op jit(solution)/shard_map/ppermute | solution.py:405
  97.0 1.1 collective-permute-done.4.got._
  98.2 0.6 all-to-all-done.2
  98.7 0.0 copy-start.6
  98.7 2.4 %gram.1 = (f32[256,1024]{1,0:T(8,128)S(1)}, f32[256,1024]{1,0:T(8,128)S(1)}) custom-call(s32[7]{0:T(128)S(1)} %stack.31.place, bf16[16,8,16,128]{3,2,1,0:T(8,128)(2,1)S(1)} %bitcast.18, bf16[16,8,16,128]{3,2,1,0:T(8,128)(2,1)S(1)} %bitcast.21, bf16[16,8,16,128]{3,2,1,0:T(8,128)(2,1)S(1)} %bitcast.23, bf16[8,8,16,128]{3,2,1,0:T(8,128)(2,1)S(1)} %bitcast.25, ...), custom_call_target="tpu_custom_call" | custom-call | tf_op jit(solution)/shard_map/gram/pallas_call | solution.py:304
  101.2 6.4 %collective-permute-start.5 = (f32[256,1024]{1,0:T(8,128)S(1)}, f32[256,1024]{1,0:T(8,128)S(1)}, u32[]{:S(2)}, u32[]{:S(2)}) collective-permute-start(f32[256,1024]{1,0:T(8,128)S(1)} %get-tuple-element.22), channel_id=1, source_target_pairs={{0,1},{1,0},{2,3},{3,2},{4,5},{5,4},{6,7},{7,6},{8,9},{9,8},{10,11... | collective-permute-start | bytes 3145736 | tf_op jit(solution)/shard_map/ppermute | solution.py:408
  107.5 0.0 copy-done.3
  107.5 0.0 copy-done.4
  107.5 0.0 copy-done.6
  107.6 1.2 settle.1
  108.8 1.0 collective-permute-done.5.got
  109.8 0.9 energies.1
  110.7 12.8 %all_to_all.26.got = f32[32,1,128]{2,1,0:T(1,128)S(1)} all-to-all(f32[32,1,128]{2,1,0:T(1,128)S(1)} %energies.1), channel_id=1, replica_groups=mesh['zh'=4,'zl'=2,'x'=4,'yl'=2,'yh'=4,'core'=2] {'zl','x','yl','core'}, dimensions={0} | all-to-all | bytes 32768 | tf_op jit(solution)/shard_map/all_to_all | solution.py:411
  123.6 16.0 %all_to_all.27.got = f32[16,1,128]{2,1,0:T(1,128)S(1)} all-to-all(f32[16,1,128]{2,1,0:T(1,128)S(1)} %again.1), channel_id=1, replica_groups=mesh['zh'=4,'zl'=2,'x'=4,'yl'=2,'yh'=4,'core'=2] {'zh','yh'}, dimensions={0} | all-to-all | bytes 16384 | tf_op jit(solution)/shard_map/all_to_all | solution.py:412
  139.6 0.7 last.1
  (1 shorter events, 0.0 us)
Async XLA Ops:
  4.2 21.4 %all-to-all-start = ((f32[8,72,128]{2,1,0:T(8,128)}), f32[8,72,128]{2,1,0:T(8,128)S(1)}, u32[]{:S(2)}, u32[]{:S(2)}) async-start(f32[8,72,128]{2,1,0:T(8,128)} %half.1), calls=%async_computation | async-start | bytes 589824 | tf_op jit(solution)/shard_map/all_to_all | solution.py:392
  27.0 0.7 copy-start.1
  27.6 34.9 %copy-start = (bf16[256,16,128]{2,1,0:T(8,128)(2,1)}, bf16[256,16,128]{2,1,0:T(8,128)(2,1)S(1)}, u32[]{:S(2)}) copy-start(bf16[256,16,128]{2,1,0:T(8,128)(2,1)S(1)} %get-tuple-element.20) | copy-start | bytes 3145732
  56.0 17.2 %collective-permute-start = (bf16[64,32,128]{2,1,0:T(8,128)(2,1)S(1)}, bf16[64,32,128]{2,1,0:T(8,128)(2,1)S(1)}, u32[]{:S(2)}, u32[]{:S(2)}) collective-permute-start(bf16[64,32,128]{2,1,0:T(8,128)(2,1)S(1)} %all_to_all.25), channel_id=1, source_target_pairs={{0,16},{16,32},{32,48},{48,0},{1,17},{17,33},{33,49},{49,1},{2,18}... | collective-permute-start | bytes 1572872 | tf_op jit(solution)/shard_map/ppermute | solution.py:397
  59.1 14.1 %collective-permute-start.1 = (bf16[64,32,128]{2,1,0:T(8,128)(2,1)S(1)}, bf16[64,32,128]{2,1,0:T(8,128)(2,1)S(1)}, u32[]{:S(2)}, u32[]{:S(2)}) collective-permute-start(bf16[64,32,128]{2,1,0:T(8,128)(2,1)S(1)} %all_to_all.25), channel_id=1, source_target_pairs={{0,48},{16,0},{32,16},{48,32},{1,49},{17,1},{33,17},{49,33},{2,50}... | collective-permute-start | bytes 1572872 | tf_op jit(solution)/shard_map/ppermute | solution.py:397
  62.5 36.2 %all-to-all-start.2 = ((bf16[256,16,128]{2,1,0:T(8,128)(2,1)}), bf16[256,16,128]{2,1,0:T(8,128)(2,1)S(1)}, u32[]{:S(2)}, u32[]{:S(2)}) async-start(bf16[256,16,128]{2,1,0:T(8,128)(2,1)} %copy-done), calls=%async_computation.2 | async-start | bytes 2097152 | tf_op jit(solution)/shard_map/all_to_all | solution.py:400
  73.2 16.1 %copy-start.2 = (bf16[32,2048]{1,0:T(8,128)(2,1)S(1)}, bf16[32,2048]{1,0:T(8,128)(2,1)}, u32[]{:S(2)}) copy-start(bf16[32,2048]{1,0:T(8,128)(2,1)} %copy-done.1) | copy-start | bytes 393220
  74.0 33.5 %copy-start.3 = (f32[2048]{0:T(1024)S(1)}, f32[2048]{0:T(1024)}, u32[]{:S(2)}) copy-start(f32[2048]{0:T(1024)} %param.13) | copy-start | bytes 24580
  74.0 33.6 %copy-start.4 = (f32[8]{0:T(128)S(1)}, f32[8]{0:T(128)}, u32[]{:S(2)}) copy-start(f32[8]{0:T(128)} %eps_occ.3) | copy-start | bytes 100
  74.0 12.4 %collective-permute-start.2 = (bf16[32,32,128]{2,1,0:T(8,128)(2,1)}, bf16[32,32,128]{2,1,0:T(8,128)(2,1)S(1)}, u32[]{:S(2)}, u32[]{:S(2)}) collective-permute-start(bf16[32,32,128]{2,1,0:T(8,128)(2,1)} %get-tuple-element.14), channel_id=1, source_target_pairs={{0,48},{16,0},{32,16},{48,32},{1,49},{17,1},{33,17},{49,33},{2,50}... | collective-permute-start | bytes 786440 | tf_op jit(solution)/shard_map/ppermute | solution.py:399
  77.0 12.3 %collective-permute-start.3 = (bf16[32,32,128]{2,1,0:T(8,128)(2,1)S(1)}, bf16[32,32,128]{2,1,0:T(8,128)(2,1)S(1)}, u32[]{:S(2)}, u32[]{:S(2)}) collective-permute-start(bf16[32,32,128]{2,1,0:T(8,128)(2,1)S(1)} %get-tuple-element.15), channel_id=1, source_target_pairs={{0,16},{16,32},{32,48},{48,0},{1,17},{17,33},{33,49},{49,1},{2,18}... | collective-permute-start | bytes 786440 | tf_op jit(solution)/shard_map/ppermute | solution.py:399
  90.4 0.7 copy-start.5
  91.0 7.2 %collective-permute-start.4 = (f32[64,1024]{1,0:T(8,128)S(1)}, f32[64,1024]{1,0:T(8,128)S(1)}, u32[]{:S(2)}, u32[]{:S(2)}) collective-permute-start(f32[64,1024]{1,0:T(8,128)S(1)} %get-tuple-element.18), channel_id=1, source_target_pairs={{0,1},{1,0},{2,3},{3,2},{4,5},{5,4},{6,7},{7,6},{8,9},{9,8},{10,11... | collective-permute-start | bytes 786440 | tf_op jit(solution)/shard_map/ppermute | solution.py:405
  98.7 8.8 %copy-start.6 = (f32[32,1024]{1,0:T(8,128)S(1)}, f32[32,1024]{1,0:T(8,128)}, u32[]{:S(2)}) copy-start(f32[32,1024]{1,0:T(8,128)} %copy-done.5) | copy-start | bytes 393220
  101.2 8.6 %collective-permute-start.5 = (f32[256,1024]{1,0:T(8,128)S(1)}, f32[256,1024]{1,0:T(8,128)S(1)}, u32[]{:S(2)}, u32[]{:S(2)}) collective-permute-start(f32[256,1024]{1,0:T(8,128)S(1)} %get-tuple-element.22), channel_id=1, source_target_pairs={{0,1},{1,0},{2,3},{3,2},{4,5},{5,4},{6,7},{7,6},{8,9},{9,8},{10,11... | collective-permute-start | bytes 3145736 | tf_op jit(solution)/shard_map/ppermute | solution.py:408
